TPU v7x, 128 devices: a whole 4x4x4 slice. The times are simulated.
128 devices in a mesh: gx: 4 (over z), gy: 32 (over y, x, core).
Axes of the slice: x: 4, y: 4, z: 4, core: 2. Of those that a mesh axis runs over, the one named last changes fastest.
Arguments:
- heat_source: float32 [6144, 1024], P(('gx', 'gy')), may hold values from -18 to 18
- stiffness: float32 [2048, 384, 384], P(('gx', 'gy')), may hold values from -1 to 32, as said below
- element_faces: int32 [2048, 6], P(('gx', 'gy')), may hold values from 0 to 6143, as said below
Outputs:
- solution: float32 [6144, 1024], P(('gx', 'gy'))
- residual: float32 [6144, 1024], P(('gx', 'gy'))
Inputs may be any that keep to these rules, and one draw needn't show every extreme that they name: `element_faces`: the elements form a periodic grid of 8 x 64 x 4 hexahedra; device (i, j) of gx and gy holds the block of 2 x 2 x 4 elements at streamwise block i and spanwise block j, in a local order of its own, and owns the lower x, lower y and lower z faces of its elements, numbered in an order of its own. So every face number appears exactly twice, and a device's elements reference faces of itself, of the next device along gx (cyclic, same gy index; exactly 8 references) and of the next device along gy (cyclic, same gx index; exactly 8 references). `stiffness`: each element matrix is symmetric with a positive diagonal and strictly diagonally dominant.
All inputs are finite; a program needn't handle non-finite values.
Results may differ from a plain program's by a relative error of at most 0.0002.
Values sent between devices are 32-bit elements; how exact they have to be, the bound alone decides.
No kernel may reach another device: no remote copies, remote signals or barrier semaphores. Data moves between devices by JAX's collectives and lax.ppermute only.
A program may use at most 128 MiB of HBM per device.

v0:
```python
import jax
import jax.numpy as jnp
from jax import lax
from jax.sharding import PartitionSpec as P

BLOCK = 64
EX = 2
EY = 2
EZ = 4
SOURCES = 16
ITERS = 3


def passed_along(value, axis, steps):
    count = lax.axis_size(axis)
    pairs = [(source, (source + steps) % count) for source in range(count)]
    return lax.ppermute(value, axis, pairs)


def source_sum(first_vec, second_vec):
    return jnp.sum(
        (first_vec * second_vec).reshape(first_vec.shape[0], SOURCES, BLOCK), axis=(0, 2)
    )


def spread(per_source):
    return jnp.repeat(per_source, BLOCK)[None, :]


def local(heat_source, stiffness, element_faces):
    face_dev = heat_source.shape[0]
    elements = element_faces.shape[0]
    references = 6 * elements
    row_width = heat_source.shape[1]
    outer = lax.axis_size("gx")
    inner = lax.axis_size("gy")
    outer_at = lax.axis_index("gx")
    inner_at = lax.axis_index("gy")
    self_dev = outer_at * inner + inner_at
    x_next = (outer_at + 1) % outer * inner + inner_at
    y_next = outer_at * inner + (inner_at + 1) % inner
    x_count = EY * EZ
    y_count = EX * EZ
    flat_faces = element_faces.reshape(references)
    owner_dev = flat_faces // face_dev
    local_face = flat_faces % face_dev
    is_self = owner_dev == self_dev
    is_x = owner_dev == x_next
    is_y = owner_dev == y_next
    rank_x = jnp.cumsum(is_x.astype(jnp.int32)) - 1
    rank_y = jnp.cumsum(is_y.astype(jnp.int32)) - 1
    ref_ids = jnp.arange(references, dtype=jnp.int32)
    refs_x = (
        jnp.zeros((x_count,), jnp.int32)
        .at[jnp.where(is_x, rank_x, x_count)]
        .set(ref_ids, mode="drop")
    )
    refs_y = (
        jnp.zeros((y_count,), jnp.int32)
        .at[jnp.where(is_y, rank_y, y_count)]
        .set(ref_ids, mode="drop")
    )
    wanted_x = passed_along(local_face[refs_x], "gx", 1)
    wanted_y = passed_along(local_face[refs_y], "gy", 1)
    table_index = jnp.where(
        is_self, local_face, jnp.where(is_x, face_dev + rank_x, face_dev + x_count + rank_y)
    )
    self_target = jnp.where(is_self, local_face, face_dev)
    matrix = stiffness.reshape(elements, 6, BLOCK, 6, BLOCK)

    def squares(residual):
        return lax.psum(source_sum(residual, residual), ("gx", "gy"))

    solution = jnp.zeros_like(heat_source)
    residual = heat_source
    direction = heat_source
    norm_now = squares(residual)
    for iteration in range(ITERS):
        send_got_x = passed_along(direction[wanted_x], "gx", -1)
        send_got_y = passed_along(direction[wanted_y], "gy", -1)
        table = jnp.concatenate([direction, send_got_x, send_got_y], axis=0)
        blocks = table[table_index].reshape(elements, 6, SOURCES, BLOCK)
        flux_terms = jnp.einsum(
            "ekbjc,ejsc->eksb",
            matrix,
            blocks,
            precision=lax.Precision.HIGHEST,
            preferred_element_type=jnp.float32,
        )
        flux_rows = flux_terms.reshape(references, row_width)
        got_x = passed_along(flux_rows[refs_x], "gx", 1)
        got_y = passed_along(flux_rows[refs_y], "gy", 1)
        result = (
            jnp.zeros((face_dev + 1, row_width), jnp.float32)
            .at[self_target]
            .add(flux_rows)[:face_dev]
        )
        applied = result.at[wanted_x].add(got_x).at[wanted_y].add(got_y)
        step_size = norm_now / lax.psum(source_sum(direction, applied), ("gx", "gy"))
        solution = solution + spread(step_size) * direction
        residual = residual - spread(step_size) * applied
        norm_next = squares(residual)
        direction = residual + spread(norm_next / norm_now) * direction
        norm_now = norm_next
    return (solution, residual)


def solution(mesh):
    return jax.shard_map(
        local,
        mesh=mesh,
        in_specs=(P(("gx", "gy"), None), P(("gx", "gy"), None, None), P(("gx", "gy"), None)),
        out_specs=(P(("gx", "gy"), None), P(("gx", "gy"), None)),
        check_vma=False,
    )
```

profile of v0, /device:TPU:0, one launch (start us, length us, event | category | flops | bytes accessed | tf_op | source)
XLA Modules:
  0.0 486.5 jit_solution(13445269767935727332)
XLA Ops:
  0.7 0.7 sign_compare_fusion
  1.4 0.7 broadcast_remainder_fusion
  3.2 0.9 scatter_custom_fusion.1
  4.2 0.6 gather_fusion.2
  4.9 0.9 scatter_custom_fusion
  5.8 0.6 gather_fusion
  6.4 2.1 collective-permute-start
  8.5 2.6 collective-permute-done.2
  11.2 1.0 collective-permute-done
  12.1 1.5 gather_fusion.1
  13.7 1.5 gather_fusion.3
  15.2 4.2 collective-permute-start.3
  19.4 1.7 collective-permute-start.1
  21.2 17.1 %reshape.252 = f32[16,6,64,6,64]{4,3,2,1,0:T(8,128)} reshape(f32[16,384,384]{2,1,0:T(8,128)} %param.4) | data formatting | bytes 18874368 | tf_op jit(solution)/shard_map/reshape | solution.py:69
  38.3 0.7 gather_fusion.4
  39.3 28.8 %fusion.6 = f32[16,6,16,64]{3,2,1,0:T(8,128)S(1)} fusion(f32[16,6,64,6,64]{4,3,2,1,0:T(8,128)} %reshape.252, f32[16,6,16,64,1]{3,2,1,0,4:T(8,128)S(1)} %reshape.502), kind=kOutput, calls=%fused_computation.34 | convolution fusion | flops 452984832 | bytes 10223616 | tf_op jit(solution)/shard_map/ekbjc,ejsc->eksb/dot_general | solution.py:83
  69.9 1.4 scatter_custom_fusion.2
  71.4 2.7 collective-permute-done.4
  74.1 0.8 scatter_fusion
  74.9 1.7 collective-permute-done.5
  76.6 0.8 scatter_fusion.1
  77.8 63.2 %all-reduce = (f32[16]{0:T(128)S(1)}, f32[16]{0:T(128)S(1)}) all-reduce(f32[16]{0:T(128)S(1)} %reduce_sum.74, f32[16]{0:T(128)S(1)} %reduce_sum.77), channel_id=1, replica_groups=mesh['gx'=4,'gy'=32] {'gx','gy'}, use_global_device_ids=true, to_apply=%region_2.3 | all-reduce | flops 32 | bytes 256 | tf_op jit(solution)/shard_map/psum | solution.py:72
  141.3 63.8 %psum.44 = f32[16]{0:T(128)S(1)} all-reduce(f32[16]{0:T(128)S(1)} %reduce_sum.83), channel_id=1, replica_groups=mesh['gx'=4,'gy'=32] {'gx','gy'}, use_global_device_ids=true, to_apply=%region_15.16 | all-reduce | flops 16 | bytes 128 | tf_op jit(solution)/shard_map/psum | solution.py:72
  206.4 1.0 collective-permute-start.6
  207.4 1.1 collective-permute-start.7
  208.5 1.9 collective-permute-done.6
  210.4 0.7 gather_fusion.9
  211.4 28.8 %fusion.9 = f32[16,6,16,64]{3,2,1,0:T(8,128)S(1)} fusion(f32[16,6,64,6,64]{4,3,2,1,0:T(8,128)} %reshape.252, f32[16,6,16,64,1]{3,2,1,0,4:T(8,128)S(1)} %reshape.504), kind=kOutput, calls=%fused_computation.35 | convolution fusion | flops 452984832 | bytes 10223616 | tf_op jit(solution)/shard_map/ekbjc,ejsc->eksb/dot_general | solution.py:83
  241.0 1.3 collective-permute-start.8
  243.0 1.4 scatter_custom_fusion.5
  244.4 1.8 collective-permute-done.8
  246.2 0.8 scatter_fusion.2
  247.0 2.6 collective-permute-done.9
  249.6 0.8 scatter_fusion.3
  250.6 62.3 %psum.45 = f32[16]{0:T(128)S(1)} all-reduce(f32[16]{0:T(128)S(1)} %reduce_sum.89), channel_id=1, replica_groups=mesh['gx'=4,'gy'=32] {'gx','gy'}, use_global_device_ids=true, to_apply=%region_21.22 | all-reduce | flops 16 | bytes 128 | tf_op jit(solution)/shard_map/psum | solution.py:99
  313.4 64.6 %psum.46 = f32[16]{0:T(128)S(1)} all-reduce(f32[16]{0:T(128)S(1)} %reduce_sum.110), channel_id=1, replica_groups=mesh['gx'=4,'gy'=32] {'gx','gy'}, use_global_device_ids=true, to_apply=%region_24.25 | all-reduce | flops 16 | bytes 128 | tf_op jit(solution)/shard_map/psum | solution.py:72
  379.6 1.6 collective-permute-start.11
  381.2 2.1 collective-permute-done.10
  383.3 0.7 gather_fusion.14
  384.2 28.8 %fusion.12 = f32[16,6,16,64]{3,2,1,0:T(8,128)S(1)} fusion(f32[16,6,64,6,64]{4,3,2,1,0:T(8,128)} %reshape.252, f32[16,6,16,64,1]{3,2,1,0,4:T(8,128)S(1)} %reshape.506), kind=kOutput, calls=%fused_computation.36 | convolution fusion | flops 452984832 | bytes 10223616 | tf_op jit(solution)/shard_map/ekbjc,ejsc->eksb/dot_general | solution.py:83
  413.9 1.1 collective-permute-start.12
  415.7 1.4 scatter_custom_fusion.8
  417.1 2.0 collective-permute-done.12
  419.1 0.8 scatter_fusion.4
  419.8 2.5 collective-permute-done.13
  422.3 0.8 scatter_fusion.5
  423.3 62.3 %psum.47 = f32[16]{0:T(128)S(1)} all-reduce(f32[16]{0:T(128)S(1)} %reduce_sum.113), channel_id=1, replica_groups=mesh['gx'=4,'gy'=32] {'gx','gy'}, use_global_device_ids=true, to_apply=%region_30.31 | all-reduce | flops 16 | bytes 128 | tf_op jit(solution)/shard_map/psum | solution.py:99
  485.7 0.8 multiply_subtract_fusion
  (91 shorter events, 11.4 us)
Async XLA Ops:
  0.6 37.7 %copy-start = (f32[48,1024]{1,0:T(8,128)S(1)}, f32[48,1024]{1,0:T(8,128)}, u32[]{:S(2)}) copy-start(f32[48,1024]{1,0:T(8,128)} %param.3) | copy-start | bytes 589828
  4.8 6.3 %collective-permute-start.2 = (s32[8]{0:T(128)S(1)}, s32[8]{0:T(128)S(1)}, u32[]{:S(2)}, u32[]{:S(2)}) collective-permute-start(s32[8]{0:T(128)S(1)} %gather_fusion.2), channel_id=1, source_target_pairs={{0,1},{1,2},{2,3},{3,4},{4,5},{5,6},{6,7},{7,8},{8,9},{9,10},{10,1... | collective-permute-start | bytes 104 | tf_op jit(solution)/shard_map/ppermute | solution.py:17
  6.4 5.7 %collective-permute-start = (s32[8]{0:T(128)S(1)}, s32[8]{0:T(128)S(1)}, u32[]{:S(2)}, u32[]{:S(2)}) collective-permute-start(s32[8]{0:T(128)S(1)} %gather_fusion), channel_id=1, source_target_pairs={{0,32},{32,64},{64,96},{96,0},{1,33},{33,65},{65,97},{97,1},{2,34}... | collective-permute-start | bytes 104 | tf_op jit(solution)/shard_map/ppermute | solution.py:17
  15.2 23.1 %collective-permute-start.3 = (f32[8,1024]{1,0:T(8,128)S(1)}, f32[8,1024]{1,0:T(8,128)S(1)}, u32[]{:S(2)}, u32[]{:S(2)}) collective-permute-start(f32[8,1024]{1,0:T(8,128)S(1)} %gather_fusion.3), channel_id=1, source_target_pairs={{0,31},{1,0},{2,1},{3,2},{4,3},{5,4},{6,5},{7,6},{8,7},{9,8},{10,9... | collective-permute-start | bytes 98312 | tf_op jit(solution)/shard_map/ppermute | solution.py:17
  19.4 18.9 %collective-permute-start.1 = (f32[8,1024]{1,0:T(8,128)S(1)}, f32[8,1024]{1,0:T(8,128)S(1)}, u32[]{:S(2)}, u32[]{:S(2)}) collective-permute-start(f32[8,1024]{1,0:T(8,128)S(1)} %gather_fusion.1), channel_id=1, source_target_pairs={{0,96},{32,0},{64,32},{96,64},{1,97},{33,1},{65,33},{97,65},{2,98}... | collective-permute-start | bytes 98312 | tf_op jit(solution)/shard_map/ppermute | solution.py:17
  68.9 5.2 %collective-permute-start.4 = (f32[8,1024]{1,0:T(8,128)S(1)}, f32[8,1024]{1,0:T(8,128)S(1)}, u32[]{:S(2)}, u32[]{:S(2)}) collective-permute-start(f32[8,1024]{1,0:T(8,128)S(1)} %gather_fusion.5), channel_id=1, source_target_pairs={{0,32},{32,64},{64,96},{96,0},{1,33},{33,65},{65,97},{97,1},{2,34}... | collective-permute-start | bytes 98312 | tf_op jit(solution)/shard_map/ppermute | solution.py:17
  69.8 6.7 %collective-permute-start.5 = (f32[8,1024]{1,0:T(8,128)S(1)}, f32[8,1024]{1,0:T(8,128)S(1)}, u32[]{:S(2)}, u32[]{:S(2)}) collective-permute-start(f32[8,1024]{1,0:T(8,128)S(1)} %gather_fusion.6), channel_id=1, source_target_pairs={{0,1},{1,2},{2,3},{3,4},{4,5},{5,6},{6,7},{7,8},{8,9},{9,10},{10,1... | collective-permute-start | bytes 98312 | tf_op jit(solution)/shard_map/ppermute | solution.py:17
  206.4 4.0 collective-permute-start.6
  207.4 3.0 collective-permute-start.7
  241.0 5.2 %collective-permute-start.8 = (f32[8,1024]{1,0:T(8,128)S(1)}, f32[8,1024]{1,0:T(8,128)S(1)}, u32[]{:S(2)}, u32[]{:S(2)}) collective-permute-start(f32[8,1024]{1,0:T(8,128)S(1)} %gather_fusion.10), channel_id=1, source_target_pairs={{0,32},{32,64},{64,96},{96,0},{1,33},{33,65},{65,97},{97,1},{2,34}... | collective-permute-start | bytes 98312 | tf_op jit(solution)/shard_map/ppermute | solution.py:17
  242.9 6.7 %collective-permute-start.9 = (f32[8,1024]{1,0:T(8,128)S(1)}, f32[8,1024]{1,0:T(8,128)S(1)}, u32[]{:S(2)}, u32[]{:S(2)}) collective-permute-start(f32[8,1024]{1,0:T(8,128)S(1)} %gather_fusion.11), channel_id=1, source_target_pairs={{0,1},{1,2},{2,3},{3,4},{4,5},{5,6},{6,7},{7,8},{8,9},{9,10},{10,1... | collective-permute-start | bytes 98312 | tf_op jit(solution)/shard_map/ppermute | solution.py:17
  379.3 4.0 collective-permute-start.10
  379.6 3.7 collective-permute-start.11
  413.9 5.2 %collective-permute-start.12 = (f32[8,1024]{1,0:T(8,128)S(1)}, f32[8,1024]{1,0:T(8,128)S(1)}, u32[]{:S(2)}, u32[]{:S(2)}) collective-permute-start(f32[8,1024]{1,0:T(8,128)S(1)} %gather_fusion.15), channel_id=1, source_target_pairs={{0,32},{32,64},{64,96},{96,0},{1,33},{33,65},{65,97},{97,1},{2,34}... | collective-permute-start | bytes 98312 | tf_op jit(solution)/shard_map/ppermute | solution.py:17
  415.6 6.7 %collective-permute-start.13 = (f32[8,1024]{1,0:T(8,128)S(1)}, f32[8,1024]{1,0:T(8,128)S(1)}, u32[]{:S(2)}, u32[]{:S(2)}) collective-permute-start(f32[8,1024]{1,0:T(8,128)S(1)} %gather_fusion.16), channel_id=1, source_target_pairs={{0,1},{1,2},{2,3},{3,4},{4,5},{5,6},{6,7},{7,8},{8,9},{9,10},{10,1... | collective-permute-start | bytes 98312 | tf_op jit(solution)/shard_map/ppermute | solution.py:17
where the time goes:
time: 488 us; the launch traced here: 487 us
  blocking collectives  316 us (65%)
  matrix products  86.4 us (18%)
  local copies, waits for them, and re-layouts  34.2 us (7%)
  waiting for transfers between devices  20.9 us (4%)
  starting transfers between devices  15.1 us (3%)
  other arithmetic  12.6 us (3%)
    psum x3, blocking collectives, squares(): return lax.psum(source_sum(residual, residual), ('gx', 'gy'))  192 us
    psum x2, blocking collectives, local(): lax.psum(source_sum(direction, applied), ('gx', 'gy'))  125 us
    dot_general x3, matrix products, local(): jnp.einsum('ekbjc,ejsc->eksb', matrix, blocks, precision=lax.Precision.HI...  86.4 us
    ppermute x14, waiting for transfers between devices, passed_along(): return lax.ppermute(value, axis, pairs)  20.9 us
    reshape x1, local copies, waits for them, and re-layouts, local(): matrix = stiffness.reshape(elements, 6, BLOCK, 6, BLOCK)  17.1 us
    ppermute x14, starting transfers between devices, passed_along(): return lax.ppermute(value, axis, pairs)  15.1 us
  transfers between devices with their start and end apart: 14, of which 10 were waited for; matrix products, arithmetic and copies ran while one was open for 6% of the time, Pallas kernels for 0%

commit v1 on v0

v1 whole, which is shorter than its diff:
```python
import functools

import jax
import jax.numpy as jnp
from jax import lax
from jax.experimental import pallas as pl
from jax.experimental.pallas import tpu as pltpu
from jax.sharding import PartitionSpec as P

BLOCK = 64
SOURCES = 16
ELEMENTS = 16
ROWS = 48
SLOTS = 8
ORDER = 384

LOW = 0
UPP = 64
ROW_LOW = 128
ROW_UPP = 192
SEND_UP = 256
SEND_DOWN = 272
SEND_ROW = 288
SPARE = 304
TABLE = 312

VMEM = pl.BlockSpec(memory_space=pltpu.VMEM)
SMEM = pl.BlockSpec(memory_space=pltpu.SMEM)


def params():
    return pltpu.CompilerParams(vmem_limit_bytes=24 << 20)


def vmem(shape, dtype=jnp.float32):
    return pltpu.VMEM(shape, dtype)


def in_low_half(shape):
    return lax.broadcasted_iota(jnp.int32, shape, len(shape) - 1) < BLOCK


def table_kernel(ids, faces, source, table, down_x, down_y, owner, user):
    for row in range(ROWS):
        for part in range(3):
            user[part * ROWS + row] = -1
    own = ids[0]
    for element in range(ELEMENTS):
        for axis in range(3):
            row = faces[2 * axis, element] - own
            owner[row] = element * 4 + axis
            table[ROW_LOW + element * 4 + axis] = row
            row = faces[2 * axis + 1, element] - own
            if axis < 2:
                away = faces[2 * axis + 1, element] - ids[1 + axis] + ROWS * (1 + axis)
                here = jnp.logical_and(row >= 0, row < ROWS)
                user[jnp.where(here, row, away)] = element
            else:
                user[row] = element
            table[ROW_UPP + element * 4 + axis] = row
    count = [jnp.int32(0), jnp.int32(0)]
    for row in range(ROWS):
        ref = owner[row]
        axis = ref & 3
        element = ref >> 2
        other = user[row]
        here = other >= 0
        slot = jnp.where(axis == 0, count[0], count[1])
        table[LOW + ref] = jnp.where(here, other, ELEMENTS + slot)
        table[jnp.where(here, UPP + other * 4 + axis, SPARE)] = element
        table[jnp.where(here, SPARE, SEND_DOWN + axis * SLOTS + slot)] = element
        table[jnp.where(here, SPARE, SEND_ROW + axis * SLOTS + slot)] = row
        step = jnp.where(here, 0, 1)
        count[0] = count[0] + jnp.where(axis == 0, step, 0)
        count[1] = count[1] + jnp.where(axis == 1, step, 0)
    for axis in range(2):
        slot = jnp.int32(0)
        for row in range(ROWS):
            element = user[ROWS * (1 + axis) + row]
            here = element >= 0
            at = element * 4 + axis
            table[jnp.where(here, UPP + at, SPARE)] = ELEMENTS + slot
            table[jnp.where(here, ROW_UPP + at, SPARE)] = ROWS + axis * SLOTS + slot
            table[jnp.where(here, SEND_UP + axis * SLOTS + slot, SPARE)] = element
            slot = slot + jnp.where(here, 1, 0)
    for axis, out in enumerate((down_x, down_y)):
        for slot in range(4):
            at = SEND_ROW + axis * SLOTS + slot
            out[slot] = jnp.concatenate([source[table[at]], source[table[at + 4]]], axis=1)


def split_kernel(matrix, high, low):
    def body(element, _):
        full = matrix[element]
        top = full.astype(jnp.bfloat16)
        high[element] = top
        low[element] = (full - top.astype(jnp.float32)).astype(jnp.bfloat16)
        return 0

    lax.fori_loop(0, ELEMENTS, body, 0)


def multiply(table, get, high, low, vector, flux, ups, downs, moments, left):
    low_half = in_low_half((SOURCES, 128))
    norm = jnp.zeros((SOURCES, 128), jnp.float32)
    energy = jnp.zeros((SOURCES, 128), jnp.float32)
    for element in range(ELEMENTS):
        tiles = []
        for axis in range(3):
            tile = get(element, axis)
            tiles.append(tile)
            vector[element, axis] = tile
            norm = norm + tile * tile
            first = tile.astype(jnp.bfloat16)
            rest = tile - first.astype(jnp.float32)
            second = rest.astype(jnp.bfloat16)
            third = (rest - second.astype(jnp.float32)).astype(jnp.bfloat16)
            for part, value in enumerate((first, second, third)):
                left[element, part * 16 : part * 16 + 16, axis * 128 : axis * 128 + 128] = value
        rows = left[element]
        by_high = jnp.dot(rows, high[element], preferred_element_type=jnp.float32)
        by_low = jnp.dot(rows[:32], low[element], preferred_element_type=jnp.float32)
        total = by_high[0:16] + (by_high[16:32] + by_low[0:16] + (by_high[32:48] + by_low[16:32]))
        for axis in range(3):
            part = total[:, axis * 128 : axis * 128 + 128]
            flux[element, axis] = part
            energy = energy + tiles[axis] * part
    for axis in range(2):
        for slot in range(4):
            at = SEND_UP + axis * SLOTS + slot
            ups[axis][slot] = jnp.where(
                low_half, pltpu.roll(flux[table[at + 4], axis], 64, 1), flux[table[at], axis]
            )
            if downs is not None:
                at = SEND_DOWN + axis * SLOTS + slot
                downs[axis][slot] = jnp.where(
                    low_half, flux[table[at], axis], pltpu.roll(flux[table[at + 4], axis], 64, 1)
                )
    lane = lax.broadcasted_iota(jnp.int32, (SOURCES, 128), 1)
    half_norm = 0.5 * jnp.sum(norm, axis=1, keepdims=True)
    whole_energy = jnp.sum(energy, axis=1, keepdims=True)
    moments[...] = jnp.where(lane == 0, half_norm, jnp.where(lane == 1, whole_energy, 0.0))


def first_kernel(table, source, ghost_x, ghost_y, high, low,
                 vector, flux, up_x, up_y, down_x, down_y, moments, rows, left):
    for row in range(ROWS):
        rows[row] = source[row]
    for axis, ghost in enumerate((ghost_x, ghost_y)):
        for slot in range(4):
            rows[ROWS + axis * SLOTS + slot] = ghost[slot][:, :BLOCK]
            rows[ROWS + axis * SLOTS + slot + 4] = ghost[slot][:, BLOCK:]

    def get(element, axis):
        at = element * 4 + axis
        return jnp.concatenate([rows[table[ROW_LOW + at]], rows[table[ROW_UPP + at]]], axis=1)

    multiply(table, get, high, low, vector, flux, (up_x, up_y), (down_x, down_y), moments, left)


def gather_flux(previous, nexts, prevs, every):
    low_half = in_low_half((SOURCES, 128))
    every[0:ELEMENTS] = previous[...]
    for axis in range(2):
        for slot in range(4):
            ahead = nexts[axis][slot]
            behind = prevs[axis][slot]
            every[ELEMENTS + slot, axis] = jnp.where(low_half, ahead, behind)
            every[ELEMENTS + slot + 4, axis] = pltpu.roll(jnp.where(low_half, behind, ahead), 64, 1)


def later_kernel(last, table, previous, next_x, next_y, prev_x, prev_y, high, low,
                 vector, flux, up_x, up_y, *rest):
    if last:
        moments, every, left = rest
        downs = None
    else:
        down_x, down_y, moments, every, left = rest
        downs = (down_x, down_y)
    low_half = in_low_half((SOURCES, 128))
    gather_flux(previous, (next_x, next_y), (prev_x, prev_y), every)

    def get(element, axis):
        at = element * 4 + axis
        across = jnp.where(low_half, every[table[UPP + at], axis], every[table[LOW + at], axis])
        return every[element, axis] + pltpu.roll(across, 64, 1)

    multiply(table, get, high, low, vector, flux, (up_x, up_y), downs, moments, left)


def final_kernel(table, sums, zeroth, firsts, seconds, flux, prev_x, prev_y, answer, residual, every):
    mu = [sums[:, i : i + 1] for i in range(6)]
    centre_0 = mu[1] / mu[0]
    bent = {i: mu[i + 1] - centre_0 * mu[i] for i in range(1, 5)}
    centre_1 = bent[2] / bent[1] - centre_0
    span_1 = bent[1] / mu[0]
    twice = {i: bent[i + 1] - centre_1 * bent[i] - span_1 * mu[i] for i in (2, 3)}
    centre_2 = twice[3] / twice[2] - bent[2] / bent[1]
    span_2 = twice[2] / bent[1]
    alpha_0 = 1.0 / centre_0
    beta_0 = span_1 * alpha_0 * alpha_0
    alpha_1 = 1.0 / (centre_1 - span_1 * alpha_0)
    beta_1 = span_2 * alpha_1 * alpha_1
    alpha_2 = 1.0 / (centre_2 - span_2 * alpha_1)
    low_half = in_low_half((SOURCES, 128))
    every[0:ELEMENTS] = flux[...]
    for axis, prev in enumerate((prev_x, prev_y)):
        for slot in range(4):
            behind = prev[slot]
            every[ELEMENTS + slot, axis] = behind
            every[ELEMENTS + slot + 4, axis] = pltpu.roll(behind, 64, 1)
    for element in range(ELEMENTS):
        for axis in range(3):
            at = element * 4 + axis
            k0 = zeroth[element, axis]
            k1 = firsts[element, axis]
            k2 = seconds[element, axis]
            k3 = every[element, axis] + pltpu.roll(every[table[LOW + at], axis], 64, 1)
            r1 = k0 - alpha_0 * k1
            ar1 = k1 - alpha_0 * k2
            aar1 = k2 - alpha_0 * k3
            d1 = r1 + beta_0 * k0
            ad1 = ar1 + beta_0 * k1
            aad1 = aar1 + beta_0 * k2
            r2 = r1 - alpha_1 * ad1
            ar2 = ar1 - alpha_1 * aad1
            d2 = r2 + beta_1 * d1
            ad2 = ar2 + beta_1 * ad1
            x = alpha_0 * k0 + (alpha_1 * d1 + alpha_2 * d2)
            r = r2 - alpha_2 * ad2
            row = table[ROW_LOW + at]
            answer[row] = x[:, :BLOCK]
            residual[row] = r[:, :BLOCK]


def passed(value, axis, target):
    count = lax.axis_size(axis)
    return lax.ppermute(value, axis, [(i, target(i)) for i in range(count)])


def ahead(value, axis):
    return passed(value, axis, lambda i: (i + 1) % lax.axis_size(axis))


def back(value, axis):
    return passed(value, axis, lambda i: (i - 1) % lax.axis_size(axis))


def over_all(value):
    for step in (1, 2, 4, 8, 16):
        value = value + passed(value, "gy", lambda i: i ^ step)
    for step in (1, 2):
        value = value + passed(value, "gx", lambda i: i ^ step)
    return value


def local(heat_source, stiffness, element_faces):
    outer, inner = lax.axis_size("gx"), lax.axis_size("gy")
    at_x, at_y = lax.axis_index("gx"), lax.axis_index("gy")
    ids = jnp.stack(
        [
            at_x * inner + at_y,
            (at_x + 1) % outer * inner + at_y,
            at_x * inner + (at_y + 1) % inner,
        ]
    ).astype(jnp.int32) * ROWS
    source = heat_source.reshape(ROWS, SOURCES, BLOCK)
    pack = vmem((4, SOURCES, 128))
    state = vmem((ELEMENTS, 3, SOURCES, 128))
    matrix = vmem((ELEMENTS, ORDER, ORDER), jnp.bfloat16)
    moment = vmem((SOURCES, 128))
    left = pltpu.VMEM((ELEMENTS, 48, ORDER), jnp.bfloat16)
    every = pltpu.VMEM((ELEMENTS + SLOTS, 3, SOURCES, 128), jnp.float32)

    table, down_x, down_y = pl.pallas_call(
        table_kernel,
        out_shape=(jax.ShapeDtypeStruct((TABLE,), jnp.int32), pack, pack),
        in_specs=[SMEM, SMEM, VMEM],
        out_specs=(SMEM, VMEM, VMEM),
        scratch_shapes=[pltpu.SMEM((ROWS,), jnp.int32), pltpu.SMEM((3 * ROWS,), jnp.int32)],
        compiler_params=params(),
        name="table",
    )(ids, element_faces.T, source)
    ghost_x, ghost_y = back(down_x, "gx"), back(down_y, "gy")
    high, low = pl.pallas_call(
        split_kernel,
        out_shape=(matrix, matrix),
        in_specs=[VMEM],
        out_specs=(VMEM, VMEM),
        compiler_params=params(),
        cost_estimate=pl.CostEstimate(flops=10_000_000, bytes_accessed=18 << 20, transcendentals=0),
        name="split",
    )(stiffness)
    k0, flux, up_x, up_y, down_x, down_y, moment_0 = pl.pallas_call(
        first_kernel,
        out_shape=(state, state, pack, pack, pack, pack, moment),
        in_specs=[SMEM] + [VMEM] * 5,
        out_specs=(VMEM,) * 7,
        scratch_shapes=[pltpu.VMEM((64, SOURCES, BLOCK), jnp.float32), left],
        compiler_params=params(),
        name="first",
    )(table, source, ghost_x, ghost_y, high, low)

    def exchanged():
        return back(down_x, "gx"), back(down_y, "gy"), ahead(up_x, "gx"), ahead(up_y, "gy")

    next_x, next_y, prev_x, prev_y = exchanged()
    k1, flux, up_x, up_y, down_x, down_y, moment_1 = pl.pallas_call(
        functools.partial(later_kernel, False),
        out_shape=(state, state, pack, pack, pack, pack, moment),
        in_specs=[SMEM] + [VMEM] * 7,
        out_specs=(VMEM,) * 7,
        scratch_shapes=[every, left],
        compiler_params=params(),
        name="second",
    )(table, flux, next_x, next_y, prev_x, prev_y, high, low)
    next_x, next_y, prev_x, prev_y = exchanged()
    k2, flux, up_x, up_y, moment_2 = pl.pallas_call(
        functools.partial(later_kernel, True),
        out_shape=(state, state, pack, pack, moment),
        in_specs=[SMEM] + [VMEM] * 7,
        out_specs=(VMEM,) * 5,
        scratch_shapes=[every, left],
        compiler_params=params(),
        name="third",
    )(table, flux, next_x, next_y, prev_x, prev_y, high, low)
    sums = over_all(
        jnp.concatenate(
            [moment_0[:, :2], moment_1[:, :2], moment_2[:, :2], jnp.zeros((SOURCES, 122), jnp.float32)],
            axis=1,
        )
    )
    prev_x, prev_y = ahead(up_x, "gx"), ahead(up_y, "gy")
    answer, residual = pl.pallas_call(
        final_kernel,
        out_shape=(vmem((ROWS, SOURCES, BLOCK)),) * 2,
        in_specs=[SMEM] + [VMEM] * 7,
        out_specs=(VMEM, VMEM),
        scratch_shapes=[every],
        compiler_params=params(),
        name="final",
    )(table, sums, k0, k1, k2, flux, prev_x, prev_y)
    return answer.reshape(ROWS, SOURCES * BLOCK), residual.reshape(ROWS, SOURCES * BLOCK)


def solution(mesh):
    return jax.shard_map(
        local,
        mesh=mesh,
        in_specs=(P(("gx", "gy"), None), P(("gx", "gy"), None, None), P(("gx", "gy"), None)),
        out_specs=(P(("gx", "gy"), None), P(("gx", "gy"), None)),
        check_vma=False,
    )
```

time: 488 us -> 75.9 us (0.16)
  blocking collectives: 316 us -> 0 us
  matrix products: 86.4 us -> 0 us
  local copies, waits for them, and re-layouts: 34.2 us -> 7.16 us
  waiting for transfers between devices: 20.9 us -> 38.2 us
  Pallas kernels: 0 us -> 13.2 us
  other arithmetic: 12.6 us -> 0.18 us
    psum x5 -> x0, blocking collectives: 316 us -> none  [the longest x3 192 us: squares(): return lax.psum(source_sum(residual, residual), ('gx', 'gy'))]
    dot_general x3 -> x0, matrix products: 86.4 us -> none  [local(): jnp.einsum('ekbjc,ejsc->eksb', matrix, blocks, precision=lax.Precision.HI...]
    ppermute x14 -> x19, waiting for transfers between devices: 20.9 us -> 38.2 us  [passed(): return lax.ppermute(value, axis, [(i, target(i)) for i in range(count)])]
    reshape x7 -> x3, local copies, waits for them, and re-layouts: 18.5 us -> 2.71 us  [the longest x1 1.05 us: local(): source = heat_source.reshape(ROWS, SOURCES, BLOCK)]
    pallas_call x0 -> x6, Pallas kernels: none -> 13.2 us  [the longest x1 2.5 us: local(): pl.pallas_call(table_kernel, out_shape=(jax.ShapeDtypeStruct((TABLE,), jn...]
    gather x17 -> x0, local copies, waits for them, and re-layouts: 12.2 us -> none  [the longest x3 2.64 us: local(): send_got_y = passed_along(direction[wanted_y], 'gy', -1)]
    scatter-add x9 -> x0, other arithmetic: 8.74 us -> none  [the longest x6 4.52 us: local(): applied = result.at[wanted_x].add(got_x).at[wanted_y].add(got_y)]
    ppermute x14 -> x19, starting transfers between devices: 15.1 us -> 16.2 us  [passed(): return lax.ppermute(value, axis, [(i, target(i)) for i in range(count)])]
  transfers between devices with their start and end apart: 14 -> 19, of which waited for: 10 -> 13; matrix products, arithmetic and copies ran while one was open for 6% -> 0% of each run, Pallas kernels for 0% -> 2%
where the time goes in v1:
time: 75.9 us; the launch traced here: 75.7 us
  waiting for transfers between devices  38.2 us (50%)
  starting transfers between devices  16.2 us (21%)
  Pallas kernels  13.2 us (17%)
  local copies, waits for them, and re-layouts  7.16 us (9%)
  between operations  0.76 us (1%)
    ppermute x19, waiting for transfers between devices, passed(): return lax.ppermute(value, axis, [(i, target(i)) for i in range(count)])  38.2 us
    ppermute x19, starting transfers between devices, passed(): return lax.ppermute(value, axis, [(i, target(i)) for i in range(count)])  16.2 us
    unnamed x4, local copies, waits for them, and re-layouts  4.37 us
    pallas_call x1, Pallas kernels, local(): pl.pallas_call(table_kernel, out_shape=(jax.ShapeDtypeStruct((TABLE,), jn...  2.5 us
    pallas_call x1, Pallas kernels, local(): pl.pallas_call(functools.partial(later_kernel, False), out_shape=(state,...  2.49 us
    pallas_call x1, Pallas kernels, local(): pl.pallas_call(functools.partial(later_kernel, True), out_shape=(state, s...  2.47 us
    pallas_call x1, Pallas kernels, local(): pl.pallas_call(first_kernel, out_shape=(state, state, pack, pack, pack, p...  2.46 us
    pallas_call x1, Pallas kernels, local(): pl.pallas_call(split_kernel, out_shape=(matrix, matrix), in_specs=[VMEM],...  1.79 us
  transfers between devices with their start and end apart: 19, of which 13 were waited for; matrix products, arithmetic and copies ran while one was open for 0% of the time, Pallas kernels for 2%

profile of v1, /device:TPU:0, one launch (start us, length us, event | category | flops | bytes accessed | tf_op | source)
XLA Modules:
  0.0 75.7 jit_solution(4372832289558999769)
XLA Ops:
  0.7 1.0 %reshape.13.source = f32[48,16,64]{2,1,0:T(8,128)S(1)} reshape(f32[48,1024]{1,0:T(8,128)} %param.3) | data formatting | bytes 393216 | tf_op jit(solution)/shard_map/reshape | solution.py:267
  1.7 0.1 add_multiply_fusion.ids
  1.8 0.7 copy-done.1
  2.5 2.5 %table.1 = (s32[312]{0:T(512)S(1)}, f32[4,16,128]{2,1,0:T(8,128)S(1)}, f32[4,16,128]{2,1,0:T(8,128)S(1)}) custom-call(s32[3]{0:T(128)S(1)} %add_multiply_fusion.ids, s32[6,16]{1,0:T(8,128)S(1)} %bitcast.10, f32[48,16,64]{2,1,0:T(8,128)S(1)} %reshape.13.source), custom_call_target="tpu_custom_call" | custom-call | tf_op jit(solution)/shard_map/table/pallas_call | solution.py:275
  5.0 4.2 %collective-permute-start = (f32[4,16,128]{2,1,0:T(8,128)S(1)}, f32[4,16,128]{2,1,0:T(8,128)S(1)}, u32[]{:S(2)}, u32[]{:S(2)}) collective-permute-start(f32[4,16,128]{2,1,0:T(8,128)S(1)} %get-tuple-element.29), channel_id=1, source_target_pairs={{0,96},{32,0},{64,32},{96,64},{1,97},{33,1},{65,33},{97,65},{2,98}... | collective-permute-start | bytes 98312 | tf_op jit(solution)/shard_map/ppermute | solution.py:238
  9.2 4.4 %collective-permute-start.1 = (f32[4,16,128]{2,1,0:T(8,128)S(1)}, f32[4,16,128]{2,1,0:T(8,128)S(1)}, u32[]{:S(2)}, u32[]{:S(2)}) collective-permute-start(f32[4,16,128]{2,1,0:T(8,128)S(1)} %get-tuple-element.30), channel_id=1, source_target_pairs={{0,31},{1,0},{2,1},{3,2},{4,3},{5,4},{6,5},{7,6},{8,7},{9,8},{10,9... | collective-permute-start | bytes 98312 | tf_op jit(solution)/shard_map/ppermute | solution.py:238
  13.5 3.7 %copy-done = f32[16,384,384]{2,1,0:T(8,128)S(1)} copy-done((f32[16,384,384]{2,1,0:T(8,128)S(1)}, f32[16,384,384]{2,1,0:T(8,128)}, u32[]{:S(2)}) %copy-start) | copy-done | bytes 9437208
  17.2 1.8 %split.1 = (bf16[16,384,384]{2,1,0:T(8,128)(2,1)S(1)}, bf16[16,384,384]{2,1,0:T(8,128)(2,1)S(1)}) custom-call(f32[16,384,384]{2,1,0:T(8,128)S(1)} %copy-done), custom_call_target="tpu_custom_call" | custom-call | flops 10000000 | bytes 18874368 | tf_op jit(solution)/shard_map/split/pallas_call | solution.py:285
  19.0 0.0 collective-permute-done.ghost_x
  19.0 2.5 %first.1 = (f32[16,3,16,128]{3,2,1,0:T(8,128)S(1)}, f32[16,3,16,128]{3,2,1,0:T(8,128)S(1)}, f32[4,16,128]{2,1,0:T(8,128)S(1)}, f32[4,16,128]{2,1,0:T(8,128)S(1)}...) custom-call(s32[312]{0:T(512)S(1)} %get-tuple-element.28.table, ...), custom_call_target="tpu_custom_call" | custom-call | tf_op jit(solution)/shard_map/first/pallas_call | solution.py:294
  21.5 0.5 collective-permute-start.2
  22.0 0.9 %collective-permute-start.3 = (f32[4,16,128]{2,1,0:T(8,128)S(1)}, f32[4,16,128]{2,1,0:T(8,128)S(1)}, u32[]{:S(2)}, u32[]{:S(2)}) collective-permute-start(f32[4,16,128]{2,1,0:T(8,128)S(1)} %get-tuple-element.36), channel_id=1, source_target_pairs={{0,31},{1,0},{2,1},{3,2},{4,3},{5,4},{6,5},{7,6},{8,7},{9,8},{10,9... | collective-permute-start | bytes 98312 | tf_op jit(solution)/shard_map/ppermute | solution.py:238
  22.9 1.6 %collective-permute-start.4 = (f32[4,16,128]{2,1,0:T(8,128)S(1)}, f32[4,16,128]{2,1,0:T(8,128)S(1)}, u32[]{:S(2)}, u32[]{:S(2)}) collective-permute-start(f32[4,16,128]{2,1,0:T(8,128)S(1)} %get-tuple-element.37), channel_id=1, source_target_pairs={{0,32},{32,64},{64,96},{96,0},{1,33},{33,65},{65,97},{97,1},{2,34}... | collective-permute-start | bytes 98312 | tf_op jit(solution)/shard_map/ppermute | solution.py:238
  24.5 1.0 %collective-permute-done.2.next_x = f32[4,16,128]{2,1,0:T(8,128)S(1)} collective-permute-done((f32[4,16,128]{2,1,0:T(8,128)S(1)}, f32[4,16,128]{2,1,0:T(8,128)S(1)}, u32[]{:S(2)}, u32[]{:S(2)}) %collective-permute-start.2) | collective-permute-done | bytes 32800 | tf_op jit(solution)/shard_map/ppermute | solution.py:238
  25.5 0.0 collective-permute-done.3.next_y
  25.5 2.5 %collective-permute-done.4.prev_x = f32[4,16,128]{2,1,0:T(8,128)S(1)} collective-permute-done((f32[4,16,128]{2,1,0:T(8,128)S(1)}, f32[4,16,128]{2,1,0:T(8,128)S(1)}, u32[]{:S(2)}, u32[]{:S(2)}) %collective-permute-start.4) | collective-permute-done | bytes 32800 | tf_op jit(solution)/shard_map/ppermute | solution.py:238
  28.0 3.2 %collective-permute-done.5.prev_y = f32[4,16,128]{2,1,0:T(8,128)S(1)} collective-permute-done((f32[4,16,128]{2,1,0:T(8,128)S(1)}, f32[4,16,128]{2,1,0:T(8,128)S(1)}, u32[]{:S(2)}, u32[]{:S(2)}) %collective-permute-start.5) | collective-permute-done | bytes 32800 | tf_op jit(solution)/shard_map/ppermute | solution.py:238
  31.1 2.5 %second.1 = (f32[16,3,16,128]{3,2,1,0:T(8,128)S(1)}, f32[16,3,16,128]{3,2,1,0:T(8,128)S(1)}, f32[4,16,128]{2,1,0:T(8,128)S(1)}, f32[4,16,128]{2,1,0:T(8,128)S(1)...) custom-call(s32[312]{0:T(512)S(1)} %get-tuple-element.28.table, ...), custom_call_target="tpu_custom_call" | custom-call | tf_op jit(solution)/shard_map/second/pallas_call | solution.py:308
  33.6 1.7 %collective-permute-start.6 = (f32[4,16,128]{2,1,0:T(8,128)S(1)}, f32[4,16,128]{2,1,0:T(8,128)S(1)}, u32[]{:S(2)}, u32[]{:S(2)}) collective-permute-start(f32[4,16,128]{2,1,0:T(8,128)S(1)} %get-tuple-element.41), channel_id=1, source_target_pairs={{0,96},{32,0},{64,32},{96,64},{1,97},{33,1},{65,33},{97,65},{2,98}... | collective-permute-start | bytes 98312 | tf_op jit(solution)/shard_map/ppermute | solution.py:238
  35.3 0.0 collective-permute-start.7
  35.3 0.4 collective-permute-start.8
  35.7 0.2 collective-permute-start.9
  36.0 0.1 pad.3.clone
  36.0 1.6 %collective-permute-done.6.next_x = f32[4,16,128]{2,1,0:T(8,128)S(1)} collective-permute-done((f32[4,16,128]{2,1,0:T(8,128)S(1)}, f32[4,16,128]{2,1,0:T(8,128)S(1)}, u32[]{:S(2)}, u32[]{:S(2)}) %collective-permute-start.6) | collective-permute-done | bytes 32800 | tf_op jit(solution)/shard_map/ppermute | solution.py:238
  37.6 2.8 %collective-permute-done.8.prev_x = f32[4,16,128]{2,1,0:T(8,128)S(1)} collective-permute-done((f32[4,16,128]{2,1,0:T(8,128)S(1)}, f32[4,16,128]{2,1,0:T(8,128)S(1)}, u32[]{:S(2)}, u32[]{:S(2)}) %collective-permute-start.8) | collective-permute-done | bytes 32800 | tf_op jit(solution)/shard_map/ppermute | solution.py:238
  40.5 1.9 %collective-permute-done.9.prev_y = f32[4,16,128]{2,1,0:T(8,128)S(1)} collective-permute-done((f32[4,16,128]{2,1,0:T(8,128)S(1)}, f32[4,16,128]{2,1,0:T(8,128)S(1)}, u32[]{:S(2)}, u32[]{:S(2)}) %collective-permute-start.9) | collective-permute-done | bytes 32800 | tf_op jit(solution)/shard_map/ppermute | solution.py:238
  42.4 2.5 %third.1 = (f32[16,3,16,128]{3,2,1,0:T(8,128)S(1)}, f32[16,3,16,128]{3,2,1,0:T(8,128)S(1)}, f32[4,16,128]{2,1,0:T(8,128)S(1)}, f32[4,16,128]{2,1,0:T(8,128)S(1)}, f32[16,128]{1,0:T(8,128)S(1)}) custom-call(s32[312]{0:T(512)S(1)} %get-tuple-element.28.table, f32[16,3,16,128]{3,2,1,0:T(8,128)S(1)} %get-tuple-element.40.previous, ...), custom_call_target="tpu_custom_call" | custom-call | tf_op jit(solution)/shard_map/third/pallas_call | solution.py:318
  44.9 0.1 maximum_maximum_fusion
  45.0 0.0 collective-permute-start.10
  45.0 1.2 %collective-permute-done.10 = f32[16,128]{1,0:T(8,128)S(1)} collective-permute-done((f32[16,128]{1,0:T(8,128)S(1)}, f32[16,128]{1,0:T(8,128)S(1)}, u32[]{:S(2)}, u32[]{:S(2)}) %collective-permute-start.10) | collective-permute-done | bytes 8224 | tf_op jit(solution)/shard_map/ppermute | solution.py:238
  46.2 0.0 collective-permute-start.11
  46.2 3.6 %collective-permute-done.11 = f32[16,128]{1,0:T(8,128)S(1)} collective-permute-done((f32[16,128]{1,0:T(8,128)S(1)}, f32[16,128]{1,0:T(8,128)S(1)}, u32[]{:S(2)}, u32[]{:S(2)}) %collective-permute-start.11) | collective-permute-done | bytes 8224 | tf_op jit(solution)/shard_map/ppermute | solution.py:238
  49.8 0.0 collective-permute-start.12
  49.8 5.2 %collective-permute-done.12 = f32[16,128]{1,0:T(8,128)S(1)} collective-permute-done((f32[16,128]{1,0:T(8,128)S(1)}, f32[16,128]{1,0:T(8,128)S(1)}, u32[]{:S(2)}, u32[]{:S(2)}) %collective-permute-start.12) | collective-permute-done | bytes 8224 | tf_op jit(solution)/shard_map/ppermute | solution.py:238
  55.0 0.0 collective-permute-start.17
  55.0 0.1 collective-permute-start.18
  55.1 3.6 %collective-permute-done.13 = f32[16,128]{1,0:T(8,128)S(1)} collective-permute-done((f32[16,128]{1,0:T(8,128)S(1)}, f32[16,128]{1,0:T(8,128)S(1)}, u32[]{:S(2)}, u32[]{:S(2)}) %collective-permute-start.13) | collective-permute-done | bytes 8224 | tf_op jit(solution)/shard_map/ppermute | solution.py:238
  58.6 0.0 collective-permute-start.14
  58.6 5.2 %collective-permute-done.14 = f32[16,128]{1,0:T(8,128)S(1)} collective-permute-done((f32[16,128]{1,0:T(8,128)S(1)}, f32[16,128]{1,0:T(8,128)S(1)}, u32[]{:S(2)}, u32[]{:S(2)}) %collective-permute-start.14) | collective-permute-done | bytes 8224 | tf_op jit(solution)/shard_map/ppermute | solution.py:238
  63.8 0.0 collective-permute-start.15
  63.8 3.6 %collective-permute-done.15 = f32[16,128]{1,0:T(8,128)S(1)} collective-permute-done((f32[16,128]{1,0:T(8,128)S(1)}, f32[16,128]{1,0:T(8,128)S(1)}, u32[]{:S(2)}, u32[]{:S(2)}) %collective-permute-start.15) | collective-permute-done | bytes 8224 | tf_op jit(solution)/shard_map/ppermute | solution.py:238
  67.4 2.3 %collective-permute-start.16 = (f32[16,128]{1,0:T(8,128)S(1)}, f32[16,128]{1,0:T(8,128)S(1)}, u32[]{:S(2)}, u32[]{:S(2)}) collective-permute-start(f32[16,128]{1,0:T(8,128)S(1)} %add.55), channel_id=1, source_target_pairs={{0,64},{32,96},{64,0},{96,32},{1,65},{33,97},{65,1},{97,33},{2,66}... | collective-permute-start | bytes 24584 | tf_op jit(solution)/shard_map/ppermute | solution.py:238
  69.7 2.9 %collective-permute-done.16 = f32[16,128]{1,0:T(8,128)S(1)} collective-permute-done((f32[16,128]{1,0:T(8,128)S(1)}, f32[16,128]{1,0:T(8,128)S(1)}, u32[]{:S(2)}, u32[]{:S(2)}) %collective-permute-start.16) | collective-permute-done | bytes 8224 | tf_op jit(solution)/shard_map/ppermute | solution.py:238
  72.6 0.0 collective-permute-done.17.prev_x
  72.6 0.0 collective-permute-done.18.prev_y
  72.6 1.5 %final.1 = (f32[48,16,64]{2,1,0:T(8,128)S(1)}, f32[48,16,64]{2,1,0:T(8,128)S(1)}) custom-call(s32[312]{0:T(512)S(1)} %get-tuple-element.28.table, f32[16,128]{1,0:T(8,128)S(1)} %add.56.sums, f32[16,3,16,128]{3,2,1,0:T(8,128)S(1)} %get-tuple-element.46.zeroth, f32[16,3,16,128]{3,2,1,0:T(8,128)S(1)} %get-tuple-element.47.firsts, ...), custom_call_target="tpu_custom_call" | custom-call | tf_op jit(solution)/shard_map/final/pallas_call | solution.py:334
  74.1 0.8 %reshape.14 = f32[48,1024]{1,0:T(8,128)} reshape(f32[48,16,64]{2,1,0:T(8,128)S(1)} %get-tuple-element.52) | data formatting | bytes 393216 | tf_op jit(solution)/shard_map/reshape | solution.py:343
  74.9 0.8 %reshape.15 = f32[48,1024]{1,0:T(8,128)} reshape(f32[48,16,64]{2,1,0:T(8,128)S(1)} %get-tuple-element.53) | data formatting | bytes 393216 | tf_op jit(solution)/shard_map/reshape | solution.py:343
  (14 shorter events, 0.0 us)
Async XLA Ops:
  1.8 0.7 copy-start.1
  5.0 14.0 %collective-permute-start = (f32[4,16,128]{2,1,0:T(8,128)S(1)}, f32[4,16,128]{2,1,0:T(8,128)S(1)}, u32[]{:S(2)}, u32[]{:S(2)}) collective-permute-start(f32[4,16,128]{2,1,0:T(8,128)S(1)} %get-tuple-element.29), channel_id=1, source_target_pairs={{0,96},{32,0},{64,32},{96,64},{1,97},{33,1},{65,33},{97,65},{2,98}... | collective-permute-start | bytes 98312 | tf_op jit(solution)/shard_map/ppermute | solution.py:238
  9.2 9.9 %collective-permute-start.1 = (f32[4,16,128]{2,1,0:T(8,128)S(1)}, f32[4,16,128]{2,1,0:T(8,128)S(1)}, u32[]{:S(2)}, u32[]{:S(2)}) collective-permute-start(f32[4,16,128]{2,1,0:T(8,128)S(1)} %get-tuple-element.30), channel_id=1, source_target_pairs={{0,31},{1,0},{2,1},{3,2},{4,3},{5,4},{6,5},{7,6},{8,7},{9,8},{10,9... | collective-permute-start | bytes 98312 | tf_op jit(solution)/shard_map/ppermute | solution.py:238
  13.5 3.7 %copy-start = (f32[16,384,384]{2,1,0:T(8,128)S(1)}, f32[16,384,384]{2,1,0:T(8,128)}, u32[]{:S(2)}) copy-start(f32[16,384,384]{2,1,0:T(8,128)} %matrix.1) | copy-start | bytes 28311556
  21.5 4.0 %collective-permute-start.2 = (f32[4,16,128]{2,1,0:T(8,128)S(1)}, f32[4,16,128]{2,1,0:T(8,128)S(1)}, u32[]{:S(2)}, u32[]{:S(2)}) collective-permute-start(f32[4,16,128]{2,1,0:T(8,128)S(1)} %get-tuple-element.35), channel_id=1, source_target_pairs={{0,96},{32,0},{64,32},{96,64},{1,97},{33,1},{65,33},{97,65},{2,98}... | collective-permute-start | bytes 98312 | tf_op jit(solution)/shard_map/ppermute | solution.py:238
  22.0 3.5 %collective-permute-start.3 = (f32[4,16,128]{2,1,0:T(8,128)S(1)}, f32[4,16,128]{2,1,0:T(8,128)S(1)}, u32[]{:S(2)}, u32[]{:S(2)}) collective-permute-start(f32[4,16,128]{2,1,0:T(8,128)S(1)} %get-tuple-element.36), channel_id=1, source_target_pairs={{0,31},{1,0},{2,1},{3,2},{4,3},{5,4},{6,5},{7,6},{8,7},{9,8},{10,9... | collective-permute-start | bytes 98312 | tf_op jit(solution)/shard_map/ppermute | solution.py:238
  22.9 5.1 %collective-permute-start.4 = (f32[4,16,128]{2,1,0:T(8,128)S(1)}, f32[4,16,128]{2,1,0:T(8,128)S(1)}, u32[]{:S(2)}, u32[]{:S(2)}) collective-permute-start(f32[4,16,128]{2,1,0:T(8,128)S(1)} %get-tuple-element.37), channel_id=1, source_target_pairs={{0,32},{32,64},{64,96},{96,0},{1,33},{33,65},{65,97},{97,1},{2,34}... | collective-permute-start | bytes 98312 | tf_op jit(solution)/shard_map/ppermute | solution.py:238
  24.5 6.7 %collective-permute-start.5 = (f32[4,16,128]{2,1,0:T(8,128)S(1)}, f32[4,16,128]{2,1,0:T(8,128)S(1)}, u32[]{:S(2)}, u32[]{:S(2)}) collective-permute-start(f32[4,16,128]{2,1,0:T(8,128)S(1)} %get-tuple-element.38), channel_id=1, source_target_pairs={{0,1},{1,2},{2,3},{3,4},{4,5},{5,6},{6,7},{7,8},{8,9},{9,10},{10,1... | collective-permute-start | bytes 98312 | tf_op jit(solution)/shard_map/ppermute | solution.py:238
  33.6 4.0 %collective-permute-start.6 = (f32[4,16,128]{2,1,0:T(8,128)S(1)}, f32[4,16,128]{2,1,0:T(8,128)S(1)}, u32[]{:S(2)}, u32[]{:S(2)}) collective-permute-start(f32[4,16,128]{2,1,0:T(8,128)S(1)} %get-tuple-element.41), channel_id=1, source_target_pairs={{0,96},{32,0},{64,32},{96,64},{1,97},{33,1},{65,33},{97,65},{2,98}... | collective-permute-start | bytes 98312 | tf_op jit(solution)/shard_map/ppermute | solution.py:238
  35.3 2.3 %collective-permute-start.7 = (f32[4,16,128]{2,1,0:T(8,128)S(1)}, f32[4,16,128]{2,1,0:T(8,128)S(1)}, u32[]{:S(2)}, u32[]{:S(2)}) collective-permute-start(f32[4,16,128]{2,1,0:T(8,128)S(1)} %get-tuple-element.42), channel_id=1, source_target_pairs={{0,31},{1,0},{2,1},{3,2},{4,3},{5,4},{6,5},{7,6},{8,7},{9,8},{10,9... | collective-permute-start | bytes 98312 | tf_op jit(solution)/shard_map/ppermute | solution.py:238
  35.3 5.1 %collective-permute-start.8 = (f32[4,16,128]{2,1,0:T(8,128)S(1)}, f32[4,16,128]{2,1,0:T(8,128)S(1)}, u32[]{:S(2)}, u32[]{:S(2)}) collective-permute-start(f32[4,16,128]{2,1,0:T(8,128)S(1)} %get-tuple-element.43), channel_id=1, source_target_pairs={{0,32},{32,64},{64,96},{96,0},{1,33},{33,65},{65,97},{97,1},{2,34}... | collective-permute-start | bytes 98312 | tf_op jit(solution)/shard_map/ppermute | solution.py:238
  35.7 6.7 %collective-permute-start.9 = (f32[4,16,128]{2,1,0:T(8,128)S(1)}, f32[4,16,128]{2,1,0:T(8,128)S(1)}, u32[]{:S(2)}, u32[]{:S(2)}) collective-permute-start(f32[4,16,128]{2,1,0:T(8,128)S(1)} %get-tuple-element.44), channel_id=1, source_target_pairs={{0,1},{1,2},{2,3},{3,4},{4,5},{5,6},{6,7},{7,8},{8,9},{9,10},{10,1... | collective-permute-start | bytes 98312 | tf_op jit(solution)/shard_map/ppermute | solution.py:238
  45.0 1.2 %collective-permute-start.10 = (f32[16,128]{1,0:T(8,128)S(1)}, f32[16,128]{1,0:T(8,128)S(1)}, u32[]{:S(2)}, u32[]{:S(2)}) collective-permute-start(f32[16,128]{1,0:T(8,128)S(1)} %maximum_maximum_fusion), channel_id=1, source_target_pairs={{0,1},{1,0},{2,3},{3,2},{4,5},{5,4},{6,7},{7,6},{8,9},{9,8},{10,11... | collective-permute-start | bytes 24584 | tf_op jit(solution)/shard_map/ppermute | solution.py:238
  46.2 3.7 %collective-permute-start.11 = (f32[16,128]{1,0:T(8,128)S(1)}, f32[16,128]{1,0:T(8,128)S(1)}, u32[]{:S(2)}, u32[]{:S(2)}) collective-permute-start(f32[16,128]{1,0:T(8,128)S(1)} %add.50), channel_id=1, source_target_pairs={{0,2},{1,3},{2,0},{3,1},{4,6},{5,7},{6,4},{7,5},{8,10},{9,11},{10,... | collective-permute-start | bytes 24584 | tf_op jit(solution)/shard_map/ppermute | solution.py:238
  49.8 5.2 %collective-permute-start.12 = (f32[16,128]{1,0:T(8,128)S(1)}, f32[16,128]{1,0:T(8,128)S(1)}, u32[]{:S(2)}, u32[]{:S(2)}) collective-permute-start(f32[16,128]{1,0:T(8,128)S(1)} %add.51), channel_id=1, source_target_pairs={{0,4},{1,5},{2,6},{3,7},{4,0},{5,1},{6,2},{7,3},{8,12},{9,13},{10,... | collective-permute-start | bytes 24584 | tf_op jit(solution)/shard_map/ppermute | solution.py:238
  55.0 3.7 %collective-permute-start.13 = (f32[16,128]{1,0:T(8,128)S(1)}, f32[16,128]{1,0:T(8,128)S(1)}, u32[]{:S(2)}, u32[]{:S(2)}) collective-permute-start(f32[16,128]{1,0:T(8,128)S(1)} %add.52), channel_id=1, source_target_pairs={{0,8},{1,9},{2,10},{3,11},{4,12},{5,13},{6,14},{7,15},{8,0},{9,1},... | collective-permute-start | bytes 24584 | tf_op jit(solution)/shard_map/ppermute | solution.py:238
  55.0 17.6 %collective-permute-start.17 = (f32[4,16,128]{2,1,0:T(8,128)S(1)}, f32[4,16,128]{2,1,0:T(8,128)S(1)}, u32[]{:S(2)}, u32[]{:S(2)}) collective-permute-start(f32[4,16,128]{2,1,0:T(8,128)S(1)} %get-tuple-element.50), channel_id=1, source_target_pairs={{0,32},{32,64},{64,96},{96,0},{1,33},{33,65},{65,97},{97,1},{2,34}... | collective-permute-start | bytes 98312 | tf_op jit(solution)/shard_map/ppermute | solution.py:238
  55.0 17.6 %collective-permute-start.18 = (f32[4,16,128]{2,1,0:T(8,128)S(1)}, f32[4,16,128]{2,1,0:T(8,128)S(1)}, u32[]{:S(2)}, u32[]{:S(2)}) collective-permute-start(f32[4,16,128]{2,1,0:T(8,128)S(1)} %get-tuple-element.51), channel_id=1, source_target_pairs={{0,1},{1,2},{2,3},{3,4},{4,5},{5,6},{6,7},{7,8},{8,9},{9,10},{10,1... | collective-permute-start | bytes 98312 | tf_op jit(solution)/shard_map/ppermute | solution.py:238
  58.6 5.2 %collective-permute-start.14 = (f32[16,128]{1,0:T(8,128)S(1)}, f32[16,128]{1,0:T(8,128)S(1)}, u32[]{:S(2)}, u32[]{:S(2)}) collective-permute-start(f32[16,128]{1,0:T(8,128)S(1)} %add.53), channel_id=1, source_target_pairs={{0,16},{1,17},{2,18},{3,19},{4,20},{5,21},{6,22},{7,23},{8,24},{9,... | collective-permute-start | bytes 24584 | tf_op jit(solution)/shard_map/ppermute | solution.py:238
  63.8 3.7 %collective-permute-start.15 = (f32[16,128]{1,0:T(8,128)S(1)}, f32[16,128]{1,0:T(8,128)S(1)}, u32[]{:S(2)}, u32[]{:S(2)}) collective-permute-start(f32[16,128]{1,0:T(8,128)S(1)} %add.54), channel_id=1, source_target_pairs={{0,32},{32,0},{64,96},{96,64},{1,33},{33,1},{65,97},{97,65},{2,34}... | collective-permute-start | bytes 24584 | tf_op jit(solution)/shard_map/ppermute | solution.py:238
  67.4 5.2 %collective-permute-start.16 = (f32[16,128]{1,0:T(8,128)S(1)}, f32[16,128]{1,0:T(8,128)S(1)}, u32[]{:S(2)}, u32[]{:S(2)}) collective-permute-start(f32[16,128]{1,0:T(8,128)S(1)} %add.55), channel_id=1, source_target_pairs={{0,64},{32,96},{64,0},{96,32},{1,65},{33,97},{65,1},{97,33},{2,66}... | collective-permute-start | bytes 24584 | tf_op jit(solution)/shard_map/ppermute | solution.py:238

commit v2 on v1

v2 whole, which is shorter than its diff:
```python
import functools

import jax
import jax.numpy as jnp
from jax import lax
from jax.experimental import pallas as pl
from jax.experimental.pallas import tpu as pltpu
from jax.sharding import PartitionSpec as P

BLOCK = 64
SOURCES = 16
ELEMENTS = 16
ROWS = 48
SLOTS = 8
ORDER = 384
EARLY = 10

LOW = 0
UPP = 64
ROW_LOW = 128
ROW_UPP = 192
SEND_UP = 256
SEND_DOWN = 272
SEND_ROW = 288
SPARE = 304
ODD = 305
TABLE = 312

VMEM = pl.BlockSpec(memory_space=pltpu.VMEM)
SMEM = pl.BlockSpec(memory_space=pltpu.SMEM)
HBM = pl.BlockSpec(memory_space=pltpu.HBM)


def params(mebibytes=24):
    return pltpu.CompilerParams(vmem_limit_bytes=mebibytes << 20)


def vmem(shape, dtype=jnp.float32):
    return pltpu.VMEM(shape, dtype)


def in_low_half(shape):
    return lax.broadcasted_iota(jnp.int32, shape, len(shape) - 1) < BLOCK


def matrix_copies(matrix, target, begin, end, sems):
    return [
        pltpu.make_async_copy(matrix.at[i], target.at[i - begin], sems.at[i - begin])
        for i in range(begin, end)
    ]


def table_kernel(ids, faces, source, matrix, table, pairs, down_x, down_y, early, owner, user, sems):
    copies = matrix_copies(matrix, early, 0, EARLY, sems)
    for copy in copies:
        copy.start()
    own = ids[0]
    for axis in range(2):
        table[ODD + axis] = ids[3 + axis]
    for row in range(3 * ROWS):
        user[row] = -1
    for element in range(ELEMENTS):
        for axis in range(3):
            at = element * 4 + axis
            row = faces[2 * axis, element] - own
            owner[row] = at
            table[ROW_LOW + at] = row
            face = faces[2 * axis + 1, element]
            row = face - own
            if axis < 2:
                here = jnp.logical_and(row >= 0, row < ROWS)
                row = jnp.where(here, row, face - ids[1 + axis])
            user[row] = element
            table[ROW_UPP + at] = row
    for group in range(ROWS // 8):
        for pair in range(8):
            pairs[pl.ds(group * 64 + pair, 8, stride=8), :] = source[
                group * 8 : group * 8 + 8, pair * 128 : pair * 128 + 128
            ]
    count = [jnp.int32(0), jnp.int32(0)]
    for row in range(ROWS):
        ref = owner[row]
        axis = ref & 3
        element = ref >> 2
        other = user[row]
        here = other >= 0
        slot = jnp.where(axis == 0, count[0], count[1])
        table[LOW + ref] = jnp.where(here, other, ELEMENTS + slot)
        table[jnp.where(here, UPP + other * 4 + axis, SPARE)] = element
        table[jnp.where(here, SPARE, SEND_DOWN + axis * SLOTS + slot)] = element
        table[jnp.where(here, SPARE, SEND_ROW + axis * SLOTS + slot)] = row
        step = jnp.where(here, 0, 1)
        count[0] = count[0] + jnp.where(axis == 0, step, 0)
        count[1] = count[1] + jnp.where(axis == 1, step, 0)
    for axis in range(2):
        slot = jnp.int32(0)
        for row in range(ROWS):
            element = user[ROWS * (1 + axis) + row]
            here = element >= 0
            at = element * 4 + axis
            table[jnp.where(here, UPP + at, SPARE)] = ELEMENTS + slot
            table[jnp.where(here, ROW_UPP + at, SPARE)] = ROWS + axis * SLOTS + slot
            table[jnp.where(here, SEND_UP + axis * SLOTS + slot, SPARE)] = element
            slot = slot + jnp.where(here, 1, 0)
    for axis, out in enumerate((down_x, down_y)):
        for slot in range(SLOTS):
            row = table[SEND_ROW + axis * SLOTS + slot]
            out[slot] = pairs[pl.ds(pl.multiple_of(row * 8, 8), 8), :]
    for copy in copies:
        copy.wait()


def split_kernel(early, matrix, high, low, late, sems):
    copies = matrix_copies(matrix, late, EARLY, ELEMENTS, sems)
    for copy in copies:
        copy.start()

    def split(full, element):
        top = full.astype(jnp.bfloat16)
        high[element] = top
        low[element] = (full - top.astype(jnp.float32)).astype(jnp.bfloat16)

    @pl.loop(0, EARLY)
    def _(element):
        split(early[element], element)

    for i, copy in enumerate(copies):
        copy.wait()
        split(late[i], EARLY + i)


def multiply(step, table, get, high, low, vector, flux, sends, moments, sums, left):
    low_half = in_low_half((SOURCES, 128))
    norm = jnp.zeros((SOURCES, 128), jnp.float32)
    energy = jnp.zeros((SOURCES, 128), jnp.float32)
    for element in range(ELEMENTS):
        tiles = []
        for axis in range(3):
            tile = get(element, axis)
            tiles.append(tile)
            if vector is not None:
                vector[element, axis] = tile
            if step < 2:
                norm = norm + tile * tile
            first = tile.astype(jnp.bfloat16)
            rest = tile - first.astype(jnp.float32)
            second = rest.astype(jnp.bfloat16)
            third = (rest - second.astype(jnp.float32)).astype(jnp.bfloat16)
            for part, value in enumerate((first, second, third)):
                left[element, part * 16 : part * 16 + 16, axis * 128 : axis * 128 + 128] = value
        rows = left[element]
        by_high = jnp.dot(rows, high[element], preferred_element_type=jnp.float32)
        by_low = jnp.dot(rows[:32], low[element], preferred_element_type=jnp.float32)
        total = by_high[0:16] + (by_high[16:32] + by_low[0:16] + (by_high[32:48] + by_low[16:32]))
        for axis in range(3):
            part = total[:, axis * 128 : axis * 128 + 128]
            flux[element, axis] = part
            if step < 2:
                energy = energy + tiles[axis] * part
    for axis in range(2):
        for slot in range(4):
            at = SEND_UP + axis * SLOTS + slot
            up = jnp.where(
                low_half, pltpu.roll(flux[table[at + 4], axis], 64, 1), flux[table[at], axis]
            )
            if step == 2:
                sends[axis][slot] = up
                continue
            at = SEND_DOWN + axis * SLOTS + slot
            down = jnp.where(
                low_half, flux[table[at], axis], pltpu.roll(flux[table[at + 4], axis], 64, 1)
            )
            odd = table[ODD + axis] == 1
            sends[2 * axis][slot] = jnp.where(odd, down, up)
            sends[2 * axis + 1][slot] = jnp.where(odd, up, down)
    if step < 2:
        sums[...] = with_moments(step, norm, energy, moments)


def with_moments(step, norm, energy, moments):
    shape = (SOURCES, 128)
    lane = lax.broadcasted_iota(jnp.int32, shape, 1)
    source = lax.broadcasted_iota(jnp.int32, shape, 0)
    half_norm = 0.5 * jnp.sum(norm, axis=1, keepdims=True)
    whole_energy = jnp.sum(energy, axis=1, keepdims=True)
    before = jnp.zeros(shape, jnp.float32) if moments is None else moments[...]
    place = lane - 2 * step * SOURCES - source
    return jnp.where(place == 0, half_norm, jnp.where(place == SOURCES, whole_energy, before))


def share_kernel(vector, flux, moments, shares):
    norm = jnp.zeros((SOURCES, 128), jnp.float32)
    energy = jnp.zeros((SOURCES, 128), jnp.float32)
    for element in range(ELEMENTS):
        for axis in range(3):
            tile = vector[element, axis]
            norm = norm + tile * tile
            energy = energy + tile * flux[element, axis]
    now = with_moments(2, norm, energy, moments)
    shares[...] = jnp.broadcast_to(jnp.sum(now, axis=0, keepdims=True), shares.shape)


def tile_of(below, above):
    low_half = in_low_half((8, 128))
    even = jnp.where(low_half, below, pltpu.roll(above, 64, 1))
    odd = jnp.where(low_half, pltpu.roll(below, 64, 1), above)
    return jnp.concatenate([even, odd], axis=0)


def first_kernel(table, pairs, ghost_x, ghost_y, high, low,
                 flux, xa, xb, ya, yb, sums, rows, left):
    for row in range(ROWS):
        rows[row] = pairs[row * 8 : row * 8 + 8, :]
    for axis, ghost in enumerate((ghost_x, ghost_y)):
        for slot in range(SLOTS):
            rows[ROWS + axis * SLOTS + slot] = ghost[slot]

    def get(element, axis):
        at = element * 4 + axis
        return tile_of(rows[table[ROW_LOW + at]], rows[table[ROW_UPP + at]])

    multiply(0, table, get, high, low, None, flux, (xa, xb, ya, yb), None, sums, left)


def gather_flux(table, previous, received, every):
    low_half = in_low_half((SOURCES, 128))
    every[0:ELEMENTS] = previous[...]
    for axis in range(2):
        ahead_low = jnp.logical_xor(low_half, table[ODD + axis] == 1)
        for slot in range(4):
            one = received[2 * axis][slot]
            two = received[2 * axis + 1][slot]
            every[ELEMENTS + slot, axis] = jnp.where(ahead_low, one, two)
            every[ELEMENTS + slot + 4, axis] = pltpu.roll(jnp.where(ahead_low, two, one), 64, 1)


def later_kernel(step, table, previous, yb, xa, xb, ya, *rest):
    if step == 1:
        moments, high, low, vector, flux, *sends, sums, every, left = rest
    else:
        high, low, vector, flux, *sends, every, left = rest
        moments = sums = None
    low_half = in_low_half((SOURCES, 128))
    gather_flux(table, previous, (xa, xb, ya, yb), every)

    def get(element, axis):
        at = element * 4 + axis
        across = jnp.where(low_half, every[table[UPP + at], axis], every[table[LOW + at], axis])
        return every[element, axis] + pltpu.roll(across, 64, 1)

    multiply(step, table, get, high, low, vector, flux, sends, moments, sums, left)


def two_sum(a, b):
    total = a + b
    part = total - a
    return total, (a - (total - part)) + (b - part)


def halves(a):
    big = 4097.0 * a
    top = big - (big - a)
    return top, a - top


def two_product(a, b):
    total = a * b
    a1, a2 = halves(a)
    b1, b2 = halves(b)
    return total, ((a1 * b1 - total) + a1 * b2 + a2 * b1) + a2 * b2


def quick(a, b):
    total = a + b
    return total, b - (total - a)


def pair_times(a, b):
    total, rest = two_product(a[0], b[0])
    return quick(total, rest + (a[0] * b[1] + a[1] * b[0]))


def pair_minus(a, b):
    total, rest = two_sum(a[0], -b[0])
    return quick(total, rest + (a[1] - b[1]))


def pair_over(a, b):
    first = a[0] / b[0]
    left = pair_minus(a, pair_times((first, jnp.zeros_like(first)), b))
    return quick(first, left[0] / b[0])


def coefficients(mu):
    centre_0 = pair_over(mu[1], mu[0])
    bent = {i: pair_minus(mu[i + 1], pair_times(centre_0, mu[i])) for i in range(1, 5)}
    slope_1 = pair_over(bent[2], bent[1])
    centre_1 = pair_minus(slope_1, centre_0)
    span_1 = pair_over(bent[1], mu[0])
    twice = {
        i: pair_minus(
            pair_minus(bent[i + 1], pair_times(centre_1, bent[i])), pair_times(span_1, mu[i])
        )
        for i in (2, 3)
    }
    centre_2 = twice[3][0] / twice[2][0] - slope_1[0]
    span_2 = twice[2][0] / bent[1][0]
    alpha_0 = 1.0 / centre_0[0]
    beta_0 = span_1[0] * alpha_0 * alpha_0
    alpha_1 = 1.0 / (centre_1[0] - span_1[0] * alpha_0)
    beta_1 = span_2 * alpha_1 * alpha_1
    alpha_2 = 1.0 / (centre_2 - span_2 * alpha_1)
    return alpha_0, beta_0, alpha_1, beta_1, alpha_2


def total_of(shares):
    parts = [(shares[i : i + 8], jnp.zeros((8, 128), jnp.float32)) for i in range(0, shares.shape[0], 8)]

    def add(a, b):
        total, lost = two_sum(a[0], b[0])
        return total, a[1] + b[1] + lost

    while len(parts) > 1:
        parts = [add(a, b) for a, b in zip(parts[::2], parts[1::2])]
    value = parts[0]
    for shift in (4, 2, 1):
        value = add(value, tuple(pltpu.roll(v, shift, 0) for v in value))
    return value


def final_kernel(table, shares, pairs, firsts, seconds, flux, prev_x, prev_y, answer, residual,
                 every, answer_pairs, residual_pairs):
    low_half = in_low_half((8, 128))
    total = total_of(shares)
    lane = lax.broadcasted_iota(jnp.int32, (8, 128), 1)
    row_of = lax.broadcasted_iota(jnp.int32, (8, 128), 0)

    def packed(tile):
        return jnp.where(low_half, tile[:8], pltpu.roll(tile[8:], 64, 1))

    def moment(part, i):
        even = jnp.sum(jnp.where(lane == i * SOURCES + row_of, total[part], 0.0), axis=1, keepdims=True)
        odd = jnp.sum(jnp.where(lane == i * SOURCES + 8 + row_of, total[part], 0.0), axis=1, keepdims=True)
        return jnp.where(low_half, even, odd)

    mu = [(moment(0, i), moment(1, i)) for i in range(6)]
    alpha_0, beta_0, alpha_1, beta_1, alpha_2 = coefficients(mu)
    every[0:ELEMENTS] = flux[...]
    for axis, prev in enumerate((prev_x, prev_y)):
        for slot in range(4):
            every[ELEMENTS + slot, axis] = prev[slot]
            every[ELEMENTS + slot + 4, axis] = pltpu.roll(prev[slot], 64, 1)
    for element in range(ELEMENTS):
        for axis in range(3):
            at = element * 4 + axis
            row = pl.ds(pl.multiple_of(table[ROW_LOW + at] * 8, 8), 8)
            other = every[table[LOW + at], axis]
            k0 = pairs[row, :]
            k1 = packed(firsts[element, axis])
            k2 = packed(seconds[element, axis])
            k3 = packed(every[element, axis]) + jnp.where(low_half, pltpu.roll(other[:8], 64, 1), other[8:])
            r1 = k0 - alpha_0 * k1
            ar1 = k1 - alpha_0 * k2
            aar1 = k2 - alpha_0 * k3
            d1 = r1 + beta_0 * k0
            ad1 = ar1 + beta_0 * k1
            aad1 = aar1 + beta_0 * k2
            r2 = r1 - alpha_1 * ad1
            ar2 = ar1 - alpha_1 * aad1
            d2 = r2 + beta_1 * d1
            ad2 = ar2 + beta_1 * ad1
            answer_pairs[row, :] = alpha_0 * k0 + (alpha_1 * d1 + alpha_2 * d2)
            residual_pairs[row, :] = r2 - alpha_2 * ad2
    for block, out in ((answer_pairs, answer), (residual_pairs, residual)):
        for group in range(ROWS // 8):
            for pair in range(8):
                out[group * 8 : group * 8 + 8, pair * 128 : pair * 128 + 128] = block[
                    pl.ds(group * 64 + pair, 8, stride=8), :
                ]


def passed(value, axis, target):
    count = lax.axis_size(axis)
    return lax.ppermute(value, axis, [(i, target(i)) for i in range(count)])


def ahead(value, axis):
    return passed(value, axis, lambda i: (i + 1) % lax.axis_size(axis))


def back(value, axis):
    return passed(value, axis, lambda i: (i - 1) % lax.axis_size(axis))


def swapped(value, axis, turn):
    count = lax.axis_size(axis)
    return passed(value, axis, lambda i: (i + 1 - 2 * ((i + turn) % 2)) % count)


def exchanged(sends):
    xa, xb, ya, yb = sends
    yb = swapped(yb, "gy", 1)
    return yb, swapped(xa, "gx", 0), swapped(xb, "gx", 1), swapped(ya, "gy", 0)


def local(heat_source, stiffness, element_faces):
    outer, inner = lax.axis_size("gx"), lax.axis_size("gy")
    at_x, at_y = lax.axis_index("gx"), lax.axis_index("gy")
    ids = jnp.stack(
        [
            (at_x * inner + at_y) * ROWS,
            ((at_x + 1) % outer * inner + at_y) * ROWS - ROWS,
            (at_x * inner + (at_y + 1) % inner) * ROWS - 2 * ROWS,
            at_x % 2,
            at_y % 2,
        ]
    ).astype(jnp.int32)
    pack = vmem((4, SOURCES, 128))
    face = vmem((SLOTS, 8, 128))
    state = vmem((ELEMENTS, 3, SOURCES, 128))
    matrix = vmem((ELEMENTS, ORDER, ORDER), jnp.bfloat16)
    moment = vmem((SOURCES, 128))
    left = pltpu.VMEM((ELEMENTS, 48, ORDER), jnp.bfloat16)
    every = pltpu.VMEM((ELEMENTS + SLOTS, 3, SOURCES, 128), jnp.float32)
    pairs_shape = (ROWS * 8, 128)

    table, pairs, down_x, down_y, early = pl.pallas_call(
        table_kernel,
        out_shape=(
            pltpu.SMEM((TABLE,), jnp.int32),
            vmem(pairs_shape),
            face,
            face,
            vmem((EARLY, ORDER, ORDER)),
        ),
        in_specs=[SMEM, SMEM, VMEM, HBM],
        out_specs=(SMEM, VMEM, VMEM, VMEM, VMEM),
        scratch_shapes=[
            pltpu.SMEM((ROWS,), jnp.int32),
            pltpu.SMEM((3 * ROWS,), jnp.int32),
            pltpu.SemaphoreType.DMA((EARLY,)),
        ],
        compiler_params=params(52),
        name="table",
    )(ids, element_faces.T, heat_source, stiffness)
    ghost_x, ghost_y = back(down_x, "gx"), back(down_y, "gy")
    high, low = pl.pallas_call(
        split_kernel,
        out_shape=(matrix, matrix),
        in_specs=[VMEM, HBM],
        out_specs=(VMEM, VMEM),
        scratch_shapes=[
            pltpu.VMEM((ELEMENTS - EARLY, ORDER, ORDER), jnp.float32),
            pltpu.SemaphoreType.DMA((ELEMENTS - EARLY,)),
        ],
        compiler_params=params(34),
        cost_estimate=pl.CostEstimate(flops=10_000_000, bytes_accessed=18 << 20, transcendentals=0),
        name="split",
    )(early, stiffness)
    flux, *sends, moments = pl.pallas_call(
        first_kernel,
        out_shape=(state, pack, pack, pack, pack, moment),
        in_specs=[SMEM] + [VMEM] * 5,
        out_specs=(VMEM,) * 6,
        scratch_shapes=[pltpu.VMEM((64, 8, 128), jnp.float32), left],
        compiler_params=params(),
        name="first",
    )(table, pairs, ghost_x, ghost_y, high, low)
    k1, flux, *sends, moments = pl.pallas_call(
        functools.partial(later_kernel, 1),
        out_shape=(state, state, pack, pack, pack, pack, moment),
        in_specs=[SMEM] + [VMEM] * 8,
        out_specs=(VMEM,) * 7,
        scratch_shapes=[every, left],
        compiler_params=params(),
        name="second",
    )(table, flux, *exchanged(sends), moments, high, low)
    k2, flux, up_x, up_y = pl.pallas_call(
        functools.partial(later_kernel, 2),
        out_shape=(state, state, pack, pack),
        in_specs=[SMEM] + [VMEM] * 7,
        out_specs=(VMEM,) * 4,
        scratch_shapes=[every, left],
        compiler_params=params(),
        name="third",
    )(table, flux, *exchanged(sends), high, low)
    shares = pl.pallas_call(
        share_kernel,
        out_shape=vmem((outer * inner, 128)),
        in_specs=[VMEM] * 3,
        out_specs=VMEM,
        compiler_params=params(),
        cost_estimate=pl.CostEstimate(flops=0, bytes_accessed=18 << 20, transcendentals=0),
        name="share",
    )(k2, flux, moments)
    prev_x, prev_y = ahead(up_x, "gx"), ahead(up_y, "gy")
    shares = lax.all_to_all(shares, ("gx", "gy"), 0, 0, tiled=True)
    natural = jax.ShapeDtypeStruct((ROWS, SOURCES * BLOCK), jnp.float32)
    return pl.pallas_call(
        final_kernel,
        out_shape=(natural, natural),
        in_specs=[SMEM] + [VMEM] * 7,
        out_specs=(VMEM, VMEM),
        scratch_shapes=[every, pltpu.VMEM(pairs_shape, jnp.float32), pltpu.VMEM(pairs_shape, jnp.float32)],
        compiler_params=params(),
        name="final",
    )(table, shares, pairs, k1, k2, flux, prev_x, prev_y)


def solution(mesh):
    return jax.shard_map(
        local,
        mesh=mesh,
        in_specs=(P(("gx", "gy"), None), P(("gx", "gy"), None, None), P(("gx", "gy"), None)),
        out_specs=(P(("gx", "gy"), None), P(("gx", "gy"), None)),
        check_vma=False,
    )
```

time: 75.9 us -> 54.7 us (0.72)
  waiting for transfers between devices: 38.2 us -> 16.8 us
  local copies, waits for them, and re-layouts: 7.16 us -> 0.61 us
  starting transfers between devices: 16.2 us -> 22.3 us
    ppermute x19 -> x12, waiting for transfers between devices: 38.2 us -> 15.4 us  [passed(): return lax.ppermute(value, axis, [(i, target(i)) for i in range(count)])]
    all_to_all x0 -> x1, starting transfers between devices: none -> 4.88 us  [local(): shares = lax.all_to_all(shares, ('gx', 'gy'), 0, 0, tiled=True)]
    unnamed x4 -> x0, local copies, waits for them, and re-layouts: 4.37 us -> none
    reshape x3 -> x0, local copies, waits for them, and re-layouts: 2.71 us -> none  [the longest x1 1.05 us: local(): source = heat_source.reshape(ROWS, SOURCES, BLOCK)]
    all_to_all x0 -> x1, waiting for transfers between devices: none -> 1.42 us  [local(): shares = lax.all_to_all(shares, ('gx', 'gy'), 0, 0, tiled=True)]
    ppermute x19 -> x12, starting transfers between devices: 16.2 us -> 17.5 us  [passed(): return lax.ppermute(value, axis, [(i, target(i)) for i in range(count)])]
    pallas_call x6 -> x7, Pallas kernels: 13.2 us -> 13.3 us  [the longest x1 3.69 us: local(): pl.pallas_call(table_kernel, out_shape=(pltpu.SMEM((TABLE,), jnp.int32),...]
  transfers between devices with their start and end apart: 19 -> 13, of which waited for: 13 -> 7; matrix products, arithmetic and copies ran while one was open for 0% -> 0% of each run, Pallas kernels for 2% -> 4%
where the time goes in v2:
time: 54.7 us; the launch traced here: 53.8 us
  starting transfers between devices  22.3 us (41%)
  waiting for transfers between devices  16.8 us (31%)
  Pallas kernels  13.3 us (24%)
  between operations  0.74 us (1%)
  local copies, waits for them, and re-layouts  0.61 us (1%)
    ppermute x12, starting transfers between devices, passed(): return lax.ppermute(value, axis, [(i, target(i)) for i in range(count)])  17.5 us
    ppermute x12, waiting for transfers between devices, passed(): return lax.ppermute(value, axis, [(i, target(i)) for i in range(count)])  15.4 us
    all_to_all x1, starting transfers between devices, local(): shares = lax.all_to_all(shares, ('gx', 'gy'), 0, 0, tiled=True)  4.88 us
    pallas_call x1, Pallas kernels, local(): pl.pallas_call(table_kernel, out_shape=(pltpu.SMEM((TABLE,), jnp.int32),...  3.69 us
    pallas_call x1, Pallas kernels, local(): pl.pallas_call(split_kernel, out_shape=(matrix, matrix), in_specs=[VMEM,...  2.11 us
    pallas_call x1, Pallas kernels, local(): pl.pallas_call(functools.partial(later_kernel, 1), out_shape=(state, stat...  1.88 us
    pallas_call x1, Pallas kernels, local(): pl.pallas_call(functools.partial(later_kernel, 2), out_shape=(state, stat...  1.85 us
    pallas_call x1, Pallas kernels, local(): pl.pallas_call(first_kernel, out_shape=(state, pack, pack, pack, pack, mo...  1.8 us
  transfers between devices with their start and end apart: 13, of which 7 were waited for; matrix products, arithmetic and copies ran while one was open for 0% of the time, Pallas kernels for 4%

profile of v2, /device:TPU:0, one launch (start us, length us, event | category | flops | bytes accessed | tf_op | source)
XLA Modules:
  0.0 53.8 jit_solution(7990379126532893137)
XLA Ops:
  0.7 0.6 %stack.23.ids = s32[5]{0:T(128)} concatenate(s32[1]{0:T(128)} %bitcast, s32[1]{0:T(128)} %bitcast.1, s32[1]{0:T(128)} %bitcast.2, s32[1]{0:T(128)} %bitcast.3, s32[1]{0:T(128)} %bitcast.4), dimensions={0} | concatenate | bytes 40 | tf_op jit(solution)/shard_map/stack | solution.py:409
  1.3 3.7 %table.1 = (s32[312]{0:T(512)S(4)}, f32[384,128]{1,0:T(8,128)S(1)}, f32[8,8,128]{2,1,0:T(8,128)S(1)}, f32[8,8,128]{2,1,0:T(8,128)S(1)}, f32[10,384,384]{2,1,0:T(8,128)S(1)}) custom-call(s32[5]{0:T(128)} %stack.23.ids, s32[6,16]{1,0:T(8,128)} %bitcast.11, f32[48,1024]{1,0:T(8,128)} %source.1, f32[16,384,384]{2,1,0:T(8,128)} %matrix.3), custom_call_target="tpu_custom_call" | custom-call | tf_op jit(solution)/shard_map/table/pallas_call | solution.py:427
  5.0 4.2 %collective-permute-start = (f32[8,8,128]{2,1,0:T(8,128)S(1)}, f32[8,8,128]{2,1,0:T(8,128)S(1)}, u32[]{:S(2)}, u32[]{:S(2)}) collective-permute-start(f32[8,8,128]{2,1,0:T(8,128)S(1)} %get-tuple-element.28), channel_id=1, source_target_pairs={{0,96},{32,0},{64,32},{96,64},{1,97},{33,1},{65,33},{97,65},{2,98}... | collective-permute-start | bytes 98312 | tf_op jit(solution)/shard_map/ppermute | solution.py:384
  9.2 4.4 %collective-permute-start.1 = (f32[8,8,128]{2,1,0:T(8,128)S(1)}, f32[8,8,128]{2,1,0:T(8,128)S(1)}, u32[]{:S(2)}, u32[]{:S(2)}) collective-permute-start(f32[8,8,128]{2,1,0:T(8,128)S(1)} %get-tuple-element.29), channel_id=1, source_target_pairs={{0,31},{1,0},{2,1},{3,2},{4,3},{5,4},{6,5},{7,6},{8,7},{9,8},{10,9... | collective-permute-start | bytes 98312 | tf_op jit(solution)/shard_map/ppermute | solution.py:384
  13.5 2.1 %split.1 = (bf16[16,384,384]{2,1,0:T(8,128)(2,1)S(1)}, bf16[16,384,384]{2,1,0:T(8,128)(2,1)S(1)}) custom-call(f32[10,384,384]{2,1,0:T(8,128)S(1)} %get-tuple-element.30.early, f32[16,384,384]{2,1,0:T(8,128)} %matrix.3), custom_call_target="tpu_custom_call" | custom-call | flops 10000000 | bytes 18874368 | tf_op jit(solution)/shard_map/split/pallas_call | solution.py:447
  15.7 0.0 collective-permute-done.ghost_x
  15.7 0.0 collective-permute-done.1.ghost_y
  15.7 1.8 %first.1 = (f32[16,3,16,128]{3,2,1,0:T(8,128)S(1)}, f32[4,16,128]{2,1,0:T(8,128)S(1)}, f32[4,16,128]{2,1,0:T(8,128)S(1)}, f32[4,16,128]{2,1,0:T(8,128)S(1)}, f32...) custom-call(s32[312]{0:T(512)S(4)} %get-tuple-element.26.table, f32[384,128]{1,0:T(8,128)S(1)} %get-tuple-element.27.pairs, ...), custom_call_target="tpu_custom_call" | custom-call | tf_op jit(solution)/shard_map/first/pallas_call | solution.py:460
  17.5 4.6 %collective-permute-start.2 = (f32[4,16,128]{2,1,0:T(8,128)S(1)}, f32[4,16,128]{2,1,0:T(8,128)S(1)}, u32[]{:S(2)}, u32[]{:S(2)}) collective-permute-start(f32[4,16,128]{2,1,0:T(8,128)S(1)} %get-tuple-element.34), channel_id=1, source_target_pairs={{0,31},{1,2},{2,1},{3,4},{4,3},{5,6},{6,5},{7,8},{8,7},{9,10},{10,... | collective-permute-start | bytes 98312 | tf_op jit(solution)/shard_map/ppermute | solution.py:384
  22.1 0.0 collective-permute-start.3
  22.1 0.8 %collective-permute-start.4 = (f32[4,16,128]{2,1,0:T(8,128)S(1)}, f32[4,16,128]{2,1,0:T(8,128)S(1)}, u32[]{:S(2)}, u32[]{:S(2)}) collective-permute-start(f32[4,16,128]{2,1,0:T(8,128)S(1)} %get-tuple-element.36), channel_id=1, source_target_pairs={{0,96},{32,64},{64,32},{96,0},{1,97},{33,65},{65,33},{97,1},{2,98}... | collective-permute-start | bytes 98312 | tf_op jit(solution)/shard_map/ppermute | solution.py:384
  22.8 0.0 collective-permute-start.5
  22.9 1.4 %collective-permute-done.2.yb = f32[4,16,128]{2,1,0:T(8,128)S(1)} collective-permute-done((f32[4,16,128]{2,1,0:T(8,128)S(1)}, f32[4,16,128]{2,1,0:T(8,128)S(1)}, u32[]{:S(2)}, u32[]{:S(2)}) %collective-permute-start.2) | collective-permute-done | bytes 32800 | tf_op jit(solution)/shard_map/ppermute | solution.py:384
  24.2 1.8 %collective-permute-done.3.xa = f32[4,16,128]{2,1,0:T(8,128)S(1)} collective-permute-done((f32[4,16,128]{2,1,0:T(8,128)S(1)}, f32[4,16,128]{2,1,0:T(8,128)S(1)}, u32[]{:S(2)}, u32[]{:S(2)}) %collective-permute-start.3) | collective-permute-done | bytes 32800 | tf_op jit(solution)/shard_map/ppermute | solution.py:384
  26.0 1.2 %collective-permute-done.4.xb = f32[4,16,128]{2,1,0:T(8,128)S(1)} collective-permute-done((f32[4,16,128]{2,1,0:T(8,128)S(1)}, f32[4,16,128]{2,1,0:T(8,128)S(1)}, u32[]{:S(2)}, u32[]{:S(2)}) %collective-permute-start.4) | collective-permute-done | bytes 32800 | tf_op jit(solution)/shard_map/ppermute | solution.py:384
  27.2 0.0 collective-permute-done.5.ya
  27.2 1.9 %second.1 = (f32[16,3,16,128]{3,2,1,0:T(8,128)S(1)}, f32[16,3,16,128]{3,2,1,0:T(8,128)S(1)}, f32[4,16,128]{2,1,0:T(8,128)S(1)}, f32[4,16,128]{2,1,0:T(8,128)S(1)...) custom-call(s32[312]{0:T(512)S(4)} %get-tuple-element.26.table, ...), custom_call_target="tpu_custom_call" | custom-call | tf_op jit(solution)/shard_map/second/pallas_call | solution.py:469
  29.1 1.6 %collective-permute-start.6 = (f32[4,16,128]{2,1,0:T(8,128)S(1)}, f32[4,16,128]{2,1,0:T(8,128)S(1)}, u32[]{:S(2)}, u32[]{:S(2)}) collective-permute-start(f32[4,16,128]{2,1,0:T(8,128)S(1)} %get-tuple-element.40), channel_id=1, source_target_pairs={{0,31},{1,2},{2,1},{3,4},{4,3},{5,6},{6,5},{7,8},{8,7},{9,10},{10,... | collective-permute-start | bytes 98312 | tf_op jit(solution)/shard_map/ppermute | solution.py:384
  30.7 0.0 collective-permute-start.7
  30.7 0.8 %collective-permute-start.8 = (f32[4,16,128]{2,1,0:T(8,128)S(1)}, f32[4,16,128]{2,1,0:T(8,128)S(1)}, u32[]{:S(2)}, u32[]{:S(2)}) collective-permute-start(f32[4,16,128]{2,1,0:T(8,128)S(1)} %get-tuple-element.42), channel_id=1, source_target_pairs={{0,96},{32,64},{64,32},{96,0},{1,97},{33,65},{65,33},{97,1},{2,98}... | collective-permute-start | bytes 98312 | tf_op jit(solution)/shard_map/ppermute | solution.py:384
  31.5 0.0 collective-permute-start.9
  31.5 4.3 %collective-permute-done.6.yb = f32[4,16,128]{2,1,0:T(8,128)S(1)} collective-permute-done((f32[4,16,128]{2,1,0:T(8,128)S(1)}, f32[4,16,128]{2,1,0:T(8,128)S(1)}, u32[]{:S(2)}, u32[]{:S(2)}) %collective-permute-start.6) | collective-permute-done | bytes 32800 | tf_op jit(solution)/shard_map/ppermute | solution.py:384
  35.8 0.0 collective-permute-done.7.xa
  35.8 0.0 collective-permute-done.8.xb
  35.9 0.0 collective-permute-done.9.ya
  35.9 1.8 %third.1 = (f32[16,3,16,128]{3,2,1,0:T(8,128)S(1)}, f32[16,3,16,128]{3,2,1,0:T(8,128)S(1)}, f32[4,16,128]{2,1,0:T(8,128)S(1)}, f32[4,16,128]{2,1,0:T(8,128)S(1)}) custom-call(s32[312]{0:T(512)S(4)} %get-tuple-element.26.table, f32[16,3,16,128]{3,2,1,0:T(8,128)S(1)} %get-tuple-element.39.previous, f32[4,16,128]{2,1,0:T(8,128)S(1)} %collective-permute-done.6.yb, ...), custom_call_target="tpu_custom_call" | custom-call | tf_op jit(solution)/shard_map/third/pallas_call | solution.py:478
  37.7 0.8 %share.1 = f32[128,128]{1,0:T(8,128)} custom-call(f32[16,3,16,128]{3,2,1,0:T(8,128)S(1)} %get-tuple-element.44.vector.seconds, f32[16,3,16,128]{3,2,1,0:T(8,128)S(1)} %get-tuple-element.45.flux, f32[16,128]{1,0:T(8,128)S(1)} %get-tuple-element.46.moments), custom_call_target="tpu_custom_call" | custom-call | bytes 18874368 | tf_op jit(solution)/shard_map/share/pallas_call | solution.py:487
  38.5 4.9 %all-to-all-start = ((f32[128,1,128]{2,1,0:T(1,128)}), f32[128,1,128]{2,1,0:T(1,128)S(1)}, u32[]{:S(2)}, u32[]{:S(2)}) async-start(f32[128,1,128]{2,1,0:T(1,128)} %bitcast.7), calls=%async_computation | async-start | bytes 131072 | tf_op jit(solution)/shard_map/all_to_all | solution.py:497
  43.4 1.1 %collective-permute-start.10 = (f32[4,16,128]{2,1,0:T(8,128)S(1)}, f32[4,16,128]{2,1,0:T(8,128)S(1)}, u32[]{:S(2)}, u32[]{:S(2)}) collective-permute-start(f32[4,16,128]{2,1,0:T(8,128)S(1)} %get-tuple-element.48), channel_id=1, source_target_pairs={{0,32},{32,64},{64,96},{96,0},{1,33},{33,65},{65,97},{97,1},{2,34}... | collective-permute-start | bytes 98312 | tf_op jit(solution)/shard_map/ppermute | solution.py:384
  44.5 0.0 collective-permute-start.11
  44.5 4.1 %collective-permute-done.10.prev_x = f32[4,16,128]{2,1,0:T(8,128)S(1)} collective-permute-done((f32[4,16,128]{2,1,0:T(8,128)S(1)}, f32[4,16,128]{2,1,0:T(8,128)S(1)}, u32[]{:S(2)}, u32[]{:S(2)}) %collective-permute-start.10) | collective-permute-done | bytes 32800 | tf_op jit(solution)/shard_map/ppermute | solution.py:384
  48.6 2.6 %collective-permute-done.11.prev_y = f32[4,16,128]{2,1,0:T(8,128)S(1)} collective-permute-done((f32[4,16,128]{2,1,0:T(8,128)S(1)}, f32[4,16,128]{2,1,0:T(8,128)S(1)}, u32[]{:S(2)}, u32[]{:S(2)}) %collective-permute-start.11) | collective-permute-done | bytes 32800 | tf_op jit(solution)/shard_map/ppermute | solution.py:384
  51.2 1.4 %all-to-all-done = f32[128,1,128]{2,1,0:T(1,128)S(1)} async-done(((f32[128,1,128]{2,1,0:T(1,128)}), f32[128,1,128]{2,1,0:T(1,128)S(1)}, u32[]{:S(2)}, u32[]{:S(2)}) %all-to-all-start) | async-done | bytes 65568 | tf_op jit(solution)/shard_map/all_to_all | solution.py:497
  52.6 1.2 %final.1 = (f32[48,1024]{1,0:T(8,128)}, f32[48,1024]{1,0:T(8,128)}) custom-call(s32[312]{0:T(512)S(4)} %get-tuple-element.26.table, f32[128,128]{1,0:T(8,128)S(1)} %bitcast.10, f32[384,128]{1,0:T(8,128)S(1)} %get-tuple-element.27.pairs, f32[16,3,16,128]{3,2,1,0:T(8,128)S(1)} %get-tuple-element.47.firsts, ...), custom_call_target="tpu_custom_call" | custom-call | tf_op jit(solution)/shard_map/final/pallas_call | solution.py:499
Async XLA Ops:
  5.0 10.7 %collective-permute-start = (f32[8,8,128]{2,1,0:T(8,128)S(1)}, f32[8,8,128]{2,1,0:T(8,128)S(1)}, u32[]{:S(2)}, u32[]{:S(2)}) collective-permute-start(f32[8,8,128]{2,1,0:T(8,128)S(1)} %get-tuple-element.28), channel_id=1, source_target_pairs={{0,96},{32,0},{64,32},{96,64},{1,97},{33,1},{65,33},{97,65},{2,98}... | collective-permute-start | bytes 98312 | tf_op jit(solution)/shard_map/ppermute | solution.py:384
  9.2 6.5 %collective-permute-start.1 = (f32[8,8,128]{2,1,0:T(8,128)S(1)}, f32[8,8,128]{2,1,0:T(8,128)S(1)}, u32[]{:S(2)}, u32[]{:S(2)}) collective-permute-start(f32[8,8,128]{2,1,0:T(8,128)S(1)} %get-tuple-element.29), channel_id=1, source_target_pairs={{0,31},{1,0},{2,1},{3,2},{4,3},{5,4},{6,5},{7,6},{8,7},{9,8},{10,9... | collective-permute-start | bytes 98312 | tf_op jit(solution)/shard_map/ppermute | solution.py:384
  17.5 6.7 %collective-permute-start.2 = (f32[4,16,128]{2,1,0:T(8,128)S(1)}, f32[4,16,128]{2,1,0:T(8,128)S(1)}, u32[]{:S(2)}, u32[]{:S(2)}) collective-permute-start(f32[4,16,128]{2,1,0:T(8,128)S(1)} %get-tuple-element.34), channel_id=1, source_target_pairs={{0,31},{1,2},{2,1},{3,4},{4,3},{5,6},{6,5},{7,8},{8,7},{9,10},{10,... | collective-permute-start | bytes 98312 | tf_op jit(solution)/shard_map/ppermute | solution.py:384
  22.1 3.9 %collective-permute-start.3 = (f32[4,16,128]{2,1,0:T(8,128)S(1)}, f32[4,16,128]{2,1,0:T(8,128)S(1)}, u32[]{:S(2)}, u32[]{:S(2)}) collective-permute-start(f32[4,16,128]{2,1,0:T(8,128)S(1)} %get-tuple-element.35), channel_id=1, source_target_pairs={{0,32},{32,0},{64,96},{96,64},{1,33},{33,1},{65,97},{97,65},{2,34}... | collective-permute-start | bytes 98312 | tf_op jit(solution)/shard_map/ppermute | solution.py:384
  22.1 5.1 %collective-permute-start.4 = (f32[4,16,128]{2,1,0:T(8,128)S(1)}, f32[4,16,128]{2,1,0:T(8,128)S(1)}, u32[]{:S(2)}, u32[]{:S(2)}) collective-permute-start(f32[4,16,128]{2,1,0:T(8,128)S(1)} %get-tuple-element.36), channel_id=1, source_target_pairs={{0,96},{32,64},{64,32},{96,0},{1,97},{33,65},{65,33},{97,1},{2,98}... | collective-permute-start | bytes 98312 | tf_op jit(solution)/shard_map/ppermute | solution.py:384
  22.8 4.4 %collective-permute-start.5 = (f32[4,16,128]{2,1,0:T(8,128)S(1)}, f32[4,16,128]{2,1,0:T(8,128)S(1)}, u32[]{:S(2)}, u32[]{:S(2)}) collective-permute-start(f32[4,16,128]{2,1,0:T(8,128)S(1)} %get-tuple-element.37), channel_id=1, source_target_pairs={{0,1},{1,0},{2,3},{3,2},{4,5},{5,4},{6,7},{7,6},{8,9},{9,8},{10,11... | collective-permute-start | bytes 98312 | tf_op jit(solution)/shard_map/ppermute | solution.py:384
  29.1 6.7 %collective-permute-start.6 = (f32[4,16,128]{2,1,0:T(8,128)S(1)}, f32[4,16,128]{2,1,0:T(8,128)S(1)}, u32[]{:S(2)}, u32[]{:S(2)}) collective-permute-start(f32[4,16,128]{2,1,0:T(8,128)S(1)} %get-tuple-element.40), channel_id=1, source_target_pairs={{0,31},{1,2},{2,1},{3,4},{4,3},{5,6},{6,5},{7,8},{8,7},{9,10},{10,... | collective-permute-start | bytes 98312 | tf_op jit(solution)/shard_map/ppermute | solution.py:384
  30.7 5.1 %collective-permute-start.7 = (f32[4,16,128]{2,1,0:T(8,128)S(1)}, f32[4,16,128]{2,1,0:T(8,128)S(1)}, u32[]{:S(2)}, u32[]{:S(2)}) collective-permute-start(f32[4,16,128]{2,1,0:T(8,128)S(1)} %get-tuple-element.41), channel_id=1, source_target_pairs={{0,32},{32,0},{64,96},{96,64},{1,33},{33,1},{65,97},{97,65},{2,34}... | collective-permute-start | bytes 98312 | tf_op jit(solution)/shard_map/ppermute | solution.py:384
  30.7 5.1 %collective-permute-start.8 = (f32[4,16,128]{2,1,0:T(8,128)S(1)}, f32[4,16,128]{2,1,0:T(8,128)S(1)}, u32[]{:S(2)}, u32[]{:S(2)}) collective-permute-start(f32[4,16,128]{2,1,0:T(8,128)S(1)} %get-tuple-element.42), channel_id=1, source_target_pairs={{0,96},{32,64},{64,32},{96,0},{1,97},{33,65},{65,33},{97,1},{2,98}... | collective-permute-start | bytes 98312 | tf_op jit(solution)/shard_map/ppermute | solution.py:384
  31.5 4.4 %collective-permute-start.9 = (f32[4,16,128]{2,1,0:T(8,128)S(1)}, f32[4,16,128]{2,1,0:T(8,128)S(1)}, u32[]{:S(2)}, u32[]{:S(2)}) collective-permute-start(f32[4,16,128]{2,1,0:T(8,128)S(1)} %get-tuple-element.43), channel_id=1, source_target_pairs={{0,1},{1,0},{2,3},{3,2},{4,5},{5,4},{6,7},{7,6},{8,9},{9,8},{10,11... | collective-permute-start | bytes 98312 | tf_op jit(solution)/shard_map/ppermute | solution.py:384
  38.5 14.1 %all-to-all-start = ((f32[128,1,128]{2,1,0:T(1,128)}), f32[128,1,128]{2,1,0:T(1,128)S(1)}, u32[]{:S(2)}, u32[]{:S(2)}) async-start(f32[128,1,128]{2,1,0:T(1,128)} %bitcast.7), calls=%async_computation | async-start | bytes 131072 | tf_op jit(solution)/shard_map/all_to_all | solution.py:497
  43.4 5.2 %collective-permute-start.10 = (f32[4,16,128]{2,1,0:T(8,128)S(1)}, f32[4,16,128]{2,1,0:T(8,128)S(1)}, u32[]{:S(2)}, u32[]{:S(2)}) collective-permute-start(f32[4,16,128]{2,1,0:T(8,128)S(1)} %get-tuple-element.48), channel_id=1, source_target_pairs={{0,32},{32,64},{64,96},{96,0},{1,33},{33,65},{65,97},{97,1},{2,34}... | collective-permute-start | bytes 98312 | tf_op jit(solution)/shard_map/ppermute | solution.py:384
  44.5 6.7 %collective-permute-start.11 = (f32[4,16,128]{2,1,0:T(8,128)S(1)}, f32[4,16,128]{2,1,0:T(8,128)S(1)}, u32[]{:S(2)}, u32[]{:S(2)}) collective-permute-start(f32[4,16,128]{2,1,0:T(8,128)S(1)} %get-tuple-element.49), channel_id=1, source_target_pairs={{0,1},{1,2},{2,3},{3,4},{4,5},{5,6},{6,7},{7,8},{8,9},{9,10},{10,1... | collective-permute-start | bytes 98312 | tf_op jit(solution)/shard_map/ppermute | solution.py:384

commit v3 on v2

--- a/solution.py
+++ b/solution.py
@@ -13,18 +13,17 @@
 ROWS = 48
 SLOTS = 8
 ORDER = 384
-EARLY = 10
+EARLY = 5
 
 LOW = 0
-UPP = 64
-ROW_LOW = 128
-ROW_UPP = 192
-SEND_UP = 256
-SEND_DOWN = 272
-SEND_ROW = 288
-SPARE = 304
-ODD = 305
-TABLE = 312
+UPP = 68
+ROW_LOW = 132
+ROW_UPP = 196
+SEND_UP = 260
+SEND_DOWN = 278
+LIST = 9
+ODD = 296
+TABLE = 304
 
 VMEM = pl.BlockSpec(memory_space=pltpu.VMEM)
 SMEM = pl.BlockSpec(memory_space=pltpu.SMEM)
@@ -50,13 +49,18 @@
     ]
 
 
-def table_kernel(ids, faces, source, matrix, table, pairs, down_x, down_y, early, owner, user, sems):
+def table_kernel(outer, inner, faces, source, matrix, table, pairs, down_x, down_y, early, owner, user, sems):
     copies = matrix_copies(matrix, early, 0, EARLY, sems)
     for copy in copies:
         copy.start()
-    own = ids[0]
-    for axis in range(2):
-        table[ODD + axis] = ids[3 + axis]
+    at_x, at_y = lax.axis_index("gx"), lax.axis_index("gy")
+    own = (at_x * inner + at_y) * ROWS
+    shifts = (
+        (lax.rem(at_x + 1, outer) * inner + at_y) * ROWS - ROWS,
+        (at_x * inner + lax.rem(at_y + 1, inner)) * ROWS - 2 * ROWS,
+    )
+    table[ODD] = lax.rem(at_x, 2)
+    table[ODD + 1] = lax.rem(at_y, 2)
     for row in range(3 * ROWS):
         user[row] = -1
     for element in range(ELEMENTS):
@@ -69,7 +73,7 @@
             row = face - own
             if axis < 2:
                 here = jnp.logical_and(row >= 0, row < ROWS)
-                row = jnp.where(here, row, face - ids[1 + axis])
+                row = jnp.where(here, row, face - shifts[axis])
             user[row] = element
             table[ROW_UPP + at] = row
     for group in range(ROWS // 8):
@@ -77,34 +81,32 @@
             pairs[pl.ds(group * 64 + pair, 8, stride=8), :] = source[
                 group * 8 : group * 8 + 8, pair * 128 : pair * 128 + 128
             ]
-    count = [jnp.int32(0), jnp.int32(0)]
+    ends = [jnp.int32(SEND_DOWN), jnp.int32(SEND_DOWN + LIST)]
     for row in range(ROWS):
         ref = owner[row]
         axis = ref & 3
-        element = ref >> 2
         other = user[row]
-        here = other >= 0
-        slot = jnp.where(axis == 0, count[0], count[1])
-        table[LOW + ref] = jnp.where(here, other, ELEMENTS + slot)
-        table[jnp.where(here, UPP + other * 4 + axis, SPARE)] = element
-        table[jnp.where(here, SPARE, SEND_DOWN + axis * SLOTS + slot)] = element
-        table[jnp.where(here, SPARE, SEND_ROW + axis * SLOTS + slot)] = row
-        step = jnp.where(here, 0, 1)
-        count[0] = count[0] + jnp.where(axis == 0, step, 0)
-        count[1] = count[1] + jnp.where(axis == 1, step, 0)
+        table[LOW + ref] = other
+        table[UPP + other * 4 + axis] = ref >> 2
+        table[jnp.where(axis == 0, ends[0], ends[1])] = ref
+        step = jnp.where(other < 0, 1, 0)
+        in_x = jnp.where(axis == 0, step, 0)
+        ends = [ends[0] + in_x, ends[1] + (step - in_x)]
     for axis in range(2):
-        slot = jnp.int32(0)
+        for slot in range(SLOTS):
+            table[LOW + table[SEND_DOWN + axis * LIST + slot]] = ELEMENTS + slot
+        end = jnp.int32(SEND_UP + axis * LIST)
         for row in range(ROWS):
             element = user[ROWS * (1 + axis) + row]
-            here = element >= 0
-            at = element * 4 + axis
-            table[jnp.where(here, UPP + at, SPARE)] = ELEMENTS + slot
-            table[jnp.where(here, ROW_UPP + at, SPARE)] = ROWS + axis * SLOTS + slot
-            table[jnp.where(here, SEND_UP + axis * SLOTS + slot, SPARE)] = element
-            slot = slot + jnp.where(here, 1, 0)
+            table[end] = element
+            end = end + jnp.where(element < 0, 0, 1)
+        for slot in range(SLOTS):
+            at = table[SEND_UP + axis * LIST + slot] * 4 + axis
+            table[UPP + at] = ELEMENTS + slot
+            table[ROW_UPP + at] = ROWS + axis * SLOTS + slot
     for axis, out in enumerate((down_x, down_y)):
         for slot in range(SLOTS):
-            row = table[SEND_ROW + axis * SLOTS + slot]
+            row = table[ROW_LOW + table[SEND_DOWN + axis * LIST + slot]]
             out[slot] = pairs[pl.ds(pl.multiple_of(row * 8, 8), 8), :]
     for copy in copies:
         copy.wait()
@@ -140,8 +142,7 @@
             tiles.append(tile)
             if vector is not None:
                 vector[element, axis] = tile
-            if step < 2:
-                norm = norm + tile * tile
+            norm = norm + tile * tile
             first = tile.astype(jnp.bfloat16)
             rest = tile - first.astype(jnp.float32)
             second = rest.astype(jnp.bfloat16)
@@ -155,26 +156,28 @@
         for axis in range(3):
             part = total[:, axis * 128 : axis * 128 + 128]
             flux[element, axis] = part
-            if step < 2:
-                energy = energy + tiles[axis] * part
+            energy = energy + tiles[axis] * part
     for axis in range(2):
         for slot in range(4):
-            at = SEND_UP + axis * SLOTS + slot
+            at = SEND_UP + axis * LIST + slot
             up = jnp.where(
                 low_half, pltpu.roll(flux[table[at + 4], axis], 64, 1), flux[table[at], axis]
             )
             if step == 2:
                 sends[axis][slot] = up
                 continue
-            at = SEND_DOWN + axis * SLOTS + slot
+            at = SEND_DOWN + axis * LIST + slot
             down = jnp.where(
-                low_half, flux[table[at], axis], pltpu.roll(flux[table[at + 4], axis], 64, 1)
+                low_half, flux[table[at] >> 2, axis], pltpu.roll(flux[table[at + 4] >> 2, axis], 64, 1)
             )
             odd = table[ODD + axis] == 1
             sends[2 * axis][slot] = jnp.where(odd, down, up)
             sends[2 * axis + 1][slot] = jnp.where(odd, up, down)
+    now = with_moments(step, norm, energy, moments)
     if step < 2:
-        sums[...] = with_moments(step, norm, energy, moments)
+        sums[...] = now
+    else:
+        sums[...] = jnp.broadcast_to(jnp.sum(now, axis=0, keepdims=True), sums.shape)
 
 
 def with_moments(step, norm, energy, moments):
@@ -188,18 +191,6 @@
     return jnp.where(place == 0, half_norm, jnp.where(place == SOURCES, whole_energy, before))
 
 
-def share_kernel(vector, flux, moments, shares):
-    norm = jnp.zeros((SOURCES, 128), jnp.float32)
-    energy = jnp.zeros((SOURCES, 128), jnp.float32)
-    for element in range(ELEMENTS):
-        for axis in range(3):
-            tile = vector[element, axis]
-            norm = norm + tile * tile
-            energy = energy + tile * flux[element, axis]
-    now = with_moments(2, norm, energy, moments)
-    shares[...] = jnp.broadcast_to(jnp.sum(now, axis=0, keepdims=True), shares.shape)
-
-
 def tile_of(below, above):
     low_half = in_low_half((8, 128))
     even = jnp.where(low_half, below, pltpu.roll(above, 64, 1))
@@ -207,7 +198,7 @@
     return jnp.concatenate([even, odd], axis=0)
 
 
-def first_kernel(table, pairs, ghost_x, ghost_y, high, low,
+def first_kernel(table, pairs, ghost_y, ghost_x, high, low,
                  flux, xa, xb, ya, yb, sums, rows, left):
     for row in range(ROWS):
         rows[row] = pairs[row * 8 : row * 8 + 8, :]
@@ -234,12 +225,8 @@
             every[ELEMENTS + slot + 4, axis] = pltpu.roll(jnp.where(ahead_low, two, one), 64, 1)
 
 
-def later_kernel(step, table, previous, yb, xa, xb, ya, *rest):
-    if step == 1:
-        moments, high, low, vector, flux, *sends, sums, every, left = rest
-    else:
-        high, low, vector, flux, *sends, every, left = rest
-        moments = sums = None
+def later_kernel(step, table, previous, yb, xa, xb, ya, moments, high, low, vector, flux, *rest):
+    *sends, sums, every, left = rest
     low_half = in_low_half((SOURCES, 128))
     gather_flux(table, previous, (xa, xb, ya, yb), every)
 
@@ -405,16 +392,6 @@
 
 def local(heat_source, stiffness, element_faces):
     outer, inner = lax.axis_size("gx"), lax.axis_size("gy")
-    at_x, at_y = lax.axis_index("gx"), lax.axis_index("gy")
-    ids = jnp.stack(
-        [
-            (at_x * inner + at_y) * ROWS,
-            ((at_x + 1) % outer * inner + at_y) * ROWS - ROWS,
-            (at_x * inner + (at_y + 1) % inner) * ROWS - 2 * ROWS,
-            at_x % 2,
-            at_y % 2,
-        ]
-    ).astype(jnp.int32)
     pack = vmem((4, SOURCES, 128))
     face = vmem((SLOTS, 8, 128))
     state = vmem((ELEMENTS, 3, SOURCES, 128))
@@ -425,7 +402,7 @@
     pairs_shape = (ROWS * 8, 128)
 
     table, pairs, down_x, down_y, early = pl.pallas_call(
-        table_kernel,
+        functools.partial(table_kernel, outer, inner),
         out_shape=(
             pltpu.SMEM((TABLE,), jnp.int32),
             vmem(pairs_shape),
@@ -433,7 +410,7 @@
             face,
             vmem((EARLY, ORDER, ORDER)),
         ),
-        in_specs=[SMEM, SMEM, VMEM, HBM],
+        in_specs=[SMEM, VMEM, HBM],
         out_specs=(SMEM, VMEM, VMEM, VMEM, VMEM),
         scratch_shapes=[
             pltpu.SMEM((ROWS,), jnp.int32),
@@ -442,8 +419,9 @@
         ],
         compiler_params=params(52),
         name="table",
-    )(ids, element_faces.T, heat_source, stiffness)
-    ghost_x, ghost_y = back(down_x, "gx"), back(down_y, "gy")
+    )(element_faces.T, heat_source, stiffness)
+    ghost_y = back(down_y, "gy")
+    ghost_x = back(down_x, "gx")
     high, low = pl.pallas_call(
         split_kernel,
         out_shape=(matrix, matrix),
@@ -465,7 +443,7 @@
         scratch_shapes=[pltpu.VMEM((64, 8, 128), jnp.float32), left],
         compiler_params=params(),
         name="first",
-    )(table, pairs, ghost_x, ghost_y, high, low)
+    )(table, pairs, ghost_y, ghost_x, high, low)
     k1, flux, *sends, moments = pl.pallas_call(
         functools.partial(later_kernel, 1),
         out_shape=(state, state, pack, pack, pack, pack, moment),
@@ -475,24 +453,15 @@
         compiler_params=params(),
         name="second",
     )(table, flux, *exchanged(sends), moments, high, low)
-    k2, flux, up_x, up_y = pl.pallas_call(
+    k2, flux, up_x, up_y, shares = pl.pallas_call(
         functools.partial(later_kernel, 2),
-        out_shape=(state, state, pack, pack),
-        in_specs=[SMEM] + [VMEM] * 7,
-        out_specs=(VMEM,) * 4,
+        out_shape=(state, state, pack, pack, vmem((outer * inner, 128))),
+        in_specs=[SMEM] + [VMEM] * 8,
+        out_specs=(VMEM,) * 5,
         scratch_shapes=[every, left],
         compiler_params=params(),
         name="third",
-    )(table, flux, *exchanged(sends), high, low)
-    shares = pl.pallas_call(
-        share_kernel,
-        out_shape=vmem((outer * inner, 128)),
-        in_specs=[VMEM] * 3,
-        out_specs=VMEM,
-        compiler_params=params(),
-        cost_estimate=pl.CostEstimate(flops=0, bytes_accessed=18 << 20, transcendentals=0),
-        name="share",
-    )(k2, flux, moments)
+    )(table, flux, *exchanged(sends), moments, high, low)
     prev_x, prev_y = ahead(up_x, "gx"), ahead(up_y, "gy")
     shares = lax.all_to_all(shares, ("gx", "gy"), 0, 0, tiled=True)
     natural = jax.ShapeDtypeStruct((ROWS, SOURCES * BLOCK), jnp.float32)

time: 54.7 us -> 52.6 us (0.962)
  waiting for transfers between devices: 16.8 us -> 13.8 us
  starting transfers between devices: 22.3 us -> 24.1 us
  local copies, waits for them, and re-layouts: 0.61 us -> 0 us
    ppermute x12, waiting for transfers between devices: 15.4 us -> 12.4 us  [passed(): return lax.ppermute(value, axis, [(i, target(i)) for i in range(count)])]
    pallas_call x2 -> x1, Pallas kernels: 4.48 us -> 2.76 us  [local(): pl.pallas_call(functools.partial(table_kernel, outer, inner), out_shape=(...]
    ppermute x12, starting transfers between devices: 17.5 us -> 19.1 us  [passed(): return lax.ppermute(value, axis, [(i, target(i)) for i in range(count)])]
    pallas_call x1, Pallas kernels: 2.11 us -> 3.04 us  [local(): pl.pallas_call(split_kernel, out_shape=(matrix, matrix), in_specs=[VMEM,...]
    pallas_call x1, Pallas kernels: 1.85 us -> 2.49 us  [local(): pl.pallas_call(functools.partial(later_kernel, 2), out_shape=(state, stat...]
    another operation x1 -> x0, local copies, waits for them, and re-layouts: 0.61 us -> none  [local(): jnp.stack([(at_x * inner + at_y) * ROWS, ((at_x + 1) % outer * inner + at...]
  transfers between devices with their start and end apart: 13 -> 13, of which waited for: 7 -> 6; matrix products, arithmetic and copies ran while one was open for 0% -> 0% of each run, Pallas kernels for 4% -> 6%
where the time goes in v3:
time: 52.6 us; the launch traced here: 51.8 us
  starting transfers between devices  24.1 us (46%)
  waiting for transfers between devices  13.8 us (26%)
  Pallas kernels  13.2 us (25%)
  between operations  0.7 us (1%)
    ppermute x12, starting transfers between devices, passed(): return lax.ppermute(value, axis, [(i, target(i)) for i in range(count)])  19.1 us
    ppermute x12, waiting for transfers between devices, passed(): return lax.ppermute(value, axis, [(i, target(i)) for i in range(count)])  12.4 us
    all_to_all x1, starting transfers between devices, local(): shares = lax.all_to_all(shares, ('gx', 'gy'), 0, 0, tiled=True)  4.96 us
    pallas_call x1, Pallas kernels, local(): pl.pallas_call(split_kernel, out_shape=(matrix, matrix), in_specs=[VMEM,...  3.04 us
    pallas_call x1, Pallas kernels, local(): pl.pallas_call(functools.partial(table_kernel, outer, inner), out_shape=(...  2.76 us
    pallas_call x1, Pallas kernels, local(): pl.pallas_call(functools.partial(later_kernel, 2), out_shape=(state, stat...  2.49 us
    pallas_call x1, Pallas kernels, local(): pl.pallas_call(functools.partial(later_kernel, 1), out_shape=(state, stat...  1.89 us
    pallas_call x1, Pallas kernels, local(): pl.pallas_call(first_kernel, out_shape=(state, pack, pack, pack, pack, mo...  1.8 us
  transfers between devices with their start and end apart: 13, of which 6 were waited for; matrix products, arithmetic and copies ran while one was open for 0% of the time, Pallas kernels for 6%

profile of v3, /device:TPU:0, one launch (start us, length us, event | category | flops | bytes accessed | tf_op | source)
XLA Modules:
  0.0 51.8 jit_solution(12851508580734716611)
XLA Ops:
  0.6 2.8 %table.1 = (s32[304]{0:T(512)S(4)}, f32[384,128]{1,0:T(8,128)S(1)}, f32[8,8,128]{2,1,0:T(8,128)S(1)}, f32[8,8,128]{2,1,0:T(8,128)S(1)}, f32[5,384,384]{2,1,0:T(8,128)S(1)}) custom-call(s32[6,16]{1,0:T(8,128)} %bitcast.6, f32[48,1024]{1,0:T(8,128)} %source.1, f32[16,384,384]{2,1,0:T(8,128)} %matrix.3), custom_call_target="tpu_custom_call" | custom-call | tf_op jit(solution)/shard_map/table/pallas_call | solution.py:404
  3.4 4.8 %collective-permute-start = (f32[8,8,128]{2,1,0:T(8,128)S(1)}, f32[8,8,128]{2,1,0:T(8,128)S(1)}, u32[]{:S(2)}, u32[]{:S(2)}) collective-permute-start(f32[8,8,128]{2,1,0:T(8,128)S(1)} %get-tuple-element.29), channel_id=1, source_target_pairs={{0,31},{1,0},{2,1},{3,2},{4,3},{5,4},{6,5},{7,6},{8,7},{9,8},{10,9... | collective-permute-start | bytes 98312 | tf_op jit(solution)/shard_map/ppermute | solution.py:371
  8.2 4.0 %collective-permute-start.1 = (f32[8,8,128]{2,1,0:T(8,128)S(1)}, f32[8,8,128]{2,1,0:T(8,128)S(1)}, u32[]{:S(2)}, u32[]{:S(2)}) collective-permute-start(f32[8,8,128]{2,1,0:T(8,128)S(1)} %get-tuple-element.30), channel_id=1, source_target_pairs={{0,96},{32,0},{64,32},{96,64},{1,97},{33,1},{65,33},{97,65},{2,98}... | collective-permute-start | bytes 98312 | tf_op jit(solution)/shard_map/ppermute | solution.py:371
  12.2 3.0 %split.1 = (bf16[16,384,384]{2,1,0:T(8,128)(2,1)S(1)}, bf16[16,384,384]{2,1,0:T(8,128)(2,1)S(1)}) custom-call(f32[5,384,384]{2,1,0:T(8,128)S(1)} %get-tuple-element.31.early, f32[16,384,384]{2,1,0:T(8,128)} %matrix.3), custom_call_target="tpu_custom_call" | custom-call | flops 10000000 | bytes 18874368 | tf_op jit(solution)/shard_map/split/pallas_call | solution.py:425
  15.3 0.0 collective-permute-done.ghost_y
  15.3 0.0 collective-permute-done.1.ghost_x
  15.3 1.8 %first.1 = (f32[16,3,16,128]{3,2,1,0:T(8,128)S(1)}, f32[4,16,128]{2,1,0:T(8,128)S(1)}, f32[4,16,128]{2,1,0:T(8,128)S(1)}, f32[4,16,128]{2,1,0:T(8,128)S(1)}, f32...) custom-call(s32[304]{0:T(512)S(4)} %get-tuple-element.27.table, f32[384,128]{1,0:T(8,128)S(1)} %get-tuple-element.28.pairs, ...), custom_call_target="tpu_custom_call" | custom-call | tf_op jit(solution)/shard_map/first/pallas_call | solution.py:438
  17.1 0.5 collective-permute-start.2
  17.6 1.1 %collective-permute-start.3 = (f32[4,16,128]{2,1,0:T(8,128)S(1)}, f32[4,16,128]{2,1,0:T(8,128)S(1)}, u32[]{:S(2)}, u32[]{:S(2)}) collective-permute-start(f32[4,16,128]{2,1,0:T(8,128)S(1)} %get-tuple-element.36), channel_id=1, source_target_pairs={{0,32},{32,0},{64,96},{96,64},{1,33},{33,1},{65,97},{97,65},{2,34}... | collective-permute-start | bytes 98312 | tf_op jit(solution)/shard_map/ppermute | solution.py:371
  18.7 2.5 %collective-permute-start.4 = (f32[4,16,128]{2,1,0:T(8,128)S(1)}, f32[4,16,128]{2,1,0:T(8,128)S(1)}, u32[]{:S(2)}, u32[]{:S(2)}) collective-permute-start(f32[4,16,128]{2,1,0:T(8,128)S(1)} %get-tuple-element.37), channel_id=1, source_target_pairs={{0,96},{32,64},{64,32},{96,0},{1,97},{33,65},{65,33},{97,1},{2,98}... | collective-permute-start | bytes 98312 | tf_op jit(solution)/shard_map/ppermute | solution.py:371
  21.2 0.0 collective-permute-start.5
  21.2 2.7 %collective-permute-done.2.yb = f32[4,16,128]{2,1,0:T(8,128)S(1)} collective-permute-done((f32[4,16,128]{2,1,0:T(8,128)S(1)}, f32[4,16,128]{2,1,0:T(8,128)S(1)}, u32[]{:S(2)}, u32[]{:S(2)}) %collective-permute-start.2) | collective-permute-done | bytes 32800 | tf_op jit(solution)/shard_map/ppermute | solution.py:371
  23.9 0.0 collective-permute-done.3.xa
  23.9 0.0 collective-permute-done.4.xb
  23.9 0.0 collective-permute-done.5.ya
  23.9 1.9 %second.1 = (f32[16,3,16,128]{3,2,1,0:T(8,128)S(1)}, f32[16,3,16,128]{3,2,1,0:T(8,128)S(1)}, f32[4,16,128]{2,1,0:T(8,128)S(1)}, f32[4,16,128]{2,1,0:T(8,128)S(1)...) custom-call(s32[304]{0:T(512)S(4)} %get-tuple-element.27.table, ...), custom_call_target="tpu_custom_call" | custom-call | tf_op jit(solution)/shard_map/second/pallas_call | solution.py:447
  25.8 2.4 %collective-permute-start.6 = (f32[4,16,128]{2,1,0:T(8,128)S(1)}, f32[4,16,128]{2,1,0:T(8,128)S(1)}, u32[]{:S(2)}, u32[]{:S(2)}) collective-permute-start(f32[4,16,128]{2,1,0:T(8,128)S(1)} %get-tuple-element.41), channel_id=1, source_target_pairs={{0,31},{1,2},{2,1},{3,4},{4,3},{5,6},{6,5},{7,8},{8,7},{9,10},{10,... | collective-permute-start | bytes 98312 | tf_op jit(solution)/shard_map/ppermute | solution.py:371
  28.2 0.5 %collective-permute-start.7 = (f32[4,16,128]{2,1,0:T(8,128)S(1)}, f32[4,16,128]{2,1,0:T(8,128)S(1)}, u32[]{:S(2)}, u32[]{:S(2)}) collective-permute-start(f32[4,16,128]{2,1,0:T(8,128)S(1)} %get-tuple-element.42), channel_id=1, source_target_pairs={{0,32},{32,0},{64,96},{96,64},{1,33},{33,1},{65,97},{97,65},{2,34}... | collective-permute-start | bytes 98312 | tf_op jit(solution)/shard_map/ppermute | solution.py:371
  28.7 2.1 %collective-permute-start.8 = (f32[4,16,128]{2,1,0:T(8,128)S(1)}, f32[4,16,128]{2,1,0:T(8,128)S(1)}, u32[]{:S(2)}, u32[]{:S(2)}) collective-permute-start(f32[4,16,128]{2,1,0:T(8,128)S(1)} %get-tuple-element.43), channel_id=1, source_target_pairs={{0,96},{32,64},{64,32},{96,0},{1,97},{33,65},{65,33},{97,1},{2,98}... | collective-permute-start | bytes 98312 | tf_op jit(solution)/shard_map/ppermute | solution.py:371
  30.8 0.0 collective-permute-start.9
  30.8 1.7 %collective-permute-done.6.yb = f32[4,16,128]{2,1,0:T(8,128)S(1)} collective-permute-done((f32[4,16,128]{2,1,0:T(8,128)S(1)}, f32[4,16,128]{2,1,0:T(8,128)S(1)}, u32[]{:S(2)}, u32[]{:S(2)}) %collective-permute-start.6) | collective-permute-done | bytes 32800 | tf_op jit(solution)/shard_map/ppermute | solution.py:371
  32.5 0.0 collective-permute-done.7.xa
  32.5 1.4 %collective-permute-done.8.xb = f32[4,16,128]{2,1,0:T(8,128)S(1)} collective-permute-done((f32[4,16,128]{2,1,0:T(8,128)S(1)}, f32[4,16,128]{2,1,0:T(8,128)S(1)}, u32[]{:S(2)}, u32[]{:S(2)}) %collective-permute-start.8) | collective-permute-done | bytes 32800 | tf_op jit(solution)/shard_map/ppermute | solution.py:371
  33.9 0.0 collective-permute-done.9.ya
  33.9 2.5 %third.1 = (f32[16,3,16,128]{3,2,1,0:T(8,128)S(1)}, f32[16,3,16,128]{3,2,1,0:T(8,128)S(1)}, f32[4,16,128]{2,1,0:T(8,128)S(1)}, f32[4,16,128]{2,1,0:T(8,128)S(1)}, f32[128,128]{1,0:T(8,128)}) custom-call(s32[304]{0:T(512)S(4)} %get-tuple-element.27.table, f32[16,3,16,128]{3,2,1,0:T(8,128)S(1)} %get-tuple-element.40.previous, ...), custom_call_target="tpu_custom_call" | custom-call | tf_op jit(solution)/shard_map/third/pallas_call | solution.py:456
  36.4 5.0 %all-to-all-start = ((f32[128,1,128]{2,1,0:T(1,128)}), f32[128,1,128]{2,1,0:T(1,128)S(1)}, u32[]{:S(2)}, u32[]{:S(2)}) async-start(f32[128,1,128]{2,1,0:T(1,128)} %bitcast.2), calls=%async_computation | async-start | bytes 131072 | tf_op jit(solution)/shard_map/all_to_all | solution.py:466
  41.3 1.1 %collective-permute-start.10 = (f32[4,16,128]{2,1,0:T(8,128)S(1)}, f32[4,16,128]{2,1,0:T(8,128)S(1)}, u32[]{:S(2)}, u32[]{:S(2)}) collective-permute-start(f32[4,16,128]{2,1,0:T(8,128)S(1)} %get-tuple-element.50), channel_id=1, source_target_pairs={{0,32},{32,64},{64,96},{96,0},{1,33},{33,65},{65,97},{97,1},{2,34}... | collective-permute-start | bytes 98312 | tf_op jit(solution)/shard_map/ppermute | solution.py:371
  42.5 0.0 collective-permute-start.11
  42.5 4.1 %collective-permute-done.10.prev_x = f32[4,16,128]{2,1,0:T(8,128)S(1)} collective-permute-done((f32[4,16,128]{2,1,0:T(8,128)S(1)}, f32[4,16,128]{2,1,0:T(8,128)S(1)}, u32[]{:S(2)}, u32[]{:S(2)}) %collective-permute-start.10) | collective-permute-done | bytes 32800 | tf_op jit(solution)/shard_map/ppermute | solution.py:371
  46.6 2.6 %collective-permute-done.11.prev_y = f32[4,16,128]{2,1,0:T(8,128)S(1)} collective-permute-done((f32[4,16,128]{2,1,0:T(8,128)S(1)}, f32[4,16,128]{2,1,0:T(8,128)S(1)}, u32[]{:S(2)}, u32[]{:S(2)}) %collective-permute-start.11) | collective-permute-done | bytes 32800 | tf_op jit(solution)/shard_map/ppermute | solution.py:371
  49.1 1.4 %all-to-all-done = f32[128,1,128]{2,1,0:T(1,128)S(1)} async-done(((f32[128,1,128]{2,1,0:T(1,128)}), f32[128,1,128]{2,1,0:T(1,128)S(1)}, u32[]{:S(2)}, u32[]{:S(2)}) %all-to-all-start) | async-done | bytes 65568 | tf_op jit(solution)/shard_map/all_to_all | solution.py:466
  50.6 1.2 %final.1 = (f32[48,1024]{1,0:T(8,128)}, f32[48,1024]{1,0:T(8,128)}) custom-call(s32[304]{0:T(512)S(4)} %get-tuple-element.27.table, f32[128,128]{1,0:T(8,128)S(1)} %bitcast.5, f32[384,128]{1,0:T(8,128)S(1)} %get-tuple-element.28.pairs, f32[16,3,16,128]{3,2,1,0:T(8,128)S(1)} %get-tuple-element.47.firsts, f32[16,3,16,128]{3,2,1,0:T(8,128)S(1)} %get-tuple-element.48.seconds, ...), custom_call_target="tpu_custom_call" | custom-call | tf_op jit(solution)/shard_map/final/pallas_call | solution.py:468
Async XLA Ops:
  3.4 11.9 %collective-permute-start = (f32[8,8,128]{2,1,0:T(8,128)S(1)}, f32[8,8,128]{2,1,0:T(8,128)S(1)}, u32[]{:S(2)}, u32[]{:S(2)}) collective-permute-start(f32[8,8,128]{2,1,0:T(8,128)S(1)} %get-tuple-element.29), channel_id=1, source_target_pairs={{0,31},{1,0},{2,1},{3,2},{4,3},{5,4},{6,5},{7,6},{8,7},{9,8},{10,9... | collective-permute-start | bytes 98312 | tf_op jit(solution)/shard_map/ppermute | solution.py:371
  8.2 7.1 %collective-permute-start.1 = (f32[8,8,128]{2,1,0:T(8,128)S(1)}, f32[8,8,128]{2,1,0:T(8,128)S(1)}, u32[]{:S(2)}, u32[]{:S(2)}) collective-permute-start(f32[8,8,128]{2,1,0:T(8,128)S(1)} %get-tuple-element.30), channel_id=1, source_target_pairs={{0,96},{32,0},{64,32},{96,64},{1,97},{33,1},{65,33},{97,65},{2,98}... | collective-permute-start | bytes 98312 | tf_op jit(solution)/shard_map/ppermute | solution.py:371
  17.1 6.7 %collective-permute-start.2 = (f32[4,16,128]{2,1,0:T(8,128)S(1)}, f32[4,16,128]{2,1,0:T(8,128)S(1)}, u32[]{:S(2)}, u32[]{:S(2)}) collective-permute-start(f32[4,16,128]{2,1,0:T(8,128)S(1)} %get-tuple-element.35), channel_id=1, source_target_pairs={{0,31},{1,2},{2,1},{3,4},{4,3},{5,6},{6,5},{7,8},{8,7},{9,10},{10,... | collective-permute-start | bytes 98312 | tf_op jit(solution)/shard_map/ppermute | solution.py:371
  17.6 6.3 %collective-permute-start.3 = (f32[4,16,128]{2,1,0:T(8,128)S(1)}, f32[4,16,128]{2,1,0:T(8,128)S(1)}, u32[]{:S(2)}, u32[]{:S(2)}) collective-permute-start(f32[4,16,128]{2,1,0:T(8,128)S(1)} %get-tuple-element.36), channel_id=1, source_target_pairs={{0,32},{32,0},{64,96},{96,64},{1,33},{33,1},{65,97},{97,65},{2,34}... | collective-permute-start | bytes 98312 | tf_op jit(solution)/shard_map/ppermute | solution.py:371
  18.7 5.2 %collective-permute-start.4 = (f32[4,16,128]{2,1,0:T(8,128)S(1)}, f32[4,16,128]{2,1,0:T(8,128)S(1)}, u32[]{:S(2)}, u32[]{:S(2)}) collective-permute-start(f32[4,16,128]{2,1,0:T(8,128)S(1)} %get-tuple-element.37), channel_id=1, source_target_pairs={{0,96},{32,64},{64,32},{96,0},{1,97},{33,65},{65,33},{97,1},{2,98}... | collective-permute-start | bytes 98312 | tf_op jit(solution)/shard_map/ppermute | solution.py:371
  21.2 2.7 %collective-permute-start.5 = (f32[4,16,128]{2,1,0:T(8,128)S(1)}, f32[4,16,128]{2,1,0:T(8,128)S(1)}, u32[]{:S(2)}, u32[]{:S(2)}) collective-permute-start(f32[4,16,128]{2,1,0:T(8,128)S(1)} %get-tuple-element.38), channel_id=1, source_target_pairs={{0,1},{1,0},{2,3},{3,2},{4,5},{5,4},{6,7},{7,6},{8,9},{9,8},{10,11... | collective-permute-start | bytes 98312 | tf_op jit(solution)/shard_map/ppermute | solution.py:371
  25.8 6.7 %collective-permute-start.6 = (f32[4,16,128]{2,1,0:T(8,128)S(1)}, f32[4,16,128]{2,1,0:T(8,128)S(1)}, u32[]{:S(2)}, u32[]{:S(2)}) collective-permute-start(f32[4,16,128]{2,1,0:T(8,128)S(1)} %get-tuple-element.41), channel_id=1, source_target_pairs={{0,31},{1,2},{2,1},{3,4},{4,3},{5,6},{6,5},{7,8},{8,7},{9,10},{10,... | collective-permute-start | bytes 98312 | tf_op jit(solution)/shard_map/ppermute | solution.py:371
  28.2 4.3 %collective-permute-start.7 = (f32[4,16,128]{2,1,0:T(8,128)S(1)}, f32[4,16,128]{2,1,0:T(8,128)S(1)}, u32[]{:S(2)}, u32[]{:S(2)}) collective-permute-start(f32[4,16,128]{2,1,0:T(8,128)S(1)} %get-tuple-element.42), channel_id=1, source_target_pairs={{0,32},{32,0},{64,96},{96,64},{1,33},{33,1},{65,97},{97,65},{2,34}... | collective-permute-start | bytes 98312 | tf_op jit(solution)/shard_map/ppermute | solution.py:371
  28.7 5.1 %collective-permute-start.8 = (f32[4,16,128]{2,1,0:T(8,128)S(1)}, f32[4,16,128]{2,1,0:T(8,128)S(1)}, u32[]{:S(2)}, u32[]{:S(2)}) collective-permute-start(f32[4,16,128]{2,1,0:T(8,128)S(1)} %get-tuple-element.43), channel_id=1, source_target_pairs={{0,96},{32,64},{64,32},{96,0},{1,97},{33,65},{65,33},{97,1},{2,98}... | collective-permute-start | bytes 98312 | tf_op jit(solution)/shard_map/ppermute | solution.py:371
  30.8 3.1 %collective-permute-start.9 = (f32[4,16,128]{2,1,0:T(8,128)S(1)}, f32[4,16,128]{2,1,0:T(8,128)S(1)}, u32[]{:S(2)}, u32[]{:S(2)}) collective-permute-start(f32[4,16,128]{2,1,0:T(8,128)S(1)} %get-tuple-element.44), channel_id=1, source_target_pairs={{0,1},{1,0},{2,3},{3,2},{4,5},{5,4},{6,7},{7,6},{8,9},{9,8},{10,11... | collective-permute-start | bytes 98312 | tf_op jit(solution)/shard_map/ppermute | solution.py:371
  36.4 14.2 %all-to-all-start = ((f32[128,1,128]{2,1,0:T(1,128)}), f32[128,1,128]{2,1,0:T(1,128)S(1)}, u32[]{:S(2)}, u32[]{:S(2)}) async-start(f32[128,1,128]{2,1,0:T(1,128)} %bitcast.2), calls=%async_computation | async-start | bytes 131072 | tf_op jit(solution)/shard_map/all_to_all | solution.py:466
  41.3 5.2 %collective-permute-start.10 = (f32[4,16,128]{2,1,0:T(8,128)S(1)}, f32[4,16,128]{2,1,0:T(8,128)S(1)}, u32[]{:S(2)}, u32[]{:S(2)}) collective-permute-start(f32[4,16,128]{2,1,0:T(8,128)S(1)} %get-tuple-element.50), channel_id=1, source_target_pairs={{0,32},{32,64},{64,96},{96,0},{1,33},{33,65},{65,97},{97,1},{2,34}... | collective-permute-start | bytes 98312 | tf_op jit(solution)/shard_map/ppermute | solution.py:371
  42.5 6.7 %collective-permute-start.11 = (f32[4,16,128]{2,1,0:T(8,128)S(1)}, f32[4,16,128]{2,1,0:T(8,128)S(1)}, u32[]{:S(2)}, u32[]{:S(2)}) collective-permute-start(f32[4,16,128]{2,1,0:T(8,128)S(1)} %get-tuple-element.51), channel_id=1, source_target_pairs={{0,1},{1,2},{2,3},{3,4},{4,5},{5,6},{6,7},{7,8},{8,9},{9,10},{10,1... | collective-permute-start | bytes 98312 | tf_op jit(solution)/shard_map/ppermute | solution.py:371

commit v4 on v3

--- a/solution.py
+++ b/solution.py
@@ -49,7 +49,12 @@
     ]
 
 
-def table_kernel(outer, inner, faces, source, matrix, table, pairs, down_x, down_y, early, owner, user, sems):
+def table_kernel(outer, inner, faces_hbm, source_hbm, matrix, table, pairs, down_x, down_y, early,
+                 owner, user, faces, source, sems, faces_sem, source_sem):
+    faces_copy = pltpu.make_async_copy(faces_hbm, faces, faces_sem)
+    source_copy = pltpu.make_async_copy(source_hbm, source, source_sem)
+    faces_copy.start()
+    source_copy.start()
     copies = matrix_copies(matrix, early, 0, EARLY, sems)
     for copy in copies:
         copy.start()
@@ -63,6 +68,7 @@
     table[ODD + 1] = lax.rem(at_y, 2)
     for row in range(3 * ROWS):
         user[row] = -1
+    faces_copy.wait()
     for element in range(ELEMENTS):
         for axis in range(3):
             at = element * 4 + axis
@@ -76,11 +82,6 @@
                 row = jnp.where(here, row, face - shifts[axis])
             user[row] = element
             table[ROW_UPP + at] = row
-    for group in range(ROWS // 8):
-        for pair in range(8):
-            pairs[pl.ds(group * 64 + pair, 8, stride=8), :] = source[
-                group * 8 : group * 8 + 8, pair * 128 : pair * 128 + 128
-            ]
     ends = [jnp.int32(SEND_DOWN), jnp.int32(SEND_DOWN + LIST)]
     for row in range(ROWS):
         ref = owner[row]
@@ -104,6 +105,12 @@
             at = table[SEND_UP + axis * LIST + slot] * 4 + axis
             table[UPP + at] = ELEMENTS + slot
             table[ROW_UPP + at] = ROWS + axis * SLOTS + slot
+    source_copy.wait()
+    for group in range(ROWS // 8):
+        for pair in range(8):
+            pairs[pl.ds(group * 64 + pair, 8, stride=8), :] = source[
+                group * 8 : group * 8 + 8, pair * 128 : pair * 128 + 128
+            ]
     for axis, out in enumerate((down_x, down_y)):
         for slot in range(SLOTS):
             row = table[ROW_LOW + table[SEND_DOWN + axis * LIST + slot]]
@@ -112,15 +119,15 @@
         copy.wait()
 
 
-def split_kernel(early, matrix, high, low, late, sems):
+def split_kernel(early, matrix, parts, late, sems):
     copies = matrix_copies(matrix, late, EARLY, ELEMENTS, sems)
     for copy in copies:
         copy.start()
 
     def split(full, element):
         top = full.astype(jnp.bfloat16)
-        high[element] = top
-        low[element] = (full - top.astype(jnp.float32)).astype(jnp.bfloat16)
+        parts[element, :ORDER] = top
+        parts[element, ORDER:] = (full - top.astype(jnp.float32)).astype(jnp.bfloat16)
 
     @pl.loop(0, EARLY)
     def _(element):
@@ -131,7 +138,7 @@
         split(late[i], EARLY + i)
 
 
-def multiply(step, table, get, high, low, vector, flux, sends, moments, sums, left):
+def multiply(step, table, get, parts, vector, flux, sends, moments, sums, left):
     low_half = in_low_half((SOURCES, 128))
     norm = jnp.zeros((SOURCES, 128), jnp.float32)
     energy = jnp.zeros((SOURCES, 128), jnp.float32)
@@ -148,13 +155,15 @@
             second = rest.astype(jnp.bfloat16)
             third = (rest - second.astype(jnp.float32)).astype(jnp.bfloat16)
             for part, value in enumerate((first, second, third)):
-                left[element, part * 16 : part * 16 + 16, axis * 128 : axis * 128 + 128] = value
-        rows = left[element]
-        by_high = jnp.dot(rows, high[element], preferred_element_type=jnp.float32)
-        by_low = jnp.dot(rows[:32], low[element], preferred_element_type=jnp.float32)
-        total = by_high[0:16] + (by_high[16:32] + by_low[0:16] + (by_high[32:48] + by_low[16:32]))
+                for begin in (axis * 128, ORDER + axis * 128):
+                    left[element, part * 16 : part * 16 + 16, begin : begin + 128] = value
         for axis in range(3):
-            part = total[:, axis * 128 : axis * 128 + 128]
+            product = jnp.dot(
+                left[element],
+                parts[element, :, axis * 128 : axis * 128 + 128],
+                preferred_element_type=jnp.float32,
+            )
+            part = product[0:16] + (product[16:32] + product[32:48])
             flux[element, axis] = part
             energy = energy + tiles[axis] * part
     for axis in range(2):
@@ -198,7 +207,7 @@
     return jnp.concatenate([even, odd], axis=0)
 
 
-def first_kernel(table, pairs, ghost_y, ghost_x, high, low,
+def first_kernel(table, pairs, ghost_y, ghost_x, parts,
                  flux, xa, xb, ya, yb, sums, rows, left):
     for row in range(ROWS):
         rows[row] = pairs[row * 8 : row * 8 + 8, :]
@@ -210,7 +219,7 @@
         at = element * 4 + axis
         return tile_of(rows[table[ROW_LOW + at]], rows[table[ROW_UPP + at]])
 
-    multiply(0, table, get, high, low, None, flux, (xa, xb, ya, yb), None, sums, left)
+    multiply(0, table, get, parts, None, flux, (xa, xb, ya, yb), None, sums, left)
 
 
 def gather_flux(table, previous, received, every):
@@ -225,7 +234,7 @@
             every[ELEMENTS + slot + 4, axis] = pltpu.roll(jnp.where(ahead_low, two, one), 64, 1)
 
 
-def later_kernel(step, table, previous, yb, xa, xb, ya, moments, high, low, vector, flux, *rest):
+def later_kernel(step, table, previous, yb, xa, xb, ya, moments, parts, vector, flux, *rest):
     *sends, sums, every, left = rest
     low_half = in_low_half((SOURCES, 128))
     gather_flux(table, previous, (xa, xb, ya, yb), every)
@@ -235,7 +244,7 @@
         across = jnp.where(low_half, every[table[UPP + at], axis], every[table[LOW + at], axis])
         return every[element, axis] + pltpu.roll(across, 64, 1)
 
-    multiply(step, table, get, high, low, vector, flux, sends, moments, sums, left)
+    multiply(step, table, get, parts, vector, flux, sends, moments, sums, left)
 
 
 def two_sum(a, b):
@@ -395,9 +404,9 @@
     pack = vmem((4, SOURCES, 128))
     face = vmem((SLOTS, 8, 128))
     state = vmem((ELEMENTS, 3, SOURCES, 128))
-    matrix = vmem((ELEMENTS, ORDER, ORDER), jnp.bfloat16)
+    matrix = vmem((ELEMENTS, 2 * ORDER, ORDER), jnp.bfloat16)
     moment = vmem((SOURCES, 128))
-    left = pltpu.VMEM((ELEMENTS, 48, ORDER), jnp.bfloat16)
+    left = pltpu.VMEM((ELEMENTS, 48, 2 * ORDER), jnp.bfloat16)
     every = pltpu.VMEM((ELEMENTS + SLOTS, 3, SOURCES, 128), jnp.float32)
     pairs_shape = (ROWS * 8, 128)
 
@@ -410,23 +419,27 @@
             face,
             vmem((EARLY, ORDER, ORDER)),
         ),
-        in_specs=[SMEM, VMEM, HBM],
+        in_specs=[HBM, HBM, HBM],
         out_specs=(SMEM, VMEM, VMEM, VMEM, VMEM),
         scratch_shapes=[
             pltpu.SMEM((ROWS,), jnp.int32),
             pltpu.SMEM((3 * ROWS,), jnp.int32),
+            pltpu.SMEM((6, ELEMENTS), jnp.int32),
+            pltpu.VMEM((ROWS, SOURCES * BLOCK), jnp.float32),
             pltpu.SemaphoreType.DMA((EARLY,)),
+            pltpu.SemaphoreType.DMA,
+            pltpu.SemaphoreType.DMA,
         ],
         compiler_params=params(52),
         name="table",
     )(element_faces.T, heat_source, stiffness)
     ghost_y = back(down_y, "gy")
     ghost_x = back(down_x, "gx")
-    high, low = pl.pallas_call(
+    parts = pl.pallas_call(
         split_kernel,
-        out_shape=(matrix, matrix),
+        out_shape=matrix,
         in_specs=[VMEM, HBM],
-        out_specs=(VMEM, VMEM),
+        out_specs=VMEM,
         scratch_shapes=[
             pltpu.VMEM((ELEMENTS - EARLY, ORDER, ORDER), jnp.float32),
             pltpu.SemaphoreType.DMA((ELEMENTS - EARLY,)),
@@ -438,30 +451,30 @@
     flux, *sends, moments = pl.pallas_call(
         first_kernel,
         out_shape=(state, pack, pack, pack, pack, moment),
-        in_specs=[SMEM] + [VMEM] * 5,
+        in_specs=[SMEM] + [VMEM] * 4,
         out_specs=(VMEM,) * 6,
         scratch_shapes=[pltpu.VMEM((64, 8, 128), jnp.float32), left],
         compiler_params=params(),
         name="first",
-    )(table, pairs, ghost_y, ghost_x, high, low)
+    )(table, pairs, ghost_y, ghost_x, parts)
     k1, flux, *sends, moments = pl.pallas_call(
         functools.partial(later_kernel, 1),
         out_shape=(state, state, pack, pack, pack, pack, moment),
-        in_specs=[SMEM] + [VMEM] * 8,
+        in_specs=[SMEM] + [VMEM] * 7,
         out_specs=(VMEM,) * 7,
         scratch_shapes=[every, left],
         compiler_params=params(),
         name="second",
-    )(table, flux, *exchanged(sends), moments, high, low)
+    )(table, flux, *exchanged(sends), moments, parts)
     k2, flux, up_x, up_y, shares = pl.pallas_call(
         functools.partial(later_kernel, 2),
         out_shape=(state, state, pack, pack, vmem((outer * inner, 128))),
-        in_specs=[SMEM] + [VMEM] * 8,
+        in_specs=[SMEM] + [VMEM] * 7,
         out_specs=(VMEM,) * 5,
         scratch_shapes=[every, left],
         compiler_params=params(),
         name="third",
-    )(table, flux, *exchanged(sends), moments, high, low)
+    )(table, flux, *exchanged(sends), moments, parts)
     prev_x, prev_y = ahead(up_x, "gx"), ahead(up_y, "gy")
     shares = lax.all_to_all(shares, ("gx", "gy"), 0, 0, tiled=True)
     natural = jax.ShapeDtypeStruct((ROWS, SOURCES * BLOCK), jnp.float32)

time: 52.6 us -> 51.3 us (0.975)
  Pallas kernels: 13.2 us -> 11.9 us
    pallas_call x1, Pallas kernels: 2.76 us -> 1.9 us  [local(): pl.pallas_call(functools.partial(table_kernel, outer, inner), out_shape=(...]
where the time goes in v4:
time: 51.3 us; the launch traced here: 50.5 us
  starting transfers between devices  24.1 us (47%)
  waiting for transfers between devices  13.8 us (27%)
  Pallas kernels  11.9 us (23%)
  between operations  0.7 us (1%)
    ppermute x12, starting transfers between devices, passed(): return lax.ppermute(value, axis, [(i, target(i)) for i in range(count)])  19.1 us
    ppermute x12, waiting for transfers between devices, passed(): return lax.ppermute(value, axis, [(i, target(i)) for i in range(count)])  12.4 us
    all_to_all x1, starting transfers between devices, local(): shares = lax.all_to_all(shares, ('gx', 'gy'), 0, 0, tiled=True)  4.96 us
    pallas_call x1, Pallas kernels, local(): pl.pallas_call(split_kernel, out_shape=matrix, in_specs=[VMEM, HBM], out_...  3.04 us
    pallas_call x1, Pallas kernels, local(): pl.pallas_call(functools.partial(later_kernel, 2), out_shape=(state, stat...  2.33 us
    pallas_call x1, Pallas kernels, local(): pl.pallas_call(functools.partial(table_kernel, outer, inner), out_shape=(...  1.9 us
    pallas_call x1, Pallas kernels, local(): pl.pallas_call(functools.partial(later_kernel, 1), out_shape=(state, stat...  1.73 us
    pallas_call x1, Pallas kernels, local(): pl.pallas_call(first_kernel, out_shape=(state, pack, pack, pack, pack, mo...  1.66 us
  transfers between devices with their start and end apart: 13, of which 6 were waited for; matrix products, arithmetic and copies ran while one was open for 0% of the time, Pallas kernels for 6%

profile of v4, /device:TPU:0, one launch (start us, length us, event | category | flops | bytes accessed | tf_op | source)
XLA Modules:
  0.0 50.5 jit_solution(10573885178947794170)
XLA Ops:
  0.6 1.9 %table.1 = (s32[304]{0:T(512)S(4)}, f32[384,128]{1,0:T(8,128)S(1)}, f32[8,8,128]{2,1,0:T(8,128)S(1)}, f32[8,8,128]{2,1,0:T(8,128)S(1)}, f32[5,384,384]{2,1,0:T(8,128)S(1)}) custom-call(s32[6,16]{1,0:T(8,128)} %bitcast.6, f32[48,1024]{1,0:T(8,128)} %source_hbm.1, f32[16,384,384]{2,1,0:T(8,128)} %matrix.3), custom_call_target="tpu_custom_call" | custom-call | tf_op jit(solution)/shard_map/table/pallas_call | solution.py:413
  2.5 4.8 %collective-permute-start = (f32[8,8,128]{2,1,0:T(8,128)S(1)}, f32[8,8,128]{2,1,0:T(8,128)S(1)}, u32[]{:S(2)}, u32[]{:S(2)}) collective-permute-start(f32[8,8,128]{2,1,0:T(8,128)S(1)} %get-tuple-element.27), channel_id=1, source_target_pairs={{0,31},{1,0},{2,1},{3,2},{4,3},{5,4},{6,5},{7,6},{8,7},{9,8},{10,9... | collective-permute-start | bytes 98312 | tf_op jit(solution)/shard_map/ppermute | solution.py:380
  7.3 4.0 %collective-permute-start.1 = (f32[8,8,128]{2,1,0:T(8,128)S(1)}, f32[8,8,128]{2,1,0:T(8,128)S(1)}, u32[]{:S(2)}, u32[]{:S(2)}) collective-permute-start(f32[8,8,128]{2,1,0:T(8,128)S(1)} %get-tuple-element.28), channel_id=1, source_target_pairs={{0,96},{32,0},{64,32},{96,64},{1,97},{33,1},{65,33},{97,65},{2,98}... | collective-permute-start | bytes 98312 | tf_op jit(solution)/shard_map/ppermute | solution.py:380
  11.4 3.0 %split.1.parts = bf16[16,768,384]{2,1,0:T(8,128)(2,1)S(1)} custom-call(f32[5,384,384]{2,1,0:T(8,128)S(1)} %get-tuple-element.29.early, f32[16,384,384]{2,1,0:T(8,128)} %matrix.3), custom_call_target="tpu_custom_call" | custom-call | flops 10000000 | bytes 18874368 | tf_op jit(solution)/shard_map/split/pallas_call | solution.py:438
  14.4 0.0 collective-permute-done.ghost_y
  14.4 0.0 collective-permute-done.1.ghost_x
  14.4 1.7 %first.1 = (f32[16,3,16,128]{3,2,1,0:T(8,128)S(1)}, f32[4,16,128]{2,1,0:T(8,128)S(1)}, f32[4,16,128]{2,1,0:T(8,128)S(1)}, f32[4,16,128]{2,1,0:T(8,128)S(1)}, f32...) custom-call(s32[304]{0:T(512)S(4)} %get-tuple-element.25.table, f32[384,128]{1,0:T(8,128)S(1)} %get-tuple-element.26.pairs, ...), custom_call_target="tpu_custom_call" | custom-call | tf_op jit(solution)/shard_map/first/pallas_call | solution.py:451
  16.1 0.5 collective-permute-start.2
  16.6 1.1 %collective-permute-start.3 = (f32[4,16,128]{2,1,0:T(8,128)S(1)}, f32[4,16,128]{2,1,0:T(8,128)S(1)}, u32[]{:S(2)}, u32[]{:S(2)}) collective-permute-start(f32[4,16,128]{2,1,0:T(8,128)S(1)} %get-tuple-element.32), channel_id=1, source_target_pairs={{0,32},{32,0},{64,96},{96,64},{1,33},{33,1},{65,97},{97,65},{2,34}... | collective-permute-start | bytes 98312 | tf_op jit(solution)/shard_map/ppermute | solution.py:380
  17.7 2.5 %collective-permute-start.4 = (f32[4,16,128]{2,1,0:T(8,128)S(1)}, f32[4,16,128]{2,1,0:T(8,128)S(1)}, u32[]{:S(2)}, u32[]{:S(2)}) collective-permute-start(f32[4,16,128]{2,1,0:T(8,128)S(1)} %get-tuple-element.33), channel_id=1, source_target_pairs={{0,96},{32,64},{64,32},{96,0},{1,97},{33,65},{65,33},{97,1},{2,98}... | collective-permute-start | bytes 98312 | tf_op jit(solution)/shard_map/ppermute | solution.py:380
  20.2 0.0 collective-permute-start.5
  20.2 2.7 %collective-permute-done.2.yb = f32[4,16,128]{2,1,0:T(8,128)S(1)} collective-permute-done((f32[4,16,128]{2,1,0:T(8,128)S(1)}, f32[4,16,128]{2,1,0:T(8,128)S(1)}, u32[]{:S(2)}, u32[]{:S(2)}) %collective-permute-start.2) | collective-permute-done | bytes 32800 | tf_op jit(solution)/shard_map/ppermute | solution.py:380
  22.9 0.0 collective-permute-done.3.xa
  22.9 0.0 collective-permute-done.4.xb
  22.9 0.0 collective-permute-done.5.ya
  22.9 1.7 %second.1 = (f32[16,3,16,128]{3,2,1,0:T(8,128)S(1)}, f32[16,3,16,128]{3,2,1,0:T(8,128)S(1)}, f32[4,16,128]{2,1,0:T(8,128)S(1)}, f32[4,16,128]{2,1,0:T(8,128)S(1)...) custom-call(s32[304]{0:T(512)S(4)} %get-tuple-element.25.table, ...), custom_call_target="tpu_custom_call" | custom-call | tf_op jit(solution)/shard_map/second/pallas_call | solution.py:460
  24.6 2.5 %collective-permute-start.6 = (f32[4,16,128]{2,1,0:T(8,128)S(1)}, f32[4,16,128]{2,1,0:T(8,128)S(1)}, u32[]{:S(2)}, u32[]{:S(2)}) collective-permute-start(f32[4,16,128]{2,1,0:T(8,128)S(1)} %get-tuple-element.37), channel_id=1, source_target_pairs={{0,31},{1,2},{2,1},{3,4},{4,3},{5,6},{6,5},{7,8},{8,7},{9,10},{10,... | collective-permute-start | bytes 98312 | tf_op jit(solution)/shard_map/ppermute | solution.py:380
  27.1 0.5 %collective-permute-start.7 = (f32[4,16,128]{2,1,0:T(8,128)S(1)}, f32[4,16,128]{2,1,0:T(8,128)S(1)}, u32[]{:S(2)}, u32[]{:S(2)}) collective-permute-start(f32[4,16,128]{2,1,0:T(8,128)S(1)} %get-tuple-element.38), channel_id=1, source_target_pairs={{0,32},{32,0},{64,96},{96,64},{1,33},{33,1},{65,97},{97,65},{2,34}... | collective-permute-start | bytes 98312 | tf_op jit(solution)/shard_map/ppermute | solution.py:380
  27.6 2.1 %collective-permute-start.8 = (f32[4,16,128]{2,1,0:T(8,128)S(1)}, f32[4,16,128]{2,1,0:T(8,128)S(1)}, u32[]{:S(2)}, u32[]{:S(2)}) collective-permute-start(f32[4,16,128]{2,1,0:T(8,128)S(1)} %get-tuple-element.39), channel_id=1, source_target_pairs={{0,96},{32,64},{64,32},{96,0},{1,97},{33,65},{65,33},{97,1},{2,98}... | collective-permute-start | bytes 98312 | tf_op jit(solution)/shard_map/ppermute | solution.py:380
  29.6 0.0 collective-permute-start.9
  29.6 1.7 %collective-permute-done.6.yb = f32[4,16,128]{2,1,0:T(8,128)S(1)} collective-permute-done((f32[4,16,128]{2,1,0:T(8,128)S(1)}, f32[4,16,128]{2,1,0:T(8,128)S(1)}, u32[]{:S(2)}, u32[]{:S(2)}) %collective-permute-start.6) | collective-permute-done | bytes 32800 | tf_op jit(solution)/shard_map/ppermute | solution.py:380
  31.3 0.0 collective-permute-done.7.xa
  31.3 1.4 %collective-permute-done.8.xb = f32[4,16,128]{2,1,0:T(8,128)S(1)} collective-permute-done((f32[4,16,128]{2,1,0:T(8,128)S(1)}, f32[4,16,128]{2,1,0:T(8,128)S(1)}, u32[]{:S(2)}, u32[]{:S(2)}) %collective-permute-start.8) | collective-permute-done | bytes 32800 | tf_op jit(solution)/shard_map/ppermute | solution.py:380
  32.7 0.0 collective-permute-done.9.ya
  32.7 2.3 %third.1 = (f32[16,3,16,128]{3,2,1,0:T(8,128)S(1)}, f32[16,3,16,128]{3,2,1,0:T(8,128)S(1)}, f32[4,16,128]{2,1,0:T(8,128)S(1)}, f32[4,16,128]{2,1,0:T(8,128)S(1)}, f32[128,128]{1,0:T(8,128)}) custom-call(s32[304]{0:T(512)S(4)} %get-tuple-element.25.table, f32[16,3,16,128]{3,2,1,0:T(8,128)S(1)} %get-tuple-element.36.previous, ...), custom_call_target="tpu_custom_call" | custom-call | tf_op jit(solution)/shard_map/third/pallas_call | solution.py:469
  35.1 5.0 %all-to-all-start = ((f32[128,1,128]{2,1,0:T(1,128)}), f32[128,1,128]{2,1,0:T(1,128)S(1)}, u32[]{:S(2)}, u32[]{:S(2)}) async-start(f32[128,1,128]{2,1,0:T(1,128)} %bitcast.2), calls=%async_computation | async-start | bytes 131072 | tf_op jit(solution)/shard_map/all_to_all | solution.py:479
  40.0 1.1 %collective-permute-start.10 = (f32[4,16,128]{2,1,0:T(8,128)S(1)}, f32[4,16,128]{2,1,0:T(8,128)S(1)}, u32[]{:S(2)}, u32[]{:S(2)}) collective-permute-start(f32[4,16,128]{2,1,0:T(8,128)S(1)} %get-tuple-element.46), channel_id=1, source_target_pairs={{0,32},{32,64},{64,96},{96,0},{1,33},{33,65},{65,97},{97,1},{2,34}... | collective-permute-start | bytes 98312 | tf_op jit(solution)/shard_map/ppermute | solution.py:380
  41.2 0.0 collective-permute-start.11
  41.2 4.1 %collective-permute-done.10.prev_x = f32[4,16,128]{2,1,0:T(8,128)S(1)} collective-permute-done((f32[4,16,128]{2,1,0:T(8,128)S(1)}, f32[4,16,128]{2,1,0:T(8,128)S(1)}, u32[]{:S(2)}, u32[]{:S(2)}) %collective-permute-start.10) | collective-permute-done | bytes 32800 | tf_op jit(solution)/shard_map/ppermute | solution.py:380
  45.2 2.6 %collective-permute-done.11.prev_y = f32[4,16,128]{2,1,0:T(8,128)S(1)} collective-permute-done((f32[4,16,128]{2,1,0:T(8,128)S(1)}, f32[4,16,128]{2,1,0:T(8,128)S(1)}, u32[]{:S(2)}, u32[]{:S(2)}) %collective-permute-start.11) | collective-permute-done | bytes 32800 | tf_op jit(solution)/shard_map/ppermute | solution.py:380
  47.8 1.4 %all-to-all-done = f32[128,1,128]{2,1,0:T(1,128)S(1)} async-done(((f32[128,1,128]{2,1,0:T(1,128)}), f32[128,1,128]{2,1,0:T(1,128)S(1)}, u32[]{:S(2)}, u32[]{:S(2)}) %all-to-all-start) | async-done | bytes 65568 | tf_op jit(solution)/shard_map/all_to_all | solution.py:479
  49.3 1.2 %final.1 = (f32[48,1024]{1,0:T(8,128)}, f32[48,1024]{1,0:T(8,128)}) custom-call(s32[304]{0:T(512)S(4)} %get-tuple-element.25.table, f32[128,128]{1,0:T(8,128)S(1)} %bitcast.5, f32[384,128]{1,0:T(8,128)S(1)} %get-tuple-element.26.pairs, f32[16,3,16,128]{3,2,1,0:T(8,128)S(1)} %get-tuple-element.43.firsts, f32[16,3,16,128]{3,2,1,0:T(8,128)S(1)} %get-tuple-element.44.seconds, ...), custom_call_target="tpu_custom_call" | custom-call | tf_op jit(solution)/shard_map/final/pallas_call | solution.py:481
Async XLA Ops:
  2.5 11.9 %collective-permute-start = (f32[8,8,128]{2,1,0:T(8,128)S(1)}, f32[8,8,128]{2,1,0:T(8,128)S(1)}, u32[]{:S(2)}, u32[]{:S(2)}) collective-permute-start(f32[8,8,128]{2,1,0:T(8,128)S(1)} %get-tuple-element.27), channel_id=1, source_target_pairs={{0,31},{1,0},{2,1},{3,2},{4,3},{5,4},{6,5},{7,6},{8,7},{9,8},{10,9... | collective-permute-start | bytes 98312 | tf_op jit(solution)/shard_map/ppermute | solution.py:380
  7.3 7.1 %collective-permute-start.1 = (f32[8,8,128]{2,1,0:T(8,128)S(1)}, f32[8,8,128]{2,1,0:T(8,128)S(1)}, u32[]{:S(2)}, u32[]{:S(2)}) collective-permute-start(f32[8,8,128]{2,1,0:T(8,128)S(1)} %get-tuple-element.28), channel_id=1, source_target_pairs={{0,96},{32,0},{64,32},{96,64},{1,97},{33,1},{65,33},{97,65},{2,98}... | collective-permute-start | bytes 98312 | tf_op jit(solution)/shard_map/ppermute | solution.py:380
  16.1 6.7 %collective-permute-start.2 = (f32[4,16,128]{2,1,0:T(8,128)S(1)}, f32[4,16,128]{2,1,0:T(8,128)S(1)}, u32[]{:S(2)}, u32[]{:S(2)}) collective-permute-start(f32[4,16,128]{2,1,0:T(8,128)S(1)} %get-tuple-element.31), channel_id=1, source_target_pairs={{0,31},{1,2},{2,1},{3,4},{4,3},{5,6},{6,5},{7,8},{8,7},{9,10},{10,... | collective-permute-start | bytes 98312 | tf_op jit(solution)/shard_map/ppermute | solution.py:380
  16.6 6.3 %collective-permute-start.3 = (f32[4,16,128]{2,1,0:T(8,128)S(1)}, f32[4,16,128]{2,1,0:T(8,128)S(1)}, u32[]{:S(2)}, u32[]{:S(2)}) collective-permute-start(f32[4,16,128]{2,1,0:T(8,128)S(1)} %get-tuple-element.32), channel_id=1, source_target_pairs={{0,32},{32,0},{64,96},{96,64},{1,33},{33,1},{65,97},{97,65},{2,34}... | collective-permute-start | bytes 98312 | tf_op jit(solution)/shard_map/ppermute | solution.py:380
  17.7 5.2 %collective-permute-start.4 = (f32[4,16,128]{2,1,0:T(8,128)S(1)}, f32[4,16,128]{2,1,0:T(8,128)S(1)}, u32[]{:S(2)}, u32[]{:S(2)}) collective-permute-start(f32[4,16,128]{2,1,0:T(8,128)S(1)} %get-tuple-element.33), channel_id=1, source_target_pairs={{0,96},{32,64},{64,32},{96,0},{1,97},{33,65},{65,33},{97,1},{2,98}... | collective-permute-start | bytes 98312 | tf_op jit(solution)/shard_map/ppermute | solution.py:380
  20.2 2.7 %collective-permute-start.5 = (f32[4,16,128]{2,1,0:T(8,128)S(1)}, f32[4,16,128]{2,1,0:T(8,128)S(1)}, u32[]{:S(2)}, u32[]{:S(2)}) collective-permute-start(f32[4,16,128]{2,1,0:T(8,128)S(1)} %get-tuple-element.34), channel_id=1, source_target_pairs={{0,1},{1,0},{2,3},{3,2},{4,5},{5,4},{6,7},{7,6},{8,9},{9,8},{10,11... | collective-permute-start | bytes 98312 | tf_op jit(solution)/shard_map/ppermute | solution.py:380
  24.6 6.7 %collective-permute-start.6 = (f32[4,16,128]{2,1,0:T(8,128)S(1)}, f32[4,16,128]{2,1,0:T(8,128)S(1)}, u32[]{:S(2)}, u32[]{:S(2)}) collective-permute-start(f32[4,16,128]{2,1,0:T(8,128)S(1)} %get-tuple-element.37), channel_id=1, source_target_pairs={{0,31},{1,2},{2,1},{3,4},{4,3},{5,6},{6,5},{7,8},{8,7},{9,10},{10,... | collective-permute-start | bytes 98312 | tf_op jit(solution)/shard_map/ppermute | solution.py:380
  27.1 4.3 %collective-permute-start.7 = (f32[4,16,128]{2,1,0:T(8,128)S(1)}, f32[4,16,128]{2,1,0:T(8,128)S(1)}, u32[]{:S(2)}, u32[]{:S(2)}) collective-permute-start(f32[4,16,128]{2,1,0:T(8,128)S(1)} %get-tuple-element.38), channel_id=1, source_target_pairs={{0,32},{32,0},{64,96},{96,64},{1,33},{33,1},{65,97},{97,65},{2,34}... | collective-permute-start | bytes 98312 | tf_op jit(solution)/shard_map/ppermute | solution.py:380
  27.6 5.1 %collective-permute-start.8 = (f32[4,16,128]{2,1,0:T(8,128)S(1)}, f32[4,16,128]{2,1,0:T(8,128)S(1)}, u32[]{:S(2)}, u32[]{:S(2)}) collective-permute-start(f32[4,16,128]{2,1,0:T(8,128)S(1)} %get-tuple-element.39), channel_id=1, source_target_pairs={{0,96},{32,64},{64,32},{96,0},{1,97},{33,65},{65,33},{97,1},{2,98}... | collective-permute-start | bytes 98312 | tf_op jit(solution)/shard_map/ppermute | solution.py:380
  29.6 3.1 %collective-permute-start.9 = (f32[4,16,128]{2,1,0:T(8,128)S(1)}, f32[4,16,128]{2,1,0:T(8,128)S(1)}, u32[]{:S(2)}, u32[]{:S(2)}) collective-permute-start(f32[4,16,128]{2,1,0:T(8,128)S(1)} %get-tuple-element.40), channel_id=1, source_target_pairs={{0,1},{1,0},{2,3},{3,2},{4,5},{5,4},{6,7},{7,6},{8,9},{9,8},{10,11... | collective-permute-start | bytes 98312 | tf_op jit(solution)/shard_map/ppermute | solution.py:380
  35.1 14.2 %all-to-all-start = ((f32[128,1,128]{2,1,0:T(1,128)}), f32[128,1,128]{2,1,0:T(1,128)S(1)}, u32[]{:S(2)}, u32[]{:S(2)}) async-start(f32[128,1,128]{2,1,0:T(1,128)} %bitcast.2), calls=%async_computation | async-start | bytes 131072 | tf_op jit(solution)/shard_map/all_to_all | solution.py:479
  40.0 5.2 %collective-permute-start.10 = (f32[4,16,128]{2,1,0:T(8,128)S(1)}, f32[4,16,128]{2,1,0:T(8,128)S(1)}, u32[]{:S(2)}, u32[]{:S(2)}) collective-permute-start(f32[4,16,128]{2,1,0:T(8,128)S(1)} %get-tuple-element.46), channel_id=1, source_target_pairs={{0,32},{32,64},{64,96},{96,0},{1,33},{33,65},{65,97},{97,1},{2,34}... | collective-permute-start | bytes 98312 | tf_op jit(solution)/shard_map/ppermute | solution.py:380
  41.2 6.7 %collective-permute-start.11 = (f32[4,16,128]{2,1,0:T(8,128)S(1)}, f32[4,16,128]{2,1,0:T(8,128)S(1)}, u32[]{:S(2)}, u32[]{:S(2)}) collective-permute-start(f32[4,16,128]{2,1,0:T(8,128)S(1)} %get-tuple-element.47), channel_id=1, source_target_pairs={{0,1},{1,2},{2,3},{3,4},{4,5},{5,6},{6,7},{7,8},{8,9},{9,10},{10,1... | collective-permute-start | bytes 98312 | tf_op jit(solution)/shard_map/ppermute | solution.py:380

commit v5 on v4

--- a/solution.py
+++ b/solution.py
@@ -13,7 +13,7 @@
 ROWS = 48
 SLOTS = 8
 ORDER = 384
-EARLY = 5
+EARLY = 6
 
 LOW = 0
 UPP = 68
@@ -42,6 +42,14 @@
     return lax.broadcasted_iota(jnp.int32, shape, len(shape) - 1) < BLOCK
 
 
+def into_pairs(source, pairs, first):
+    for group in range(ROWS // 8):
+        for pair in range(8):
+            pairs[pl.ds((first + group * 8) * 8 + pair, 8, stride=8), :] = source[
+                group * 8 : group * 8 + 8, pair * 128 : pair * 128 + 128
+            ]
+
+
 def matrix_copies(matrix, target, begin, end, sems):
     return [
         pltpu.make_async_copy(matrix.at[i], target.at[i - begin], sems.at[i - begin])
@@ -49,7 +57,7 @@
     ]
 
 
-def table_kernel(outer, inner, faces_hbm, source_hbm, matrix, table, pairs, down_x, down_y, early,
+def table_kernel(outer, inner, faces_hbm, source_hbm, matrix, table, pairs, down_x, early,
                  owner, user, faces, source, sems, faces_sem, source_sem):
     faces_copy = pltpu.make_async_copy(faces_hbm, faces, faces_sem)
     source_copy = pltpu.make_async_copy(source_hbm, source, source_sem)
@@ -81,6 +89,8 @@
                 here = jnp.logical_and(row >= 0, row < ROWS)
                 row = jnp.where(here, row, face - shifts[axis])
             user[row] = element
+            if axis == 1:
+                row = jnp.where(here, row, row - (ROWS - SLOTS))
             table[ROW_UPP + at] = row
     ends = [jnp.int32(SEND_DOWN), jnp.int32(SEND_DOWN + LIST)]
     for row in range(ROWS):
@@ -104,17 +114,13 @@
         for slot in range(SLOTS):
             at = table[SEND_UP + axis * LIST + slot] * 4 + axis
             table[UPP + at] = ELEMENTS + slot
-            table[ROW_UPP + at] = ROWS + axis * SLOTS + slot
+            if axis == 0:
+                table[ROW_UPP + at] = ROWS + slot
     source_copy.wait()
-    for group in range(ROWS // 8):
-        for pair in range(8):
-            pairs[pl.ds(group * 64 + pair, 8, stride=8), :] = source[
-                group * 8 : group * 8 + 8, pair * 128 : pair * 128 + 128
-            ]
-    for axis, out in enumerate((down_x, down_y)):
-        for slot in range(SLOTS):
-            row = table[ROW_LOW + table[SEND_DOWN + axis * LIST + slot]]
-            out[slot] = pairs[pl.ds(pl.multiple_of(row * 8, 8), 8), :]
+    into_pairs(source, pairs, 0)
+    for slot in range(SLOTS):
+        row = table[ROW_LOW + table[SEND_DOWN + slot]]
+        down_x[slot] = pairs[pl.ds(pl.multiple_of(row * 8, 8), 8), :]
     for copy in copies:
         copy.wait()
 
@@ -207,17 +213,19 @@
     return jnp.concatenate([even, odd], axis=0)
 
 
-def first_kernel(table, pairs, ghost_y, ghost_x, parts,
+def first_kernel(table, pairs, next_y, next_x, parts,
                  flux, xa, xb, ya, yb, sums, rows, left):
-    for row in range(ROWS):
-        rows[row] = pairs[row * 8 : row * 8 + 8, :]
-    for axis, ghost in enumerate((ghost_x, ghost_y)):
-        for slot in range(SLOTS):
-            rows[ROWS + axis * SLOTS + slot] = ghost[slot]
+    rows[: ROWS * 8, :] = pairs[...]
+    for slot in range(SLOTS):
+        rows[(ROWS + slot) * 8 : (ROWS + slot) * 8 + 8, :] = next_x[slot]
+    into_pairs(next_y, rows, ROWS + SLOTS)
+
+    def face(at):
+        return rows[pl.ds(pl.multiple_of(table[at] * 8, 8), 8), :]
 
     def get(element, axis):
         at = element * 4 + axis
-        return tile_of(rows[table[ROW_LOW + at]], rows[table[ROW_UPP + at]])
+        return tile_of(face(ROW_LOW + at), face(ROW_UPP + at))
 
     multiply(0, table, get, parts, None, flux, (xa, xb, ya, yb), None, sums, left)
 
@@ -324,7 +332,7 @@
     return value
 
 
-def final_kernel(table, shares, pairs, firsts, seconds, flux, prev_x, prev_y, answer, residual,
+def final_kernel(table, shares, pairs, firsts, seconds, flux, prev_y, prev_x, answer, residual,
                  every, answer_pairs, residual_pairs):
     low_half = in_low_half((8, 128))
     total = total_of(shares)
@@ -402,7 +410,6 @@
 def local(heat_source, stiffness, element_faces):
     outer, inner = lax.axis_size("gx"), lax.axis_size("gy")
     pack = vmem((4, SOURCES, 128))
-    face = vmem((SLOTS, 8, 128))
     state = vmem((ELEMENTS, 3, SOURCES, 128))
     matrix = vmem((ELEMENTS, 2 * ORDER, ORDER), jnp.bfloat16)
     moment = vmem((SOURCES, 128))
@@ -410,17 +417,17 @@
     every = pltpu.VMEM((ELEMENTS + SLOTS, 3, SOURCES, 128), jnp.float32)
     pairs_shape = (ROWS * 8, 128)
 
-    table, pairs, down_x, down_y, early = pl.pallas_call(
+    next_y = back(heat_source, "gy")
+    table, pairs, down_x, early = pl.pallas_call(
         functools.partial(table_kernel, outer, inner),
         out_shape=(
             pltpu.SMEM((TABLE,), jnp.int32),
             vmem(pairs_shape),
-            face,
-            face,
+            vmem((SLOTS, 8, 128)),
             vmem((EARLY, ORDER, ORDER)),
         ),
         in_specs=[HBM, HBM, HBM],
-        out_specs=(SMEM, VMEM, VMEM, VMEM, VMEM),
+        out_specs=(SMEM, VMEM, VMEM, VMEM),
         scratch_shapes=[
             pltpu.SMEM((ROWS,), jnp.int32),
             pltpu.SMEM((3 * ROWS,), jnp.int32),
@@ -433,8 +440,6 @@
         compiler_params=params(52),
         name="table",
     )(element_faces.T, heat_source, stiffness)
-    ghost_y = back(down_y, "gy")
-    ghost_x = back(down_x, "gx")
     parts = pl.pallas_call(
         split_kernel,
         out_shape=matrix,
@@ -453,10 +458,10 @@
         out_shape=(state, pack, pack, pack, pack, moment),
         in_specs=[SMEM] + [VMEM] * 4,
         out_specs=(VMEM,) * 6,
-        scratch_shapes=[pltpu.VMEM((64, 8, 128), jnp.float32), left],
+        scratch_shapes=[pltpu.VMEM(((2 * ROWS + SLOTS) * 8, 128), jnp.float32), left],
         compiler_params=params(),
         name="first",
-    )(table, pairs, ghost_y, ghost_x, parts)
+    )(table, pairs, next_y, back(down_x, "gx"), parts)
     k1, flux, *sends, moments = pl.pallas_call(
         functools.partial(later_kernel, 1),
         out_shape=(state, state, pack, pack, pack, pack, moment),
@@ -475,7 +480,7 @@
         compiler_params=params(),
         name="third",
     )(table, flux, *exchanged(sends), moments, parts)
-    prev_x, prev_y = ahead(up_x, "gx"), ahead(up_y, "gy")
+    prev_y, prev_x = ahead(up_y, "gy"), ahead(up_x, "gx")
     shares = lax.all_to_all(shares, ("gx", "gy"), 0, 0, tiled=True)
     natural = jax.ShapeDtypeStruct((ROWS, SOURCES * BLOCK), jnp.float32)
     return pl.pallas_call(
@@ -486,7 +491,7 @@
         scratch_shapes=[every, pltpu.VMEM(pairs_shape, jnp.float32), pltpu.VMEM(pairs_shape, jnp.float32)],
         compiler_params=params(),
         name="final",
-    )(table, shares, pairs, k1, k2, flux, prev_x, prev_y)
+    )(table, shares, pairs, k1, k2, flux, prev_y, prev_x)
 
 
 def solution(mesh):

time: 51.3 us -> 51.4 us (level)
    ppermute x12, waiting for transfers between devices: 12.4 us -> 11 us  [passed(): return lax.ppermute(value, axis, [(i, target(i)) for i in range(count)])]
    all_to_all x1, waiting for transfers between devices: 1.42 us -> 2.49 us  [local(): shares = lax.all_to_all(shares, ('gx', 'gy'), 0, 0, tiled=True)]
  transfers between devices with their start and end apart: 13 -> 13, of which waited for: 6 -> 5; matrix products, arithmetic and copies ran while one was open for 0% -> 0% of each run, Pallas kernels for 6% -> 10%
where the time goes in v5:
time: 51.4 us; the launch traced here: 50.5 us
  starting transfers between devices  24.4 us (47%)
  waiting for transfers between devices  13.5 us (26%)
  Pallas kernels  11.9 us (23%)
  between operations  0.71 us (1%)
    ppermute x12, starting transfers between devices, passed(): return lax.ppermute(value, axis, [(i, target(i)) for i in range(count)])  19.5 us
    ppermute x12, waiting for transfers between devices, passed(): return lax.ppermute(value, axis, [(i, target(i)) for i in range(count)])  11 us
    all_to_all x1, starting transfers between devices, local(): shares = lax.all_to_all(shares, ('gx', 'gy'), 0, 0, tiled=True)  4.93 us
    pallas_call x1, Pallas kernels, local(): pl.pallas_call(split_kernel, out_shape=matrix, in_specs=[VMEM, HBM], out_...  2.87 us
    all_to_all x1, waiting for transfers between devices, local(): shares = lax.all_to_all(shares, ('gx', 'gy'), 0, 0, tiled=True)  2.49 us
    pallas_call x1, Pallas kernels, local(): pl.pallas_call(functools.partial(later_kernel, 2), out_shape=(state, stat...  2.33 us
    pallas_call x1, Pallas kernels, local(): pl.pallas_call(functools.partial(table_kernel, outer, inner), out_shape=(...  2.08 us
    pallas_call x1, Pallas kernels, local(): pl.pallas_call(functools.partial(later_kernel, 1), out_shape=(state, stat...  1.73 us
  transfers between devices with their start and end apart: 13, of which 5 were waited for; matrix products, arithmetic and copies ran while one was open for 0% of the time, Pallas kernels for 10%

profile of v5, /device:TPU:0, one launch (start us, length us, event | category | flops | bytes accessed | tf_op | source)
XLA Modules:
  0.0 50.5 jit_solution(1235150132933247391)
XLA Ops:
  0.6 4.8 %collective-permute-start = (f32[48,1024]{1,0:T(8,128)}, f32[48,1024]{1,0:T(8,128)S(1)}, u32[]{:S(2)}, u32[]{:S(2)}) collective-permute-start(f32[48,1024]{1,0:T(8,128)} %source_hbm.1), channel_id=1, source_target_pairs={{0,31},{1,0},{2,1},{3,2},{4,3},{5,4},{6,5},{7,6},{8,7},{9,8},{10,9... | collective-permute-start | bytes 589832 | tf_op jit(solution)/shard_map/ppermute | solution.py:388
  5.4 2.1 %table.1 = (s32[304]{0:T(512)S(4)}, f32[384,128]{1,0:T(8,128)S(1)}, f32[8,8,128]{2,1,0:T(8,128)S(1)}, f32[6,384,384]{2,1,0:T(8,128)S(1)}) custom-call(s32[6,16]{1,0:T(8,128)} %bitcast.6, f32[48,1024]{1,0:T(8,128)} %source_hbm.1, f32[16,384,384]{2,1,0:T(8,128)} %matrix.3), custom_call_target="tpu_custom_call" | custom-call | tf_op jit(solution)/shard_map/table/pallas_call | solution.py:421
  7.5 4.1 %collective-permute-start.1 = (f32[8,8,128]{2,1,0:T(8,128)S(1)}, f32[8,8,128]{2,1,0:T(8,128)S(1)}, u32[]{:S(2)}, u32[]{:S(2)}) collective-permute-start(f32[8,8,128]{2,1,0:T(8,128)S(1)} %get-tuple-element.26), channel_id=1, source_target_pairs={{0,96},{32,0},{64,32},{96,64},{1,97},{33,1},{65,33},{97,65},{2,98}... | collective-permute-start | bytes 98312 | tf_op jit(solution)/shard_map/ppermute | solution.py:388
  11.6 2.9 %split.1.parts = bf16[16,768,384]{2,1,0:T(8,128)(2,1)S(1)} custom-call(f32[6,384,384]{2,1,0:T(8,128)S(1)} %get-tuple-element.27.early, f32[16,384,384]{2,1,0:T(8,128)} %matrix.3), custom_call_target="tpu_custom_call" | custom-call | flops 10000000 | bytes 18874368 | tf_op jit(solution)/shard_map/split/pallas_call | solution.py:443
  14.5 0.0 collective-permute-done.1.next_x
  14.5 0.0 collective-permute-done.next_y
  14.5 1.7 %first.1 = (f32[16,3,16,128]{3,2,1,0:T(8,128)S(1)}, f32[4,16,128]{2,1,0:T(8,128)S(1)}, f32[4,16,128]{2,1,0:T(8,128)S(1)}, f32[4,16,128]{2,1,0:T(8,128)S(1)}, f32...) custom-call(s32[304]{0:T(512)S(4)} %get-tuple-element.24.table, f32[384,128]{1,0:T(8,128)S(1)} %get-tuple-element.25.pairs, ...), custom_call_target="tpu_custom_call" | custom-call | tf_op jit(solution)/shard_map/first/pallas_call | solution.py:456
  16.2 0.5 collective-permute-start.2
  16.7 1.1 %collective-permute-start.3 = (f32[4,16,128]{2,1,0:T(8,128)S(1)}, f32[4,16,128]{2,1,0:T(8,128)S(1)}, u32[]{:S(2)}, u32[]{:S(2)}) collective-permute-start(f32[4,16,128]{2,1,0:T(8,128)S(1)} %get-tuple-element.30), channel_id=1, source_target_pairs={{0,32},{32,0},{64,96},{96,64},{1,33},{33,1},{65,97},{97,65},{2,34}... | collective-permute-start | bytes 98312 | tf_op jit(solution)/shard_map/ppermute | solution.py:388
  17.7 2.5 %collective-permute-start.4 = (f32[4,16,128]{2,1,0:T(8,128)S(1)}, f32[4,16,128]{2,1,0:T(8,128)S(1)}, u32[]{:S(2)}, u32[]{:S(2)}) collective-permute-start(f32[4,16,128]{2,1,0:T(8,128)S(1)} %get-tuple-element.31), channel_id=1, source_target_pairs={{0,96},{32,64},{64,32},{96,0},{1,97},{33,65},{65,33},{97,1},{2,98}... | collective-permute-start | bytes 98312 | tf_op jit(solution)/shard_map/ppermute | solution.py:388
  20.3 0.0 collective-permute-start.5
  20.3 2.7 %collective-permute-done.2.yb = f32[4,16,128]{2,1,0:T(8,128)S(1)} collective-permute-done((f32[4,16,128]{2,1,0:T(8,128)S(1)}, f32[4,16,128]{2,1,0:T(8,128)S(1)}, u32[]{:S(2)}, u32[]{:S(2)}) %collective-permute-start.2) | collective-permute-done | bytes 32800 | tf_op jit(solution)/shard_map/ppermute | solution.py:388
  23.0 0.0 collective-permute-done.3.xa
  23.0 0.0 collective-permute-done.4.xb
  23.0 0.0 collective-permute-done.5.ya
  23.0 1.7 %second.1 = (f32[16,3,16,128]{3,2,1,0:T(8,128)S(1)}, f32[16,3,16,128]{3,2,1,0:T(8,128)S(1)}, f32[4,16,128]{2,1,0:T(8,128)S(1)}, f32[4,16,128]{2,1,0:T(8,128)S(1)...) custom-call(s32[304]{0:T(512)S(4)} %get-tuple-element.24.table, ...), custom_call_target="tpu_custom_call" | custom-call | tf_op jit(solution)/shard_map/second/pallas_call | solution.py:465
  24.7 2.5 %collective-permute-start.6 = (f32[4,16,128]{2,1,0:T(8,128)S(1)}, f32[4,16,128]{2,1,0:T(8,128)S(1)}, u32[]{:S(2)}, u32[]{:S(2)}) collective-permute-start(f32[4,16,128]{2,1,0:T(8,128)S(1)} %get-tuple-element.35), channel_id=1, source_target_pairs={{0,31},{1,2},{2,1},{3,4},{4,3},{5,6},{6,5},{7,8},{8,7},{9,10},{10,... | collective-permute-start | bytes 98312 | tf_op jit(solution)/shard_map/ppermute | solution.py:388
  27.2 0.5 %collective-permute-start.7 = (f32[4,16,128]{2,1,0:T(8,128)S(1)}, f32[4,16,128]{2,1,0:T(8,128)S(1)}, u32[]{:S(2)}, u32[]{:S(2)}) collective-permute-start(f32[4,16,128]{2,1,0:T(8,128)S(1)} %get-tuple-element.36), channel_id=1, source_target_pairs={{0,32},{32,0},{64,96},{96,64},{1,33},{33,1},{65,97},{97,65},{2,34}... | collective-permute-start | bytes 98312 | tf_op jit(solution)/shard_map/ppermute | solution.py:388
  27.7 2.2 %collective-permute-start.8 = (f32[4,16,128]{2,1,0:T(8,128)S(1)}, f32[4,16,128]{2,1,0:T(8,128)S(1)}, u32[]{:S(2)}, u32[]{:S(2)}) collective-permute-start(f32[4,16,128]{2,1,0:T(8,128)S(1)} %get-tuple-element.37), channel_id=1, source_target_pairs={{0,96},{32,64},{64,32},{96,0},{1,97},{33,65},{65,33},{97,1},{2,98}... | collective-permute-start | bytes 98312 | tf_op jit(solution)/shard_map/ppermute | solution.py:388
  29.9 0.0 collective-permute-start.9
  29.9 1.5 %collective-permute-done.6.yb = f32[4,16,128]{2,1,0:T(8,128)S(1)} collective-permute-done((f32[4,16,128]{2,1,0:T(8,128)S(1)}, f32[4,16,128]{2,1,0:T(8,128)S(1)}, u32[]{:S(2)}, u32[]{:S(2)}) %collective-permute-start.6) | collective-permute-done | bytes 32800 | tf_op jit(solution)/shard_map/ppermute | solution.py:388
  31.4 0.0 collective-permute-done.7.xa
  31.5 1.4 %collective-permute-done.8.xb = f32[4,16,128]{2,1,0:T(8,128)S(1)} collective-permute-done((f32[4,16,128]{2,1,0:T(8,128)S(1)}, f32[4,16,128]{2,1,0:T(8,128)S(1)}, u32[]{:S(2)}, u32[]{:S(2)}) %collective-permute-start.8) | collective-permute-done | bytes 32800 | tf_op jit(solution)/shard_map/ppermute | solution.py:388
  32.8 0.0 collective-permute-done.9.ya
  32.8 2.3 %third.1 = (f32[16,3,16,128]{3,2,1,0:T(8,128)S(1)}, f32[16,3,16,128]{3,2,1,0:T(8,128)S(1)}, f32[4,16,128]{2,1,0:T(8,128)S(1)}, f32[4,16,128]{2,1,0:T(8,128)S(1)}, f32[128,128]{1,0:T(8,128)}) custom-call(s32[304]{0:T(512)S(4)} %get-tuple-element.24.table, f32[16,3,16,128]{3,2,1,0:T(8,128)S(1)} %get-tuple-element.34.previous, ...), custom_call_target="tpu_custom_call" | custom-call | tf_op jit(solution)/shard_map/third/pallas_call | solution.py:474
  35.2 4.9 %all-to-all-start = ((f32[128,1,128]{2,1,0:T(1,128)}), f32[128,1,128]{2,1,0:T(1,128)S(1)}, u32[]{:S(2)}, u32[]{:S(2)}) async-start(f32[128,1,128]{2,1,0:T(1,128)} %bitcast.2), calls=%async_computation | async-start | bytes 131072 | tf_op jit(solution)/shard_map/all_to_all | solution.py:484
  40.1 0.1 collective-permute-start.10
  40.2 1.2 %collective-permute-start.11 = (f32[4,16,128]{2,1,0:T(8,128)S(1)}, f32[4,16,128]{2,1,0:T(8,128)S(1)}, u32[]{:S(2)}, u32[]{:S(2)}) collective-permute-start(f32[4,16,128]{2,1,0:T(8,128)S(1)} %get-tuple-element.45), channel_id=1, source_target_pairs={{0,32},{32,64},{64,96},{96,0},{1,33},{33,65},{65,97},{97,1},{2,34}... | collective-permute-start | bytes 98312 | tf_op jit(solution)/shard_map/ppermute | solution.py:388
  41.4 5.4 %collective-permute-done.10.prev_y = f32[4,16,128]{2,1,0:T(8,128)S(1)} collective-permute-done((f32[4,16,128]{2,1,0:T(8,128)S(1)}, f32[4,16,128]{2,1,0:T(8,128)S(1)}, u32[]{:S(2)}, u32[]{:S(2)}) %collective-permute-start.10) | collective-permute-done | bytes 32800 | tf_op jit(solution)/shard_map/ppermute | solution.py:388
  46.8 0.0 collective-permute-done.11.prev_x
  46.8 2.5 %all-to-all-done = f32[128,1,128]{2,1,0:T(1,128)S(1)} async-done(((f32[128,1,128]{2,1,0:T(1,128)}), f32[128,1,128]{2,1,0:T(1,128)S(1)}, u32[]{:S(2)}, u32[]{:S(2)}) %all-to-all-start) | async-done | bytes 65568 | tf_op jit(solution)/shard_map/all_to_all | solution.py:484
  49.3 1.2 %final.1 = (f32[48,1024]{1,0:T(8,128)}, f32[48,1024]{1,0:T(8,128)}) custom-call(s32[304]{0:T(512)S(4)} %get-tuple-element.24.table, f32[128,128]{1,0:T(8,128)S(1)} %bitcast.5, f32[384,128]{1,0:T(8,128)S(1)} %get-tuple-element.25.pairs, f32[16,3,16,128]{3,2,1,0:T(8,128)S(1)} %get-tuple-element.41.firsts, f32[16,3,16,128]{3,2,1,0:T(8,128)S(1)} %get-tuple-element.42.seconds, ...), custom_call_target="tpu_custom_call" | custom-call | tf_op jit(solution)/shard_map/final/pallas_call | solution.py:486
Async XLA Ops:
  0.6 13.9 %collective-permute-start = (f32[48,1024]{1,0:T(8,128)}, f32[48,1024]{1,0:T(8,128)S(1)}, u32[]{:S(2)}, u32[]{:S(2)}) collective-permute-start(f32[48,1024]{1,0:T(8,128)} %source_hbm.1), channel_id=1, source_target_pairs={{0,31},{1,0},{2,1},{3,2},{4,3},{5,4},{6,5},{7,6},{8,7},{9,8},{10,9... | collective-permute-start | bytes 589832 | tf_op jit(solution)/shard_map/ppermute | solution.py:388
  7.5 7.0 %collective-permute-start.1 = (f32[8,8,128]{2,1,0:T(8,128)S(1)}, f32[8,8,128]{2,1,0:T(8,128)S(1)}, u32[]{:S(2)}, u32[]{:S(2)}) collective-permute-start(f32[8,8,128]{2,1,0:T(8,128)S(1)} %get-tuple-element.26), channel_id=1, source_target_pairs={{0,96},{32,0},{64,32},{96,64},{1,97},{33,1},{65,33},{97,65},{2,98}... | collective-permute-start | bytes 98312 | tf_op jit(solution)/shard_map/ppermute | solution.py:388
  16.2 6.7 %collective-permute-start.2 = (f32[4,16,128]{2,1,0:T(8,128)S(1)}, f32[4,16,128]{2,1,0:T(8,128)S(1)}, u32[]{:S(2)}, u32[]{:S(2)}) collective-permute-start(f32[4,16,128]{2,1,0:T(8,128)S(1)} %get-tuple-element.29), channel_id=1, source_target_pairs={{0,31},{1,2},{2,1},{3,4},{4,3},{5,6},{6,5},{7,8},{8,7},{9,10},{10,... | collective-permute-start | bytes 98312 | tf_op jit(solution)/shard_map/ppermute | solution.py:388
  16.7 6.3 %collective-permute-start.3 = (f32[4,16,128]{2,1,0:T(8,128)S(1)}, f32[4,16,128]{2,1,0:T(8,128)S(1)}, u32[]{:S(2)}, u32[]{:S(2)}) collective-permute-start(f32[4,16,128]{2,1,0:T(8,128)S(1)} %get-tuple-element.30), channel_id=1, source_target_pairs={{0,32},{32,0},{64,96},{96,64},{1,33},{33,1},{65,97},{97,65},{2,34}... | collective-permute-start | bytes 98312 | tf_op jit(solution)/shard_map/ppermute | solution.py:388
  17.7 5.2 %collective-permute-start.4 = (f32[4,16,128]{2,1,0:T(8,128)S(1)}, f32[4,16,128]{2,1,0:T(8,128)S(1)}, u32[]{:S(2)}, u32[]{:S(2)}) collective-permute-start(f32[4,16,128]{2,1,0:T(8,128)S(1)} %get-tuple-element.31), channel_id=1, source_target_pairs={{0,96},{32,64},{64,32},{96,0},{1,97},{33,65},{65,33},{97,1},{2,98}... | collective-permute-start | bytes 98312 | tf_op jit(solution)/shard_map/ppermute | solution.py:388
  20.3 2.7 %collective-permute-start.5 = (f32[4,16,128]{2,1,0:T(8,128)S(1)}, f32[4,16,128]{2,1,0:T(8,128)S(1)}, u32[]{:S(2)}, u32[]{:S(2)}) collective-permute-start(f32[4,16,128]{2,1,0:T(8,128)S(1)} %get-tuple-element.32), channel_id=1, source_target_pairs={{0,1},{1,0},{2,3},{3,2},{4,5},{5,4},{6,7},{7,6},{8,9},{9,8},{10,11... | collective-permute-start | bytes 98312 | tf_op jit(solution)/shard_map/ppermute | solution.py:388
  24.7 6.7 %collective-permute-start.6 = (f32[4,16,128]{2,1,0:T(8,128)S(1)}, f32[4,16,128]{2,1,0:T(8,128)S(1)}, u32[]{:S(2)}, u32[]{:S(2)}) collective-permute-start(f32[4,16,128]{2,1,0:T(8,128)S(1)} %get-tuple-element.35), channel_id=1, source_target_pairs={{0,31},{1,2},{2,1},{3,4},{4,3},{5,6},{6,5},{7,8},{8,7},{9,10},{10,... | collective-permute-start | bytes 98312 | tf_op jit(solution)/shard_map/ppermute | solution.py:388
  27.2 4.3 %collective-permute-start.7 = (f32[4,16,128]{2,1,0:T(8,128)S(1)}, f32[4,16,128]{2,1,0:T(8,128)S(1)}, u32[]{:S(2)}, u32[]{:S(2)}) collective-permute-start(f32[4,16,128]{2,1,0:T(8,128)S(1)} %get-tuple-element.36), channel_id=1, source_target_pairs={{0,32},{32,0},{64,96},{96,64},{1,33},{33,1},{65,97},{97,65},{2,34}... | collective-permute-start | bytes 98312 | tf_op jit(solution)/shard_map/ppermute | solution.py:388
  27.7 5.1 %collective-permute-start.8 = (f32[4,16,128]{2,1,0:T(8,128)S(1)}, f32[4,16,128]{2,1,0:T(8,128)S(1)}, u32[]{:S(2)}, u32[]{:S(2)}) collective-permute-start(f32[4,16,128]{2,1,0:T(8,128)S(1)} %get-tuple-element.37), channel_id=1, source_target_pairs={{0,96},{32,64},{64,32},{96,0},{1,97},{33,65},{65,33},{97,1},{2,98}... | collective-permute-start | bytes 98312 | tf_op jit(solution)/shard_map/ppermute | solution.py:388
  29.9 2.9 %collective-permute-start.9 = (f32[4,16,128]{2,1,0:T(8,128)S(1)}, f32[4,16,128]{2,1,0:T(8,128)S(1)}, u32[]{:S(2)}, u32[]{:S(2)}) collective-permute-start(f32[4,16,128]{2,1,0:T(8,128)S(1)} %get-tuple-element.38), channel_id=1, source_target_pairs={{0,1},{1,0},{2,3},{3,2},{4,5},{5,4},{6,7},{7,6},{8,9},{9,8},{10,11... | collective-permute-start | bytes 98312 | tf_op jit(solution)/shard_map/ppermute | solution.py:388
  35.2 14.2 %all-to-all-start = ((f32[128,1,128]{2,1,0:T(1,128)}), f32[128,1,128]{2,1,0:T(1,128)S(1)}, u32[]{:S(2)}, u32[]{:S(2)}) async-start(f32[128,1,128]{2,1,0:T(1,128)} %bitcast.2), calls=%async_computation | async-start | bytes 131072 | tf_op jit(solution)/shard_map/all_to_all | solution.py:484
  40.1 6.7 %collective-permute-start.10 = (f32[4,16,128]{2,1,0:T(8,128)S(1)}, f32[4,16,128]{2,1,0:T(8,128)S(1)}, u32[]{:S(2)}, u32[]{:S(2)}) collective-permute-start(f32[4,16,128]{2,1,0:T(8,128)S(1)} %get-tuple-element.44), channel_id=1, source_target_pairs={{0,1},{1,2},{2,3},{3,4},{4,5},{5,6},{6,7},{7,8},{8,9},{9,10},{10,1... | collective-permute-start | bytes 98312 | tf_op jit(solution)/shard_map/ppermute | solution.py:388
  40.2 6.6 %collective-permute-start.11 = (f32[4,16,128]{2,1,0:T(8,128)S(1)}, f32[4,16,128]{2,1,0:T(8,128)S(1)}, u32[]{:S(2)}, u32[]{:S(2)}) collective-permute-start(f32[4,16,128]{2,1,0:T(8,128)S(1)} %get-tuple-element.45), channel_id=1, source_target_pairs={{0,32},{32,64},{64,96},{96,0},{1,33},{33,65},{65,97},{97,1},{2,34}... | collective-permute-start | bytes 98312 | tf_op jit(solution)/shard_map/ppermute | solution.py:388

commit v6 on v5

--- a/solution.py
+++ b/solution.py
@@ -332,23 +332,13 @@
     return value
 
 
-def final_kernel(table, shares, pairs, firsts, seconds, flux, prev_y, prev_x, answer, residual,
-                 every, answer_pairs, residual_pairs):
+def prepare_kernel(table, pairs, firsts, seconds, flux, prev_y, prev_x, n0, n1, n2, n3,
+                   every, *blocks):
     low_half = in_low_half((8, 128))
-    total = total_of(shares)
-    lane = lax.broadcasted_iota(jnp.int32, (8, 128), 1)
-    row_of = lax.broadcasted_iota(jnp.int32, (8, 128), 0)
 
     def packed(tile):
         return jnp.where(low_half, tile[:8], pltpu.roll(tile[8:], 64, 1))
 
-    def moment(part, i):
-        even = jnp.sum(jnp.where(lane == i * SOURCES + row_of, total[part], 0.0), axis=1, keepdims=True)
-        odd = jnp.sum(jnp.where(lane == i * SOURCES + 8 + row_of, total[part], 0.0), axis=1, keepdims=True)
-        return jnp.where(low_half, even, odd)
-
-    mu = [(moment(0, i), moment(1, i)) for i in range(6)]
-    alpha_0, beta_0, alpha_1, beta_1, alpha_2 = coefficients(mu)
     every[0:ELEMENTS] = flux[...]
     for axis, prev in enumerate((prev_x, prev_y)):
         for slot in range(4):
@@ -359,10 +349,39 @@
             at = element * 4 + axis
             row = pl.ds(pl.multiple_of(table[ROW_LOW + at] * 8, 8), 8)
             other = every[table[LOW + at], axis]
-            k0 = pairs[row, :]
-            k1 = packed(firsts[element, axis])
-            k2 = packed(seconds[element, axis])
-            k3 = packed(every[element, axis]) + jnp.where(low_half, pltpu.roll(other[:8], 64, 1), other[8:])
+            blocks[0][row, :] = packed(firsts[element, axis])
+            blocks[1][row, :] = packed(seconds[element, axis])
+            blocks[2][row, :] = packed(every[element, axis]) + jnp.where(
+                low_half, pltpu.roll(other[:8], 64, 1), other[8:]
+            )
+    for block, out in zip((pairs, *blocks), (n0, n1, n2, n3)):
+        for group in range(ROWS // 8):
+            for pair in range(8):
+                out[group * 8 : group * 8 + 8, pair * 128 : pair * 128 + 128] = block[
+                    pl.ds(group * 64 + pair, 8, stride=8), :
+                ]
+
+
+def final_kernel(shares, n0, n1, n2, n3, answer, residual):
+    low_half = in_low_half((8, 128))
+    total = total_of(shares)
+    lane = lax.broadcasted_iota(jnp.int32, (8, 128), 1)
+    row_of = lax.broadcasted_iota(jnp.int32, (8, 128), 0)
+
+    def moment(part, i):
+        even = jnp.sum(jnp.where(lane == i * SOURCES + row_of, total[part], 0.0), axis=1, keepdims=True)
+        odd = jnp.sum(jnp.where(lane == i * SOURCES + 8 + row_of, total[part], 0.0), axis=1, keepdims=True)
+        return jnp.where(low_half, even, odd)
+
+    mu = [(moment(0, i), moment(1, i)) for i in range(6)]
+    scalars = coefficients(mu)
+    for pair in range(8):
+        alpha_0, beta_0, alpha_1, beta_1, alpha_2 = (
+            jnp.broadcast_to(v[pair : pair + 1], (8, 128)) for v in scalars
+        )
+        for group in range(ROWS // 8):
+            at = (slice(group * 8, group * 8 + 8), slice(pair * 128, pair * 128 + 128))
+            k0, k1, k2, k3 = n0[at], n1[at], n2[at], n3[at]
             r1 = k0 - alpha_0 * k1
             ar1 = k1 - alpha_0 * k2
             aar1 = k2 - alpha_0 * k3
@@ -373,14 +392,8 @@
             ar2 = ar1 - alpha_1 * aad1
             d2 = r2 + beta_1 * d1
             ad2 = ar2 + beta_1 * ad1
-            answer_pairs[row, :] = alpha_0 * k0 + (alpha_1 * d1 + alpha_2 * d2)
-            residual_pairs[row, :] = r2 - alpha_2 * ad2
-    for block, out in ((answer_pairs, answer), (residual_pairs, residual)):
-        for group in range(ROWS // 8):
-            for pair in range(8):
-                out[group * 8 : group * 8 + 8, pair * 128 : pair * 128 + 128] = block[
-                    pl.ds(group * 64 + pair, 8, stride=8), :
-                ]
+            answer[at] = alpha_0 * k0 + (alpha_1 * d1 + alpha_2 * d2)
+            residual[at] = r2 - alpha_2 * ad2
 
 
 def passed(value, axis, target):
@@ -482,16 +495,25 @@
     )(table, flux, *exchanged(sends), moments, parts)
     prev_y, prev_x = ahead(up_y, "gy"), ahead(up_x, "gx")
     shares = lax.all_to_all(shares, ("gx", "gy"), 0, 0, tiled=True)
-    natural = jax.ShapeDtypeStruct((ROWS, SOURCES * BLOCK), jnp.float32)
+    size = (ROWS, SOURCES * BLOCK)
+    natural = jax.ShapeDtypeStruct(size, jnp.float32)
+    vectors = pl.pallas_call(
+        prepare_kernel,
+        out_shape=(vmem(size),) * 4,
+        in_specs=[SMEM] + [VMEM] * 6,
+        out_specs=(VMEM,) * 4,
+        scratch_shapes=[every] + [pltpu.VMEM(pairs_shape, jnp.float32)] * 3,
+        compiler_params=params(),
+        name="prepare",
+    )(table, pairs, k1, k2, flux, prev_y, prev_x)
     return pl.pallas_call(
         final_kernel,
         out_shape=(natural, natural),
-        in_specs=[SMEM] + [VMEM] * 7,
+        in_specs=[VMEM] * 5,
         out_specs=(VMEM, VMEM),
-        scratch_shapes=[every, pltpu.VMEM(pairs_shape, jnp.float32), pltpu.VMEM(pairs_shape, jnp.float32)],
         compiler_params=params(),
         name="final",
-    )(table, shares, pairs, k1, k2, flux, prev_y, prev_x)
+    )(shares, *vectors)
 
 
 def solution(mesh):

time: 51.4 us -> 51.3 us (level)
    pallas_call x1 -> x2, Pallas kernels: 1.21 us -> 1.59 us  [the longest x1 1.14 us: local(): pl.pallas_call(final_kernel, out_shape=(natural, natural), in_specs=[VMEM...]
  transfers between devices with their start and end apart: 13 -> 13, of which waited for: 5 -> 5; matrix products, arithmetic and copies ran while one was open for 0% -> 0% of each run, Pallas kernels for 10% -> 11%
where the time goes in v6:
time: 51.3 us; the launch traced here: 50.5 us
  starting transfers between devices  24.4 us (48%)
  waiting for transfers between devices  13.1 us (26%)
  Pallas kernels  12.3 us (24%)
  between operations  0.71 us (1%)
    ppermute x12, starting transfers between devices, passed(): return lax.ppermute(value, axis, [(i, target(i)) for i in range(count)])  19.5 us
    ppermute x12, waiting for transfers between devices, passed(): return lax.ppermute(value, axis, [(i, target(i)) for i in range(count)])  11 us
    all_to_all x1, starting transfers between devices, local(): shares = lax.all_to_all(shares, ('gx', 'gy'), 0, 0, tiled=True)  4.93 us
    pallas_call x1, Pallas kernels, local(): pl.pallas_call(split_kernel, out_shape=matrix, in_specs=[VMEM, HBM], out_...  2.87 us
    pallas_call x1, Pallas kernels, local(): pl.pallas_call(functools.partial(later_kernel, 2), out_shape=(state, stat...  2.34 us
    pallas_call x1, Pallas kernels, local(): pl.pallas_call(functools.partial(table_kernel, outer, inner), out_shape=(...  2.08 us
    all_to_all x1, waiting for transfers between devices, local(): shares = lax.all_to_all(shares, ('gx', 'gy'), 0, 0, tiled=True)  2.04 us
    pallas_call x1, Pallas kernels, local(): pl.pallas_call(functools.partial(later_kernel, 1), out_shape=(state, stat...  1.74 us
  transfers between devices with their start and end apart: 13, of which 5 were waited for; matrix products, arithmetic and copies ran while one was open for 0% of the time, Pallas kernels for 11%

profile of v6, /device:TPU:0, one launch (start us, length us, event | category | flops | bytes accessed | tf_op | source)
XLA Modules:
  0.0 50.5 jit_solution(261991576067867582)
XLA Ops:
  0.6 4.8 %collective-permute-start = (f32[48,1024]{1,0:T(8,128)}, f32[48,1024]{1,0:T(8,128)S(1)}, u32[]{:S(2)}, u32[]{:S(2)}) collective-permute-start(f32[48,1024]{1,0:T(8,128)} %source_hbm.1), channel_id=1, source_target_pairs={{0,31},{1,0},{2,1},{3,2},{4,3},{5,4},{6,5},{7,6},{8,7},{9,8},{10,9... | collective-permute-start | bytes 589832 | tf_op jit(solution)/shard_map/ppermute | solution.py:401
  5.4 2.1 %table.1 = (s32[304]{0:T(512)S(4)}, f32[384,128]{1,0:T(8,128)S(1)}, f32[8,8,128]{2,1,0:T(8,128)S(1)}, f32[6,384,384]{2,1,0:T(8,128)S(1)}) custom-call(s32[6,16]{1,0:T(8,128)} %bitcast.6, f32[48,1024]{1,0:T(8,128)} %source_hbm.1, f32[16,384,384]{2,1,0:T(8,128)} %matrix.3), custom_call_target="tpu_custom_call" | custom-call | tf_op jit(solution)/shard_map/table/pallas_call | solution.py:434
  7.5 4.1 %collective-permute-start.1 = (f32[8,8,128]{2,1,0:T(8,128)S(1)}, f32[8,8,128]{2,1,0:T(8,128)S(1)}, u32[]{:S(2)}, u32[]{:S(2)}) collective-permute-start(f32[8,8,128]{2,1,0:T(8,128)S(1)} %get-tuple-element.30), channel_id=1, source_target_pairs={{0,96},{32,0},{64,32},{96,64},{1,97},{33,1},{65,33},{97,65},{2,98}... | collective-permute-start | bytes 98312 | tf_op jit(solution)/shard_map/ppermute | solution.py:401
  11.6 2.9 %split.1.parts = bf16[16,768,384]{2,1,0:T(8,128)(2,1)S(1)} custom-call(f32[6,384,384]{2,1,0:T(8,128)S(1)} %get-tuple-element.31.early, f32[16,384,384]{2,1,0:T(8,128)} %matrix.3), custom_call_target="tpu_custom_call" | custom-call | flops 10000000 | bytes 18874368 | tf_op jit(solution)/shard_map/split/pallas_call | solution.py:456
  14.5 0.0 collective-permute-done.1.next_x
  14.5 0.0 collective-permute-done.next_y
  14.5 1.7 %first.1 = (f32[16,3,16,128]{3,2,1,0:T(8,128)S(1)}, f32[4,16,128]{2,1,0:T(8,128)S(1)}, f32[4,16,128]{2,1,0:T(8,128)S(1)}, f32[4,16,128]{2,1,0:T(8,128)S(1)}, f32...) custom-call(s32[304]{0:T(512)S(4)} %get-tuple-element.28.table, f32[384,128]{1,0:T(8,128)S(1)} %get-tuple-element.29.pairs, ...), custom_call_target="tpu_custom_call" | custom-call | tf_op jit(solution)/shard_map/first/pallas_call | solution.py:469
  16.2 0.5 collective-permute-start.2
  16.7 1.0 %collective-permute-start.3 = (f32[4,16,128]{2,1,0:T(8,128)S(1)}, f32[4,16,128]{2,1,0:T(8,128)S(1)}, u32[]{:S(2)}, u32[]{:S(2)}) collective-permute-start(f32[4,16,128]{2,1,0:T(8,128)S(1)} %get-tuple-element.34), channel_id=1, source_target_pairs={{0,32},{32,0},{64,96},{96,64},{1,33},{33,1},{65,97},{97,65},{2,34}... | collective-permute-start | bytes 98312 | tf_op jit(solution)/shard_map/ppermute | solution.py:401
  17.7 2.5 %collective-permute-start.4 = (f32[4,16,128]{2,1,0:T(8,128)S(1)}, f32[4,16,128]{2,1,0:T(8,128)S(1)}, u32[]{:S(2)}, u32[]{:S(2)}) collective-permute-start(f32[4,16,128]{2,1,0:T(8,128)S(1)} %get-tuple-element.35), channel_id=1, source_target_pairs={{0,96},{32,64},{64,32},{96,0},{1,97},{33,65},{65,33},{97,1},{2,98}... | collective-permute-start | bytes 98312 | tf_op jit(solution)/shard_map/ppermute | solution.py:401
  20.3 0.0 collective-permute-start.5
  20.3 2.7 %collective-permute-done.2.yb = f32[4,16,128]{2,1,0:T(8,128)S(1)} collective-permute-done((f32[4,16,128]{2,1,0:T(8,128)S(1)}, f32[4,16,128]{2,1,0:T(8,128)S(1)}, u32[]{:S(2)}, u32[]{:S(2)}) %collective-permute-start.2) | collective-permute-done | bytes 32800 | tf_op jit(solution)/shard_map/ppermute | solution.py:401
  23.0 0.0 collective-permute-done.3.xa
  23.0 0.0 collective-permute-done.4.xb
  23.0 0.0 collective-permute-done.5.ya
  23.0 1.7 %second.1 = (f32[16,3,16,128]{3,2,1,0:T(8,128)S(1)}, f32[16,3,16,128]{3,2,1,0:T(8,128)S(1)}, f32[4,16,128]{2,1,0:T(8,128)S(1)}, f32[4,16,128]{2,1,0:T(8,128)S(1)...) custom-call(s32[304]{0:T(512)S(4)} %get-tuple-element.28.table, ...), custom_call_target="tpu_custom_call" | custom-call | tf_op jit(solution)/shard_map/second/pallas_call | solution.py:478
  24.7 2.4 %collective-permute-start.6 = (f32[4,16,128]{2,1,0:T(8,128)S(1)}, f32[4,16,128]{2,1,0:T(8,128)S(1)}, u32[]{:S(2)}, u32[]{:S(2)}) collective-permute-start(f32[4,16,128]{2,1,0:T(8,128)S(1)} %get-tuple-element.39), channel_id=1, source_target_pairs={{0,31},{1,2},{2,1},{3,4},{4,3},{5,6},{6,5},{7,8},{8,7},{9,10},{10,... | collective-permute-start | bytes 98312 | tf_op jit(solution)/shard_map/ppermute | solution.py:401
  27.2 0.5 %collective-permute-start.7 = (f32[4,16,128]{2,1,0:T(8,128)S(1)}, f32[4,16,128]{2,1,0:T(8,128)S(1)}, u32[]{:S(2)}, u32[]{:S(2)}) collective-permute-start(f32[4,16,128]{2,1,0:T(8,128)S(1)} %get-tuple-element.40), channel_id=1, source_target_pairs={{0,32},{32,0},{64,96},{96,64},{1,33},{33,1},{65,97},{97,65},{2,34}... | collective-permute-start | bytes 98312 | tf_op jit(solution)/shard_map/ppermute | solution.py:401
  27.7 2.2 %collective-permute-start.8 = (f32[4,16,128]{2,1,0:T(8,128)S(1)}, f32[4,16,128]{2,1,0:T(8,128)S(1)}, u32[]{:S(2)}, u32[]{:S(2)}) collective-permute-start(f32[4,16,128]{2,1,0:T(8,128)S(1)} %get-tuple-element.41), channel_id=1, source_target_pairs={{0,96},{32,64},{64,32},{96,0},{1,97},{33,65},{65,33},{97,1},{2,98}... | collective-permute-start | bytes 98312 | tf_op jit(solution)/shard_map/ppermute | solution.py:401
  29.9 0.0 collective-permute-start.9
  29.9 1.5 %collective-permute-done.6.yb = f32[4,16,128]{2,1,0:T(8,128)S(1)} collective-permute-done((f32[4,16,128]{2,1,0:T(8,128)S(1)}, f32[4,16,128]{2,1,0:T(8,128)S(1)}, u32[]{:S(2)}, u32[]{:S(2)}) %collective-permute-start.6) | collective-permute-done | bytes 32800 | tf_op jit(solution)/shard_map/ppermute | solution.py:401
  31.5 0.0 collective-permute-done.7.xa
  31.5 1.4 %collective-permute-done.8.xb = f32[4,16,128]{2,1,0:T(8,128)S(1)} collective-permute-done((f32[4,16,128]{2,1,0:T(8,128)S(1)}, f32[4,16,128]{2,1,0:T(8,128)S(1)}, u32[]{:S(2)}, u32[]{:S(2)}) %collective-permute-start.8) | collective-permute-done | bytes 32800 | tf_op jit(solution)/shard_map/ppermute | solution.py:401
  32.8 0.0 collective-permute-done.9.ya
  32.8 2.3 %third.1 = (f32[16,3,16,128]{3,2,1,0:T(8,128)S(1)}, f32[16,3,16,128]{3,2,1,0:T(8,128)S(1)}, f32[4,16,128]{2,1,0:T(8,128)S(1)}, f32[4,16,128]{2,1,0:T(8,128)S(1)}, f32[128,128]{1,0:T(8,128)}) custom-call(s32[304]{0:T(512)S(4)} %get-tuple-element.28.table, f32[16,3,16,128]{3,2,1,0:T(8,128)S(1)} %get-tuple-element.38.previous, ...), custom_call_target="tpu_custom_call" | custom-call | tf_op jit(solution)/shard_map/third/pallas_call | solution.py:487
  35.2 4.9 %all-to-all-start = ((f32[128,1,128]{2,1,0:T(1,128)}), f32[128,1,128]{2,1,0:T(1,128)S(1)}, u32[]{:S(2)}, u32[]{:S(2)}) async-start(f32[128,1,128]{2,1,0:T(1,128)} %bitcast.2), calls=%async_computation | async-start | bytes 131072 | tf_op jit(solution)/shard_map/all_to_all | solution.py:497
  40.1 0.1 collective-permute-start.10
  40.2 1.2 %collective-permute-start.11 = (f32[4,16,128]{2,1,0:T(8,128)S(1)}, f32[4,16,128]{2,1,0:T(8,128)S(1)}, u32[]{:S(2)}, u32[]{:S(2)}) collective-permute-start(f32[4,16,128]{2,1,0:T(8,128)S(1)} %get-tuple-element.49), channel_id=1, source_target_pairs={{0,32},{32,64},{64,96},{96,0},{1,33},{33,65},{65,97},{97,1},{2,34}... | collective-permute-start | bytes 98312 | tf_op jit(solution)/shard_map/ppermute | solution.py:401
  41.4 5.4 %collective-permute-done.10.prev_y = f32[4,16,128]{2,1,0:T(8,128)S(1)} collective-permute-done((f32[4,16,128]{2,1,0:T(8,128)S(1)}, f32[4,16,128]{2,1,0:T(8,128)S(1)}, u32[]{:S(2)}, u32[]{:S(2)}) %collective-permute-start.10) | collective-permute-done | bytes 32800 | tf_op jit(solution)/shard_map/ppermute | solution.py:401
  46.8 0.0 collective-permute-done.11.prev_x
  46.8 0.4 prepare.1
  47.3 2.0 %all-to-all-done = f32[128,1,128]{2,1,0:T(1,128)S(1)} async-done(((f32[128,1,128]{2,1,0:T(1,128)}), f32[128,1,128]{2,1,0:T(1,128)S(1)}, u32[]{:S(2)}, u32[]{:S(2)}) %all-to-all-start) | async-done | bytes 65568 | tf_op jit(solution)/shard_map/all_to_all | solution.py:497
  49.3 1.1 %final.1 = (f32[48,1024]{1,0:T(8,128)}, f32[48,1024]{1,0:T(8,128)}) custom-call(f32[128,128]{1,0:T(8,128)S(1)} %bitcast.5, f32[48,1024]{1,0:T(8,128)S(1)} %get-tuple-element.50.n0, f32[48,1024]{1,0:T(8,128)S(1)} %get-tuple-element.51.n1, f32[48,1024]{1,0:T(8,128)S(1)} %get-tuple-element.52.n2, f32[48,1024]{1,0:T(8,128)S(1)} %get-tuple-element.53.n3), custom_call_target="tpu_custom_call" | custom-call | tf_op jit(solution)/shard_map/final/pallas_call | solution.py:509
Async XLA Ops:
  0.6 13.9 %collective-permute-start = (f32[48,1024]{1,0:T(8,128)}, f32[48,1024]{1,0:T(8,128)S(1)}, u32[]{:S(2)}, u32[]{:S(2)}) collective-permute-start(f32[48,1024]{1,0:T(8,128)} %source_hbm.1), channel_id=1, source_target_pairs={{0,31},{1,0},{2,1},{3,2},{4,3},{5,4},{6,5},{7,6},{8,7},{9,8},{10,9... | collective-permute-start | bytes 589832 | tf_op jit(solution)/shard_map/ppermute | solution.py:401
  7.5 7.0 %collective-permute-start.1 = (f32[8,8,128]{2,1,0:T(8,128)S(1)}, f32[8,8,128]{2,1,0:T(8,128)S(1)}, u32[]{:S(2)}, u32[]{:S(2)}) collective-permute-start(f32[8,8,128]{2,1,0:T(8,128)S(1)} %get-tuple-element.30), channel_id=1, source_target_pairs={{0,96},{32,0},{64,32},{96,64},{1,97},{33,1},{65,33},{97,65},{2,98}... | collective-permute-start | bytes 98312 | tf_op jit(solution)/shard_map/ppermute | solution.py:401
  16.2 6.7 %collective-permute-start.2 = (f32[4,16,128]{2,1,0:T(8,128)S(1)}, f32[4,16,128]{2,1,0:T(8,128)S(1)}, u32[]{:S(2)}, u32[]{:S(2)}) collective-permute-start(f32[4,16,128]{2,1,0:T(8,128)S(1)} %get-tuple-element.33), channel_id=1, source_target_pairs={{0,31},{1,2},{2,1},{3,4},{4,3},{5,6},{6,5},{7,8},{8,7},{9,10},{10,... | collective-permute-start | bytes 98312 | tf_op jit(solution)/shard_map/ppermute | solution.py:401
  16.7 6.3 %collective-permute-start.3 = (f32[4,16,128]{2,1,0:T(8,128)S(1)}, f32[4,16,128]{2,1,0:T(8,128)S(1)}, u32[]{:S(2)}, u32[]{:S(2)}) collective-permute-start(f32[4,16,128]{2,1,0:T(8,128)S(1)} %get-tuple-element.34), channel_id=1, source_target_pairs={{0,32},{32,0},{64,96},{96,64},{1,33},{33,1},{65,97},{97,65},{2,34}... | collective-permute-start | bytes 98312 | tf_op jit(solution)/shard_map/ppermute | solution.py:401
  17.7 5.2 %collective-permute-start.4 = (f32[4,16,128]{2,1,0:T(8,128)S(1)}, f32[4,16,128]{2,1,0:T(8,128)S(1)}, u32[]{:S(2)}, u32[]{:S(2)}) collective-permute-start(f32[4,16,128]{2,1,0:T(8,128)S(1)} %get-tuple-element.35), channel_id=1, source_target_pairs={{0,96},{32,64},{64,32},{96,0},{1,97},{33,65},{65,33},{97,1},{2,98}... | collective-permute-start | bytes 98312 | tf_op jit(solution)/shard_map/ppermute | solution.py:401
  20.3 2.7 %collective-permute-start.5 = (f32[4,16,128]{2,1,0:T(8,128)S(1)}, f32[4,16,128]{2,1,0:T(8,128)S(1)}, u32[]{:S(2)}, u32[]{:S(2)}) collective-permute-start(f32[4,16,128]{2,1,0:T(8,128)S(1)} %get-tuple-element.36), channel_id=1, source_target_pairs={{0,1},{1,0},{2,3},{3,2},{4,5},{5,4},{6,7},{7,6},{8,9},{9,8},{10,11... | collective-permute-start | bytes 98312 | tf_op jit(solution)/shard_map/ppermute | solution.py:401
  24.7 6.7 %collective-permute-start.6 = (f32[4,16,128]{2,1,0:T(8,128)S(1)}, f32[4,16,128]{2,1,0:T(8,128)S(1)}, u32[]{:S(2)}, u32[]{:S(2)}) collective-permute-start(f32[4,16,128]{2,1,0:T(8,128)S(1)} %get-tuple-element.39), channel_id=1, source_target_pairs={{0,31},{1,2},{2,1},{3,4},{4,3},{5,6},{6,5},{7,8},{8,7},{9,10},{10,... | collective-permute-start | bytes 98312 | tf_op jit(solution)/shard_map/ppermute | solution.py:401
  27.2 4.3 %collective-permute-start.7 = (f32[4,16,128]{2,1,0:T(8,128)S(1)}, f32[4,16,128]{2,1,0:T(8,128)S(1)}, u32[]{:S(2)}, u32[]{:S(2)}) collective-permute-start(f32[4,16,128]{2,1,0:T(8,128)S(1)} %get-tuple-element.40), channel_id=1, source_target_pairs={{0,32},{32,0},{64,96},{96,64},{1,33},{33,1},{65,97},{97,65},{2,34}... | collective-permute-start | bytes 98312 | tf_op jit(solution)/shard_map/ppermute | solution.py:401
  27.7 5.1 %collective-permute-start.8 = (f32[4,16,128]{2,1,0:T(8,128)S(1)}, f32[4,16,128]{2,1,0:T(8,128)S(1)}, u32[]{:S(2)}, u32[]{:S(2)}) collective-permute-start(f32[4,16,128]{2,1,0:T(8,128)S(1)} %get-tuple-element.41), channel_id=1, source_target_pairs={{0,96},{32,64},{64,32},{96,0},{1,97},{33,65},{65,33},{97,1},{2,98}... | collective-permute-start | bytes 98312 | tf_op jit(solution)/shard_map/ppermute | solution.py:401
  29.9 2.9 %collective-permute-start.9 = (f32[4,16,128]{2,1,0:T(8,128)S(1)}, f32[4,16,128]{2,1,0:T(8,128)S(1)}, u32[]{:S(2)}, u32[]{:S(2)}) collective-permute-start(f32[4,16,128]{2,1,0:T(8,128)S(1)} %get-tuple-element.42), channel_id=1, source_target_pairs={{0,1},{1,0},{2,3},{3,2},{4,5},{5,4},{6,7},{7,6},{8,9},{9,8},{10,11... | collective-permute-start | bytes 98312 | tf_op jit(solution)/shard_map/ppermute | solution.py:401
  35.2 14.2 %all-to-all-start = ((f32[128,1,128]{2,1,0:T(1,128)}), f32[128,1,128]{2,1,0:T(1,128)S(1)}, u32[]{:S(2)}, u32[]{:S(2)}) async-start(f32[128,1,128]{2,1,0:T(1,128)} %bitcast.2), calls=%async_computation | async-start | bytes 131072 | tf_op jit(solution)/shard_map/all_to_all | solution.py:497
  40.1 6.7 %collective-permute-start.10 = (f32[4,16,128]{2,1,0:T(8,128)S(1)}, f32[4,16,128]{2,1,0:T(8,128)S(1)}, u32[]{:S(2)}, u32[]{:S(2)}) collective-permute-start(f32[4,16,128]{2,1,0:T(8,128)S(1)} %get-tuple-element.48), channel_id=1, source_target_pairs={{0,1},{1,2},{2,3},{3,4},{4,5},{5,6},{6,7},{7,8},{8,9},{9,10},{10,1... | collective-permute-start | bytes 98312 | tf_op jit(solution)/shard_map/ppermute | solution.py:401
  40.2 6.6 %collective-permute-start.11 = (f32[4,16,128]{2,1,0:T(8,128)S(1)}, f32[4,16,128]{2,1,0:T(8,128)S(1)}, u32[]{:S(2)}, u32[]{:S(2)}) collective-permute-start(f32[4,16,128]{2,1,0:T(8,128)S(1)} %get-tuple-element.49), channel_id=1, source_target_pairs={{0,32},{32,64},{64,96},{96,0},{1,33},{33,65},{65,97},{97,1},{2,34}... | collective-permute-start | bytes 98312 | tf_op jit(solution)/shard_map/ppermute | solution.py:401
